TPU v7x, 256 devices: a whole 4x4x8 slice. The times are simulated.
256 devices in a mesh: row: 16 (over y, x), col: 16 (over z, core).
Axes of the slice: x: 4, y: 4, z: 8, core: 2. Of those that a mesh axis runs over, the one named last changes fastest.
Arguments:
- frozen_down_weight: bfloat16 [2, 12288, 28672], P(None, 'row', 'col'), may hold values from -0.0625 to 0.0625
- merged_weight_gradient: bfloat16 [2, 12288, 28672], P(None, 'row', 'col'), may hold values from -6 to 6
- adapter_up_matrix: bfloat16 [2, 12288, 64], P(None, 'row', 'col'), may hold values from -0.75 to 0.75
- adapter_down_matrix: bfloat16 [2, 64, 28672], P(None, 'row', 'col'), may hold values from -0.3125 to 0.3125
- magnitude: float32 [2, 28672], P(None, 'col'), may hold values from 0.5 to 2
Outputs:
- grad_b: float32 [2, 12288, 64], P(None, 'row', 'col')
- grad_a: float32 [2, 64, 28672], P(None, 'row', 'col')
- grad_mag: float32 [2, 28672], P(None, 'col')
All inputs are finite; a program needn't handle non-finite values.
Results may differ from a plain program's by a relative error of at most 0.0025.
Values may be sent and summed in bfloat16 or wider, within the bound.
No kernel may reach another device: no remote copies, remote signals or barrier semaphores. Data moves between devices by JAX's collectives and lax.ppermute only.
A program may use at most 64 MiB of HBM per device.

v0:
```python
import jax
import jax.numpy as jnp
from jax import lax
from jax.sharding import PartitionSpec as P

epsilon = 1e-06


def coefficients(squares, inner, magnitude):
    norm = jnp.sqrt(squares + epsilon)
    scale = magnitude / norm
    shrink = scale * inner / (norm * norm)
    return (scale, shrink, inner / norm)


def on_device(
    frozen_down_weight, merged_weight_gradient, adapter_up_matrix, adapter_down_matrix, magnitude
):
    complete_left_factor = lax.all_gather(adapter_up_matrix, "col", axis=2, tiled=True)
    complete_right_factor = lax.all_gather(adapter_down_matrix, "row", axis=1, tiled=True)
    rank_slice_here = adapter_down_matrix.shape[1]
    lefts = []
    rights = []
    mags = []
    for layer_position in range(frozen_down_weight.shape[0]):
        left_here = complete_left_factor[layer_position]
        right_here = complete_right_factor[layer_position]
        merged = frozen_down_weight[layer_position].astype(jnp.float32) + jnp.dot(
            left_here, right_here, preferred_element_type=jnp.float32
        )
        cot_float = merged_weight_gradient[layer_position].astype(jnp.float32)
        squares = jnp.sum(merged * merged, axis=0)
        inner = jnp.sum(cot_float * merged, axis=0)
        squares, inner = lax.psum((squares, inner), "row")
        scale, shrink, magnitude_gradient = coefficients(squares, inner, magnitude[layer_position])
        grad_merged = (scale * cot_float - shrink * merged).astype(jnp.bfloat16)
        term_left = jnp.dot(grad_merged, right_here.T, preferred_element_type=jnp.float32)
        left_factor_gradient = lax.psum_scatter(term_left, "col", scatter_dimension=1, tiled=True)

        def rank_block(start, count, left_here=left_here, grad_merged=grad_merged):
            return jnp.dot(left_here.T, grad_merged, preferred_element_type=jnp.float32)

        right_factor_gradient = lax.psum_scatter(
            rank_block(jnp.int32(0), rank_slice_here * lax.axis_size("row")),
            "row",
            scatter_dimension=0,
            tiled=True,
        )
        lefts.append(left_factor_gradient)
        rights.append(right_factor_gradient)
        mags.append(magnitude_gradient)
    return (jnp.stack(lefts), jnp.stack(rights), jnp.stack(mags))


def solution(mesh):
    in_specs = (
        P(None, "row", "col"),
        P(None, "row", "col"),
        P(None, "row", "col"),
        P(None, "row", "col"),
        P(None, "col"),
    )
    out_specs = (P(None, "row", "col"), P(None, "row", "col"), P(None, "col"))
    return jax.shard_map(
        on_device, mesh=mesh, in_specs=in_specs, out_specs=out_specs, check_vma=False
    )
```

profile of v0, /device:TPU:1, one launch (start us, length us, event | category | flops | bytes accessed | tf_op | source)
XLA Modules:
  0.0 358.4 jit_solution(3263041175668262894)
XLA Ops:
  7.2 0.0 all-reduce.10.cloned.1.call-start
  7.2 0.8 copy.12
  8.0 19.9 %all_gather.7 = bf16[2,64,1792]{2,0,1:T(2,128)(2,1)S(1)} all-gather(bf16[2,4,1792]{2,0,1:T(2,128)(2,1)S(1)} %copy.12), channel_id=1, replica_groups=mesh['row'=16,'col'=16] {'row'}, dimensions={1}, use_global_device_ids=true | all-gather | bytes 487424 | tf_op jit(solution)/shard_map/all_gather | solution.py:20
  27.9 0.0 slice-start
  27.9 0.0 copy-start.2
  27.9 0.6 fusion.12
  28.6 0.0 copy-start.3
  28.6 1.2 copy.10
  29.8 26.3 %all_gather.6 = bf16[2,768,64]{1,0,2:T(2,128)(2,1)S(1)} all-gather(bf16[2,768,4]{1,0,2:T(2,128)(2,1)S(1)} %copy.10), channel_id=1, replica_groups=mesh['row'=16,'col'=16] {'col'}, dimensions={2}, use_global_device_ids=true | all-gather | bytes 208896 | tf_op jit(solution)/shard_map/all_gather | solution.py:19
  56.1 0.3 fusion.13
  56.4 0.0 copy-start.5
  56.4 0.8 slice_reduce_fusion.1
  57.3 0.0 slice-start.1
  57.3 2.8 convert_add_fusion
  60.1 0.0 copy-start.1
  60.1 0.0 slice-done
  60.1 0.0 copy-done.2
  60.1 0.0 slice-done.1
  60.1 4.4 %multiply_reduce_fusion.1 = (f32[1792]{0:T(1024)S(1)}, f32[1792]{0:T(1024)S(1)}, f32[1792]{0:T(1024)S(1)}, f32[1792]{0:T(1024)S(1)}, f32[768,1792]{1,0:T(8,128)}) fusion(bf16[2,768,1792]{2,1,0:T(8,128)(2,1)S(1)} %bitcast.53, f32[768,1792]{1,0:T(8,128)S(1)} %convert_add_fusion, bf16[1,64,1792]{2,0,1:T(2,128)(2,1)S(1)} %get-tuple-element.19, ...), kind=kOutput, calls=%fused_computation.13 | convolution fusion | flops 192668672 | bytes 19623936 | tf_op jit(solution)/shard_map/dot_general | solution.py:28
  64.5 0.0 copy-done.3
  64.5 0.0 copy-done.5
  64.5 0.0 copy-done.1
  64.5 58.1 %all-reduce.5 = (f32[1792]{0:T(1024)S(1)}, f32[1792]{0:T(1024)S(1)}, f32[1792]{0:T(1024)S(1)}, f32[1792]{0:T(1024)S(1)}) all-reduce(f32[1792]{0:T(1024)S(1)} %get-tuple-element.5, f32[1792]{0:T(1024)S(1)} %get-tuple-element.6, f32[1792]{0:T(1024)S(1)} %get-tuple-element.4, ...), channel_id=1, replica_groups=mesh['row'=16,'col'=16] {'row'}, use_global_device_ids=true, to_apply=%region_8.0 | all-reduce | flops 7168 | bytes 57344 | tf_op jit(solution)/shard_map/psum | solution.py:34
  122.6 0.0 copy-start.4
  122.6 6.8 %fusion.1 = (bf16[768,1792]{1,0:T(8,128)(2,1)S(1)}, bf16[768,1792]{1,0:T(8,128)(2,1)S(1)}) fusion(f32[768,1792]{1,0:T(8,128)} %get-tuple-element.29, f32[1792]{0:T(1024)S(1)} %get-tuple-element.24, f32[1792]{0:T(1024)S(1)} %get-tuple-element.25, bf16[2,768,1792]{2,1,0:T(8,128)(2,1)} %param.6, f32[768,1792]{1,0:T(8,128)} %copy-done.1, ...), kind=kLoop, calls=%fused_computation.5 | loop fusion | flops 13762560 | bytes 22048768 | tf_op jit(solution)/shard_map/convert_element_type | solution.py:36
  129.4 0.0 copy-start
  129.4 1.6 copy-done
  131.0 0.0 copy-done.4
  131.0 1.6 fusion.6
  132.6 0.0 copy-start.7
  132.6 0.0 copy-start.6
  132.6 1.6 fusion.7
  134.3 0.0 all-reduce.10.cloned.1.call-update
  134.3 0.0 all-reduce.12.cloned.1.call-start
  134.3 3.3 convolution_bitcast_fusion.1
  137.6 1.4 convolution_bitcast_fusion
  139.0 0.0 all-reduce.12.cloned.1.call-update
  139.1 0.0 copy-done.7
  139.1 0.6 dynamic-slice.4
  139.7 0.0 copy-done.6
  139.7 0.6 dynamic-slice
  141.6 0.6 pad_maximum_fusion.2
  142.2 108.3 %all-reduce.10.cloned.1.call-done = (f32[768,64]{0,1:T(8,128)}, f32[768,64]{0,1:T(8,128)}) async-done(((f32[768,64]{0,1:T(8,128)}, f32[768,64]{0,1:T(8,128)}), (f32[768,64]{0,1:T(8,128)}, f32[768,64]{0,1:T(8,128)})) %all-reduce.10.cloned.1.call-update) | async-done | bytes 393232
  250.4 0.7 dynamic-slice_bitcast_fusion.2
  251.2 0.7 dynamic-slice_bitcast_fusion.3
  251.9 0.6 pad_maximum_fusion.1
  252.6 96.7 %all-reduce.12.cloned.1.call-done = (f32[64,1792]{1,0:T(8,128)}, f32[64,1792]{1,0:T(8,128)}) async-done(((f32[64,1792]{1,0:T(8,128)}, f32[64,1792]{1,0:T(8,128)}), (f32[64,1792]{1,0:T(8,128)}, f32[64,1792]{1,0:T(8,128)})) %all-reduce.12.cloned.1.call-update) | async-done | bytes 917520
  349.3 0.8 dynamic-slice_bitcast_fusion.1
  350.1 0.8 dynamic-slice_bitcast_fusion
  350.9 0.6 pad_maximum_fusion
  (4 shorter events, 0.0 us)
Async XLA Ops:
  7.2 243.3 %all-reduce.10.cloned.1.call-start = ((), (), s32[]{:S(2)}) async-start(), calls=%async_computation | async-start | bytes 786432
  27.9 32.2 %slice-start = ((s8[5505024]{0:T(1024)(128)(4,1)}), s8[4194304]{0:T(1024)(128)(4,1)S(1)}, s32[]{:S(2)}) async-start(s8[5505024]{0:T(1024)(128)(4,1)} %bitcast.52), calls=%async_computation.2 | async-start | bytes 8388608
  27.9 32.2 %copy-start.2 = (bf16[2,768,1792]{2,1,0:T(8,128)(2,1)S(1)}, bf16[2,768,1792]{2,1,0:T(8,128)(2,1)}, u32[]{:S(2)}) copy-start(bf16[2,768,1792]{2,1,0:T(8,128)(2,1)} %param.5) | copy-start | bytes 16515076
  28.6 35.9 %copy-start.3 = (bf16[1,64,1792]{2,0,1:T(2,128)(2,1)}, bf16[1,64,1792]{2,0,1:T(2,128)(2,1)S(1)}, u32[]{:S(2)}) copy-start(bf16[1,64,1792]{2,0,1:T(2,128)(2,1)S(1)} %get-tuple-element.19) | copy-start | bytes 688132
  56.4 8.1 %copy-start.5 = (bf16[1,768,64]{1,0,2:T(2,128)(2,1)}, bf16[1,768,64]{1,0,2:T(2,128)(2,1)S(1)}, u32[]{:S(2)}) copy-start(bf16[1,768,64]{1,0,2:T(2,128)(2,1)S(1)} %get-tuple-element.21) | copy-start | bytes 294916
  57.3 2.8 slice-start.1
  60.1 4.4 %copy-start.1 = (f32[768,1792]{1,0:T(8,128)}, f32[768,1792]{1,0:T(8,128)S(1)}, u32[]{:S(2)}) copy-start(f32[768,1792]{1,0:T(8,128)S(1)} %convert_add_fusion) | copy-start | bytes 16515076
  122.6 8.3 %copy-start.4 = (bf16[1,64,1792]{2,0,1:T(2,128)(2,1)S(1)}, bf16[1,64,1792]{2,0,1:T(2,128)(2,1)}, u32[]{:S(2)}) copy-start(bf16[1,64,1792]{2,0,1:T(2,128)(2,1)} %copy-done.3) | copy-start | bytes 688132
  129.4 1.6 copy-start
  132.6 6.5 %copy-start.7 = (u32[256]{0:T(256)S(1)}, u32[256]{0:T(256)}, u32[]{:S(2)}) copy-start(u32[256]{0:T(256)} %constant.16) | copy-start | bytes 3076
  132.6 7.1 %copy-start.6 = (u32[256]{0:T(256)S(1)}, u32[256]{0:T(256)}, u32[]{:S(2)}) copy-start(u32[256]{0:T(256)} %constant.8) | copy-start | bytes 3076
  134.3 215.0 %all-reduce.12.cloned.1.call-start = ((), (), s32[]{:S(2)}) async-start(), calls=%async_computation.1 | async-start | bytes 1835008
Sparse Core Ops, SparseCore 0:
  134.4 115.9 all-reduce.9
  254.1 95.1 all-reduce.11
where the time goes:
time: 359 us; the launch traced here: 358 us
  waiting for transfers between devices  205 us (57%)
  blocking collectives  104 us (29%)
  between operations  15.5 us (4%)
  matrix products  15.1 us (4%)
  local copies, waits for them, and re-layouts  9.66 us (3%)
  other arithmetic  8.64 us (2%)
    unnamed x4, waiting for transfers between devices  205 us
    psum x1, blocking collectives, on_device(): squares, inner = lax.psum((squares, inner), 'row')  58.1 us
    all_gather x1, blocking collectives, on_device(): lax.all_gather(adapter_up_matrix, 'col', axis=2, tiled=True)  26.3 us
    all_gather x1, blocking collectives, on_device(): lax.all_gather(adapter_down_matrix, 'row', axis=1, tiled=True)  19.9 us
  transfers between devices with their start and end apart: 2, of which 2 were waited for; matrix products, arithmetic and copies ran while one was open for 2% of the time, Pallas kernels for 0%

commit v1 on v0

v1 whole, which is shorter than its diff:
```python
import functools

import jax
import jax.numpy as jnp
from jax import lax
from jax.experimental import pallas as pl
from jax.experimental.pallas import tpu as pltpu
from jax.sharding import PartitionSpec as P

epsilon = 1e-06
LAYERS = 2
SIDE = 4
GROUPS = SIDE * SIDE
RANKS_HERE = 4
SLAB = LAYERS * RANKS_HERE
DEPTH = GROUPS * SLAB
BLOCK = 256
VMEM_BYTES = 48 * 1024 * 1024


def shift_x(k):
    return [(y * SIDE + x, y * SIDE + (x + k) % SIDE) for y in range(SIDE) for x in range(SIDE)]


def shift_y(k):
    return [(y * SIDE + x, (y + k) % SIDE * SIDE + x) for y in range(SIDE) for x in range(SIDE)]


def group_at(me, ky, kx):
    y, x = me // SIDE, me % SIDE
    return (y + SIDE - ky) % SIDE * SIDE + (x + SIDE - kx) % SIDE


def layer_mask(layer, shape):
    row = lax.broadcasted_iota(jnp.int32, shape, 0)
    return (row // RANKS_HERE) % LAYERS == layer


def sums_kernel(me_ref, w_ref, g_ref, b_ref, a0, a1, a2, a3, s_ref, bz_ref, bt_ref, order):
    @pl.when(pl.program_id(0) == 0)
    def _():
        me = me_ref[0]
        for ky in range(SIDE):
            for kx in range(SIDE):
                at = (ky * SIDE + kx) * SLAB
                order[at : at + SLAB, :] = b_ref[group_at(me, ky, kx)].astype(jnp.float32)
        for layer in range(LAYERS):
            masked = jnp.where(layer_mask(layer, order.shape), order[...], 0.0)
            bz_ref[layer] = masked.astype(jnp.bfloat16)
            bt_ref[layer] = masked.T.astype(jnp.bfloat16)

    a = jnp.concatenate([a0[...], a1[...], a2[...], a3[...]], axis=0)
    rows = []
    for layer in range(LAYERS):
        merged = w_ref[layer].astype(jnp.float32) + jnp.dot(
            bt_ref[layer], a, preferred_element_type=jnp.float32
        )
        cot = g_ref[layer].astype(jnp.float32)
        rows.append(jnp.sum(merged * merged, axis=0, keepdims=True))
        rows.append(jnp.sum(cot * merged, axis=0, keepdims=True))
    sums = jnp.concatenate(rows, axis=0)
    s_ref[...] = jnp.broadcast_to(sums[None], s_ref.shape)


def grads_kernel(
    me_ref, w_ref, g_ref, bz_ref, bt_ref, a0, a1, a2, a3, s_ref, mag_ref,
    x0, x1, x2, x3, tb_ref, gmag_ref, total,
):
    step = pl.program_id(0)
    a = jnp.concatenate([a0[...], a1[...], a2[...], a3[...]], axis=0)
    a_wide = a.astype(jnp.float32)
    sums = jnp.sum(s_ref[...], axis=0)
    term_a = None
    term_b = None
    for layer in range(LAYERS):
        squares = sums[2 * layer : 2 * layer + 1]
        inner = sums[2 * layer + 1 : 2 * layer + 2]
        norm = jnp.sqrt(squares + epsilon)
        scale = mag_ref[layer : layer + 1, :] / norm
        shrink = scale * inner / (norm * norm)
        gmag_ref[layer : layer + 1, :] = inner / norm
        merged = w_ref[layer].astype(jnp.float32) + jnp.dot(
            bt_ref[layer], a, preferred_element_type=jnp.float32
        )
        cot = g_ref[layer].astype(jnp.float32)
        grad = (scale * cot - shrink * merged).astype(jnp.bfloat16)
        az = jnp.where(layer_mask(layer, a_wide.shape), a_wide, 0.0).astype(jnp.bfloat16)
        part_a = jnp.dot(bz_ref[layer], grad, preferred_element_type=jnp.float32)
        part_b = lax.dot_general(
            az, grad, (((1,), (1,)), ((), ())), preferred_element_type=jnp.float32
        )
        term_a = part_a if term_a is None else term_a + part_a
        term_b = part_b if term_b is None else term_b + part_b
    for kx, out in enumerate((x0, x1, x2, x3)):
        for ky in range(SIDE):
            at = (ky * SIDE + kx) * SLAB
            out[ky] = term_a[at : at + SLAB]

    @pl.when(step == 0)
    def _():
        total[...] = term_b

    @pl.when(step > 0)
    def _():
        total[...] += term_b

    @pl.when(step == pl.num_programs(0) - 1)
    def _():
        me = me_ref[0]
        for ky in range(SIDE):
            for kx in range(SIDE):
                at = (ky * SIDE + kx) * SLAB
                tb_ref[group_at(me, ky, kx)] = total[at : at + SLAB]


def whole(shape):
    return pl.BlockSpec(shape, lambda c, me: (0,) * len(shape))


def columns(shape):
    return pl.BlockSpec(shape, lambda c, me: (0,) * (len(shape) - 1) + (c,))


def on_device(weight, cotangent, up, down, magnitude):
    layers, height, width = weight.shape
    steps = width // BLOCK
    me = lax.axis_index("row").astype(jnp.int32).reshape(1)

    up_slab = jnp.swapaxes(up, 1, 2).reshape(SLAB, height)
    up_all = lax.all_to_all(jnp.broadcast_to(up_slab, (GROUPS, SLAB, height)), "col", 0, 0)

    along_x = [down] + [lax.ppermute(down, "row", shift_x(k)) for k in range(1, SIDE)]
    down_x = jnp.stack(along_x).reshape(SIDE * SLAB, width)
    downs = [down_x] + [lax.ppermute(down_x, "row", shift_y(k)) for k in range(1, SIDE)]

    params = pltpu.CompilerParams(vmem_limit_bytes=VMEM_BYTES)
    down_specs = [columns((SIDE * SLAB, BLOCK))] * SIDE
    sums, up_rows, up_columns = pl.pallas_call(
        sums_kernel,
        grid_spec=pltpu.PrefetchScalarGridSpec(
            num_scalar_prefetch=1,
            grid=(steps,),
            in_specs=[
                columns((layers, height, BLOCK)),
                columns((layers, height, BLOCK)),
                whole((GROUPS, SLAB, height)),
                *down_specs,
            ],
            out_specs=[
                columns((GROUPS, 2 * layers, BLOCK)),
                whole((layers, DEPTH, height)),
                whole((layers, height, DEPTH)),
            ],
            scratch_shapes=[pltpu.VMEM((DEPTH, height), jnp.float32)],
        ),
        out_shape=[
            jax.ShapeDtypeStruct((GROUPS, 2 * layers, width), jnp.float32),
            jax.ShapeDtypeStruct((layers, DEPTH, height), jnp.bfloat16),
            jax.ShapeDtypeStruct((layers, height, DEPTH), jnp.bfloat16),
        ],
        compiler_params=params,
        name="column_sums",
    )(me, weight, cotangent, up_all, *downs)

    sums_all = lax.all_to_all(sums, "row", 0, 0)

    *terms_x, term_b, mags = pl.pallas_call(
        grads_kernel,
        grid_spec=pltpu.PrefetchScalarGridSpec(
            num_scalar_prefetch=1,
            grid=(steps,),
            in_specs=[
                columns((layers, height, BLOCK)),
                columns((layers, height, BLOCK)),
                whole((layers, DEPTH, height)),
                whole((layers, height, DEPTH)),
                *down_specs,
                columns((GROUPS, 2 * layers, BLOCK)),
                columns((layers, BLOCK)),
            ],
            out_specs=[
                *[columns((SIDE, SLAB, BLOCK))] * SIDE,
                whole((GROUPS, SLAB, height)),
                columns((layers, BLOCK)),
            ],
            scratch_shapes=[pltpu.VMEM((DEPTH, height), jnp.float32)],
        ),
        out_shape=[
            *[jax.ShapeDtypeStruct((SIDE, SLAB, width), jnp.float32)] * SIDE,
            jax.ShapeDtypeStruct((GROUPS, SLAB, height), jnp.float32),
            jax.ShapeDtypeStruct((layers, width), jnp.float32),
        ],
        compiler_params=params,
        name="gradients",
    )(me, weight, cotangent, up_rows, up_columns, *downs, sums_all, magnitude)

    parts_b = lax.all_to_all(term_b, "col", 0, 0)
    sum_x = terms_x[0]
    for k in range(1, SIDE):
        sum_x = sum_x + lax.ppermute(terms_x[k], "row", shift_x(-k))
    sum_y = sum_x[0]
    for k in range(1, SIDE):
        sum_y = sum_y + lax.ppermute(sum_x[k], "row", shift_y(-k))
    grad_b = jnp.sum(parts_b, axis=0).reshape(layers, RANKS_HERE, height)
    return jnp.swapaxes(grad_b, 1, 2), sum_y.reshape(layers, RANKS_HERE, width), mags


def solution(mesh):
    in_specs = (
        P(None, "row", "col"),
        P(None, "row", "col"),
        P(None, "row", "col"),
        P(None, "row", "col"),
        P(None, "col"),
    )
    out_specs = (P(None, "row", "col"), P(None, "row", "col"), P(None, "col"))
    return jax.shard_map(
        on_device, mesh=mesh, in_specs=in_specs, out_specs=out_specs, check_vma=False
    )
```

time: 359 us -> 87.8 us (0.24)
  waiting for transfers between devices: 205 us -> 18.5 us
  blocking collectives: 104 us -> 12.7 us
  starting transfers between devices: 0.08 us -> 33.4 us
  Pallas kernels: 0 us -> 18.2 us
  matrix products: 15.1 us -> 0 us
  between operations: 15.5 us -> 0.7 us
  other arithmetic: 8.64 us -> 0.94 us
  local copies, waits for them, and re-layouts: 9.66 us -> 2.71 us
    unnamed x4 -> x0, waiting for transfers between devices: 205 us -> none
    psum x1 -> x0, blocking collectives: 58.1 us -> none  [on_device(): squares, inner = lax.psum((squares, inner), 'row')]
    all_gather x2 -> x0, blocking collectives: 46.3 us -> none  [the longest x1 26.3 us: on_device(): lax.all_gather(adapter_up_matrix, 'col', axis=2, tiled=True)]
    all_to_all x0 -> x2, starting transfers between devices: none -> 19.1 us  [the longest x1 9.99 us: on_device(): lax.all_to_all(jnp.broadcast_to(up_slab, (GROUPS, SLAB, height)), 'col',...]
    pallas_call x0 -> x2, Pallas kernels: none -> 18.2 us  [the longest x1 10.2 us: on_device(): pl.pallas_call(grads_kernel, grid_spec=pltpu.PrefetchScalarGridSpec(num_s...]
    dot_general x6 -> x0, matrix products: 15.1 us -> none  [the longest x2 7.14 us: on_device(): jnp.dot(left_here, right_here, preferred_element_type=jnp.float32)]
    ppermute x0 -> x12, starting transfers between devices: none -> 14.3 us  [the longest x3 5.12 us: on_device(): lax.ppermute(down, 'row', shift_x(k))]
    ppermute x0 -> x12, waiting for transfers between devices: none -> 13.6 us  [the longest x3 7.99 us: on_device(): lax.ppermute(down_x, 'row', shift_y(k))]
  transfers between devices with their start and end apart: 2 -> 14, of which waited for: 2 -> 8; matrix products, arithmetic and copies ran while one was open for 2% -> 3% of each run, Pallas kernels for 0% -> 0%
where the time goes in v1:
time: 87.8 us; the launch traced here: 87.2 us
  starting transfers between devices  33.4 us (38%)
  waiting for transfers between devices  18.5 us (21%)
  Pallas kernels  18.2 us (21%)
  blocking collectives  12.7 us (14%)
  local copies, waits for them, and re-layouts  2.71 us (3%)
  other arithmetic  0.94 us (1%)
    all_to_all x1, blocking collectives, on_device(): sums_all = lax.all_to_all(sums, 'row', 0, 0)  12.7 us
    pallas_call x1, Pallas kernels, on_device(): pl.pallas_call(grads_kernel, grid_spec=pltpu.PrefetchScalarGridSpec(num_s...  10.2 us
    all_to_all x1, starting transfers between devices, on_device(): lax.all_to_all(jnp.broadcast_to(up_slab, (GROUPS, SLAB, height)), 'col',...  9.99 us
    all_to_all x1, starting transfers between devices, on_device(): parts_b = lax.all_to_all(term_b, 'col', 0, 0)  9.06 us
    pallas_call x1, Pallas kernels, on_device(): pl.pallas_call(sums_kernel, grid_spec=pltpu.PrefetchScalarGridSpec(num_sc...  8 us
    ppermute x3, waiting for transfers between devices, on_device(): lax.ppermute(down_x, 'row', shift_y(k))  7.99 us
    ppermute x3, starting transfers between devices, on_device(): lax.ppermute(down, 'row', shift_x(k))  5.12 us
    all_to_all x1, waiting for transfers between devices, on_device(): parts_b = lax.all_to_all(term_b, 'col', 0, 0)  4.89 us
  transfers between devices with their start and end apart: 14, of which 8 were waited for; matrix products, arithmetic and copies ran while one was open for 3% of the time, Pallas kernels for 0%

profile of v1, /device:TPU:1, one launch (start us, length us, event | category | flops | bytes accessed | tf_op | source)
XLA Modules:
  0.0 87.2 jit_solution(13726176549165168105)
XLA Ops:
  0.6 2.1 %collective-permute-start = (bf16[2,4,1792]{2,1,0:T(4,128)(2,1)}, bf16[2,4,1792]{2,1,0:T(4,128)(2,1)S(1)}, u32[]{:S(2)}, u32[]{:S(2)}) collective-permute-start(bf16[2,4,1792]{2,1,0:T(4,128)(2,1)} %param.8), channel_id=1, source_target_pairs={{0,16},{16,32},{32,48},{48,0},{64,80},{80,96},{96,112},{112,64},{1... | collective-permute-start | bytes 86024 | tf_op jit(solution)/shard_map/ppermute | solution.py:132
  2.7 1.4 %collective-permute-start.2 = (bf16[2,4,1792]{2,1,0:T(4,128)(2,1)}, bf16[2,4,1792]{2,1,0:T(4,128)(2,1)S(1)}, u32[]{:S(2)}, u32[]{:S(2)}) collective-permute-start(bf16[2,4,1792]{2,1,0:T(4,128)(2,1)} %param.8), channel_id=1, source_target_pairs={{0,48},{16,0},{32,16},{48,32},{64,112},{80,64},{96,80},{112,96},{1... | collective-permute-start | bytes 86024 | tf_op jit(solution)/shard_map/ppermute | solution.py:132
  4.1 1.6 %collective-permute-start.1 = (bf16[2,4,1792]{2,1,0:T(4,128)(2,1)}, bf16[2,4,1792]{2,1,0:T(4,128)(2,1)S(1)}, u32[]{:S(2)}, u32[]{:S(2)}) collective-permute-start(bf16[2,4,1792]{2,1,0:T(4,128)(2,1)} %param.8), channel_id=1, source_target_pairs={{0,32},{16,48},{32,0},{48,16},{64,96},{80,112},{96,64},{112,80},{1... | collective-permute-start | bytes 86024 | tf_op jit(solution)/shard_map/ppermute | solution.py:132
  5.7 0.7 reshape.22
  6.5 0.7 broadcast_in_dim.3
  7.2 10.0 %all-to-all-start = ((bf16[16,8,768]{2,1,0:T(8,128)(2,1)}), bf16[16,8,768]{2,1,0:T(8,128)(2,1)S(1)}, u32[]{:S(2)}, u32[]{:S(2)}) async-start(bf16[16,8,768]{2,1,0:T(8,128)(2,1)} %broadcast_in_dim.3), calls=%async_computation | async-start | bytes 393216 | tf_op jit(solution)/shard_map/all_to_all | solution.py:130
  17.1 0.0 collective-permute-done
  17.2 0.0 collective-permute-done.2
  17.2 0.0 collective-permute-done.1
  17.2 0.9 pad_maximum_fusion
  18.1 2.8 %collective-permute-start.5 = (bf16[32,1792]{1,0:T(8,128)(2,1)S(1)}, bf16[32,1792]{1,0:T(8,128)(2,1)S(1)}, u32[]{:S(2)}, u32[]{:S(2)}) collective-permute-start(bf16[32,1792]{1,0:T(8,128)(2,1)S(1)} %reshape.23.a0), channel_id=1, source_target_pairs={{0,192},{16,208},{32,224},{48,240},{64,0},{80,16},{96,32},{112,48}... | collective-permute-start | bytes 344072 | tf_op jit(solution)/shard_map/ppermute | solution.py:134
  20.9 0.3 collective-permute-start.4
  21.2 0.7 collective-permute-start.3
  21.9 3.8 %collective-permute-done.5.a3 = bf16[32,1792]{1,0:T(8,128)(2,1)S(1)} collective-permute-done((bf16[32,1792]{1,0:T(8,128)(2,1)S(1)}, bf16[32,1792]{1,0:T(8,128)(2,1)S(1)}, u32[]{:S(2)}, u32[]{:S(2)}) %collective-permute-start.5) | collective-permute-done | bytes 114720 | tf_op jit(solution)/shard_map/ppermute | solution.py:134
  25.7 1.1 %collective-permute-done.4.a2 = bf16[32,1792]{1,0:T(8,128)(2,1)S(1)} collective-permute-done((bf16[32,1792]{1,0:T(8,128)(2,1)S(1)}, bf16[32,1792]{1,0:T(8,128)(2,1)S(1)}, u32[]{:S(2)}, u32[]{:S(2)}) %collective-permute-start.4) | collective-permute-done | bytes 114720 | tf_op jit(solution)/shard_map/ppermute | solution.py:134
  26.8 3.1 %collective-permute-done.3.a1 = bf16[32,1792]{1,0:T(8,128)(2,1)S(1)} collective-permute-done((bf16[32,1792]{1,0:T(8,128)(2,1)S(1)}, bf16[32,1792]{1,0:T(8,128)(2,1)S(1)}, u32[]{:S(2)}, u32[]{:S(2)}) %collective-permute-start.3) | collective-permute-done | bytes 114720 | tf_op jit(solution)/shard_map/ppermute | solution.py:134
  29.9 0.0 all-to-all-done.b_ref
  29.9 0.0 copy-start
  29.9 8.0 %column_sums.1 = (f32[16,4,1792]{2,1,0:T(4,128)S(1)}, bf16[2,128,768]{2,1,0:T(8,128)(2,1)S(1)}, bf16[2,768,128]{2,1,0:T(8,128)(2,1)S(1)}) custom-call(s32[1]{0:T(128)} %bitcast.me_ref, bf16[2,768,1792]{2,1,0:T(8,128)(2,1)} %w_ref.3, bf16[2,768,1792]{2,1,0:T(8,128)(2,1)} %g_ref.3, bf16[16,8,768]{2,1,0:T(8,128)(2,1)S(1)} %all-to-all-done.b_ref, ...), custom_call_target="tpu_custom_call" | custom-call | tf_op jit(solution)/shard_map/column_sums/pallas_call | solution.py:138
  37.9 12.7 %all_to_all.15.s_ref = f32[16,4,1792]{2,1,0:T(4,128)S(1)} all-to-all(f32[16,4,1792]{2,1,0:T(4,128)S(1)} %get-tuple-element.14), channel_id=1, replica_groups=mesh['row'=16,'col'=16] {'row'}, dimensions={0} | all-to-all | bytes 917504 | tf_op jit(solution)/shard_map/all_to_all | solution.py:165
  50.7 0.0 copy-done
  50.7 10.2 %gradients.1 = (f32[4,8,1792]{2,1,0:T(8,128)S(1)}, f32[4,8,1792]{2,1,0:T(8,128)S(1)}, f32[4,8,1792]{2,1,0:T(8,128)S(1)}, f32[4,8,1792]{2,1,0:T(8,128)S(1)}, f32[16,8,768]{2,1,0:T(8,128)}, /*index=5*/f32[2,1792]{1,0:T(2,128)}) custom-call(s32[1]{0:T(128)} %bitcast.me_ref, bf16[2,768,1792]{2,1,0:T(8,128)(2,1)} %w_ref.3, bf16[2,768,1792]{2,1,0:T(8,128)(2,1)} %g_ref.3, ...), custom_call_target="tpu_custom_call" | custom-call | tf_op jit(solution)/shard_map/gradients/pallas_call | solution.py:167
  60.9 0.4 collective-permute-start.6
  61.3 1.6 %collective-permute-start.7 = (f32[4,8,1792]{2,1,0:T(8,128)S(1)}, f32[4,8,1792]{2,1,0:T(8,128)S(1)}, u32[]{:S(2)}, u32[]{:S(2)}) collective-permute-start(f32[4,8,1792]{2,1,0:T(8,128)S(1)} %get-tuple-element.18), channel_id=1, source_target_pairs={{0,32},{16,48},{32,0},{48,16},{64,96},{80,112},{96,64},{112,80},{1... | collective-permute-start | bytes 688136 | tf_op jit(solution)/shard_map/ppermute | solution.py:200
  62.9 0.0 collective-permute-start.8
  62.9 9.1 %all-to-all-start.2 = ((f32[16,8,768]{2,1,0:T(8,128)}), f32[16,8,768]{2,1,0:T(8,128)S(1)}, u32[]{:S(2)}, u32[]{:S(2)}) async-start(f32[16,8,768]{2,1,0:T(8,128)} %get-tuple-element.15), calls=%async_computation.2 | async-start | bytes 786432 | tf_op jit(solution)/shard_map/all_to_all | solution.py:197
  72.0 0.0 collective-permute-done.6
  72.0 0.0 collective-permute-done.7
  72.0 2.4 %collective-permute-done.8 = f32[4,8,1792]{2,1,0:T(8,128)S(1)} collective-permute-done((f32[4,8,1792]{2,1,0:T(8,128)S(1)}, f32[4,8,1792]{2,1,0:T(8,128)S(1)}, u32[]{:S(2)}, u32[]{:S(2)}) %collective-permute-start.8) | collective-permute-done | bytes 229408 | tf_op jit(solution)/shard_map/ppermute | solution.py:200
  74.4 1.4 %collective-permute-start.9 = (f32[8,1792]{1,0:T(8,128)S(1)}, f32[8,1792]{1,0:T(8,128)S(1)}, u32[]{:S(2)}, u32[]{:S(2)}) collective-permute-start(f32[8,1792]{1,0:T(8,128)S(1)} %get-tuple-element.21), channel_id=1, source_target_pairs={{0,192},{16,208},{32,224},{48,240},{64,0},{80,16},{96,32},{112,48}... | collective-permute-start | bytes 172040 | tf_op jit(solution)/shard_map/ppermute | solution.py:203
  75.8 0.2 collective-permute-start.11
  76.0 1.7 %collective-permute-start.10 = (f32[8,1792]{1,0:T(8,128)S(1)}, f32[8,1792]{1,0:T(8,128)S(1)}, u32[]{:S(2)}, u32[]{:S(2)}) collective-permute-start(f32[8,1792]{1,0:T(8,128)S(1)} %get-tuple-element.23), channel_id=1, source_target_pairs={{0,128},{16,144},{32,160},{48,176},{64,192},{80,208},{96,224},{112... | collective-permute-start | bytes 172040 | tf_op jit(solution)/shard_map/ppermute | solution.py:203
  77.7 0.1 collective-permute-done.9
  77.8 3.0 %collective-permute-done.11 = f32[8,1792]{1,0:T(8,128)S(1)} collective-permute-done((f32[8,1792]{1,0:T(8,128)S(1)}, f32[8,1792]{1,0:T(8,128)S(1)}, u32[]{:S(2)}, u32[]{:S(2)}) %collective-permute-start.11) | collective-permute-done | bytes 57376 | tf_op jit(solution)/shard_map/ppermute | solution.py:203
  80.8 0.1 collective-permute-done.10
  81.0 0.6 reshape.25
  81.6 4.9 %all-to-all-done.2 = f32[16,8,768]{2,1,0:T(8,128)S(1)} async-done(((f32[16,8,768]{2,1,0:T(8,128)}), f32[16,8,768]{2,1,0:T(8,128)S(1)}, u32[]{:S(2)}, u32[]{:S(2)}) %all-to-all-start.2) | async-done | bytes 393248 | tf_op jit(solution)/shard_map/all_to_all | solution.py:197
  86.5 0.6 reshape.24
  (5 shorter events, 0.1 us)
Async XLA Ops:
  0.6 16.5 %collective-permute-start = (bf16[2,4,1792]{2,1,0:T(4,128)(2,1)}, bf16[2,4,1792]{2,1,0:T(4,128)(2,1)S(1)}, u32[]{:S(2)}, u32[]{:S(2)}) collective-permute-start(bf16[2,4,1792]{2,1,0:T(4,128)(2,1)} %param.8), channel_id=1, source_target_pairs={{0,16},{16,32},{32,48},{48,0},{64,80},{80,96},{96,112},{112,64},{1... | collective-permute-start | bytes 86024 | tf_op jit(solution)/shard_map/ppermute | solution.py:132
  2.7 14.4 %collective-permute-start.2 = (bf16[2,4,1792]{2,1,0:T(4,128)(2,1)}, bf16[2,4,1792]{2,1,0:T(4,128)(2,1)S(1)}, u32[]{:S(2)}, u32[]{:S(2)}) collective-permute-start(bf16[2,4,1792]{2,1,0:T(4,128)(2,1)} %param.8), channel_id=1, source_target_pairs={{0,48},{16,0},{32,16},{48,32},{64,112},{80,64},{96,80},{112,96},{1... | collective-permute-start | bytes 86024 | tf_op jit(solution)/shard_map/ppermute | solution.py:132
  4.1 13.1 %collective-permute-start.1 = (bf16[2,4,1792]{2,1,0:T(4,128)(2,1)}, bf16[2,4,1792]{2,1,0:T(4,128)(2,1)S(1)}, u32[]{:S(2)}, u32[]{:S(2)}) collective-permute-start(bf16[2,4,1792]{2,1,0:T(4,128)(2,1)} %param.8), channel_id=1, source_target_pairs={{0,32},{16,48},{32,0},{48,16},{64,96},{80,112},{96,64},{112,80},{1... | collective-permute-start | bytes 86024 | tf_op jit(solution)/shard_map/ppermute | solution.py:132
  7.2 22.8 %all-to-all-start = ((bf16[16,8,768]{2,1,0:T(8,128)(2,1)}), bf16[16,8,768]{2,1,0:T(8,128)(2,1)S(1)}, u32[]{:S(2)}, u32[]{:S(2)}) async-start(bf16[16,8,768]{2,1,0:T(8,128)(2,1)} %broadcast_in_dim.3), calls=%async_computation | async-start | bytes 393216 | tf_op jit(solution)/shard_map/all_to_all | solution.py:130
  18.1 7.6 %collective-permute-start.5 = (bf16[32,1792]{1,0:T(8,128)(2,1)S(1)}, bf16[32,1792]{1,0:T(8,128)(2,1)S(1)}, u32[]{:S(2)}, u32[]{:S(2)}) collective-permute-start(bf16[32,1792]{1,0:T(8,128)(2,1)S(1)} %reshape.23.a0), channel_id=1, source_target_pairs={{0,192},{16,208},{32,224},{48,240},{64,0},{80,16},{96,32},{112,48}... | collective-permute-start | bytes 344072 | tf_op jit(solution)/shard_map/ppermute | solution.py:134
  20.9 5.9 %collective-permute-start.4 = (bf16[32,1792]{1,0:T(8,128)(2,1)S(1)}, bf16[32,1792]{1,0:T(8,128)(2,1)S(1)}, u32[]{:S(2)}, u32[]{:S(2)}) collective-permute-start(bf16[32,1792]{1,0:T(8,128)(2,1)S(1)} %reshape.23.a0), channel_id=1, source_target_pairs={{0,128},{16,144},{32,160},{48,176},{64,192},{80,208},{96,224},{112... | collective-permute-start | bytes 344072 | tf_op jit(solution)/shard_map/ppermute | solution.py:134
  21.2 8.7 %collective-permute-start.3 = (bf16[32,1792]{1,0:T(8,128)(2,1)S(1)}, bf16[32,1792]{1,0:T(8,128)(2,1)S(1)}, u32[]{:S(2)}, u32[]{:S(2)}) collective-permute-start(bf16[32,1792]{1,0:T(8,128)(2,1)S(1)} %reshape.23.a0), channel_id=1, source_target_pairs={{0,64},{16,80},{32,96},{48,112},{64,128},{80,144},{96,160},{112,17... | collective-permute-start | bytes 344072 | tf_op jit(solution)/shard_map/ppermute | solution.py:134
  29.9 20.7 %copy-start = (f32[2,1792]{1,0:T(2,128)S(1)}, f32[2,1792]{1,0:T(2,128)}, u32[]{:S(2)}) copy-start(f32[2,1792]{1,0:T(2,128)} %mag_ref.1) | copy-start | bytes 43012
  60.9 11.1 %collective-permute-start.6 = (f32[4,8,1792]{2,1,0:T(8,128)S(1)}, f32[4,8,1792]{2,1,0:T(8,128)S(1)}, u32[]{:S(2)}, u32[]{:S(2)}) collective-permute-start(f32[4,8,1792]{2,1,0:T(8,128)S(1)} %get-tuple-element.17), channel_id=1, source_target_pairs={{0,48},{16,0},{32,16},{48,32},{64,112},{80,64},{96,80},{112,96},{1... | collective-permute-start | bytes 688136 | tf_op jit(solution)/shard_map/ppermute | solution.py:200
  61.3 10.7 %collective-permute-start.7 = (f32[4,8,1792]{2,1,0:T(8,128)S(1)}, f32[4,8,1792]{2,1,0:T(8,128)S(1)}, u32[]{:S(2)}, u32[]{:S(2)}) collective-permute-start(f32[4,8,1792]{2,1,0:T(8,128)S(1)} %get-tuple-element.18), channel_id=1, source_target_pairs={{0,32},{16,48},{32,0},{48,16},{64,96},{80,112},{96,64},{112,80},{1... | collective-permute-start | bytes 688136 | tf_op jit(solution)/shard_map/ppermute | solution.py:200
  62.9 11.5 %collective-permute-start.8 = (f32[4,8,1792]{2,1,0:T(8,128)S(1)}, f32[4,8,1792]{2,1,0:T(8,128)S(1)}, u32[]{:S(2)}, u32[]{:S(2)}) collective-permute-start(f32[4,8,1792]{2,1,0:T(8,128)S(1)} %get-tuple-element.19), channel_id=1, source_target_pairs={{0,16},{16,32},{32,48},{48,0},{64,80},{80,96},{96,112},{112,64},{1... | collective-permute-start | bytes 688136 | tf_op jit(solution)/shard_map/ppermute | solution.py:200
  62.9 23.6 %all-to-all-start.2 = ((f32[16,8,768]{2,1,0:T(8,128)}), f32[16,8,768]{2,1,0:T(8,128)S(1)}, u32[]{:S(2)}, u32[]{:S(2)}) async-start(f32[16,8,768]{2,1,0:T(8,128)} %get-tuple-element.15), calls=%async_computation.2 | async-start | bytes 786432 | tf_op jit(solution)/shard_map/all_to_all | solution.py:197
  74.4 3.4 %collective-permute-start.9 = (f32[8,1792]{1,0:T(8,128)S(1)}, f32[8,1792]{1,0:T(8,128)S(1)}, u32[]{:S(2)}, u32[]{:S(2)}) collective-permute-start(f32[8,1792]{1,0:T(8,128)S(1)} %get-tuple-element.21), channel_id=1, source_target_pairs={{0,192},{16,208},{32,224},{48,240},{64,0},{80,16},{96,32},{112,48}... | collective-permute-start | bytes 172040 | tf_op jit(solution)/shard_map/ppermute | solution.py:203
  75.8 5.0 %collective-permute-start.11 = (f32[8,1792]{1,0:T(8,128)S(1)}, f32[8,1792]{1,0:T(8,128)S(1)}, u32[]{:S(2)}, u32[]{:S(2)}) collective-permute-start(f32[8,1792]{1,0:T(8,128)S(1)} %get-tuple-element.22), channel_id=1, source_target_pairs={{0,64},{16,80},{32,96},{48,112},{64,128},{80,144},{96,160},{112,17... | collective-permute-start | bytes 172040 | tf_op jit(solution)/shard_map/ppermute | solution.py:203
  76.0 5.0 %collective-permute-start.10 = (f32[8,1792]{1,0:T(8,128)S(1)}, f32[8,1792]{1,0:T(8,128)S(1)}, u32[]{:S(2)}, u32[]{:S(2)}) collective-permute-start(f32[8,1792]{1,0:T(8,128)S(1)} %get-tuple-element.23), channel_id=1, source_target_pairs={{0,128},{16,144},{32,160},{48,176},{64,192},{80,208},{96,224},{112... | collective-permute-start | bytes 172040 | tf_op jit(solution)/shard_map/ppermute | solution.py:203

commit v2 on v0

v2 whole, which is shorter than its diff:
```python
import jax
import jax.numpy as jnp
from jax import lax
from jax.experimental import pallas as pl
from jax.experimental.pallas import tpu as pltpu
from jax.sharding import PartitionSpec as P

epsilon = 1e-06
LAYERS = 2
GROUPS = 16
RANKS_HERE = 4
SLAB = LAYERS * RANKS_HERE
DEPTH = GROUPS * SLAB
SIDE = 4
RING = 8
REACH = RING // 2
BLOCK = 256
VMEM_BYTES = 20 * 1024 * 1024
IN_VMEM = pl.BlockSpec(memory_space=pltpu.VMEM)
IN_SMEM = pl.BlockSpec(memory_space=pltpu.SMEM)

SWAP_CORE = [(i, i ^ 1) for i in range(GROUPS)]


def z_apart(k):
    ahead = [(2 * z, (z + k) % RING * 2) for z in range(RING)]
    behind = [(2 * z + 1, (z + RING - k) % RING * 2 + 1) for z in range(RING)]
    return ahead if k == REACH else ahead + behind


def x_shift(k):
    return [(y * SIDE + x, y * SIDE + (x + k) % SIDE) for y in range(SIDE) for x in range(SIDE)]


def y_shift(k):
    return [(y * SIDE + x, (y + k) % SIDE * SIDE + x) for y in range(SIDE) for x in range(SIDE)]


def col_group(col, core_sign, k, swap):
    core = col % 2
    step = core_sign * (1 - 2 * core) * k
    return (col // 2 + RING + step) % RING * 2 + (core + swap) % 2


def row_group(row, ky, kx):
    return (row // SIDE + SIDE - ky) % SIDE * SIDE + (row % SIDE + SIDE - kx) % SIDE


def layer_mask(layer, shape):
    row = lax.broadcasted_iota(jnp.int32, shape, 0)
    return (row // RANKS_HERE) % LAYERS == layer


def stack_kernel(d0, d1, d2, d3, out_ref):
    rows = [d[layer].astype(jnp.float32) for d in (d0, d1, d2, d3) for layer in range(LAYERS)]
    out_ref[...] = jnp.concatenate(rows, axis=0).astype(jnp.bfloat16)


def sums_kernel(
    me_ref, w_ref, g_ref, pair, mine, theirs, a0, a1, a2, a3, s_ref, bz_ref, bt_ref, found, order
):
    row, col = me_ref[0], me_ref[1]

    def put(group, slab):
        for layer in range(LAYERS):
            found[group, layer * RANKS_HERE : (layer + 1) * RANKS_HERE, :] = slab[layer].astype(jnp.float32)

    for swap in range(2):
        put(col_group(col, 1, 0, swap), pair[swap])
        for k in range(1, REACH):
            put(col_group(col, -1, k, swap), mine[k - 1, swap])
            put(col_group(col, 1, k, 1 - swap), theirs[k - 1, swap])
        far = mine[REACH - 1, swap].astype(jnp.float32) + theirs[REACH - 1, 1 - swap].astype(jnp.float32)
        put(col_group(col, -1, REACH, swap), far)
    for ky in range(SIDE):
        for kx in range(SIDE):
            order[ky * SIDE + kx] = found[row_group(row, ky, kx)]
    here, there = (x[...].reshape(bz_ref.shape[1:]) for x in (found, order))
    for layer in range(LAYERS):
        mask = layer_mask(layer, here.shape)
        bz_ref[layer] = jnp.where(mask, here, 0.0).astype(jnp.bfloat16)
        bt_ref[layer] = jnp.where(mask, there, 0.0).T.astype(jnp.bfloat16)

    for start in range(0, w_ref.shape[2], BLOCK):
        here = pl.ds(start, BLOCK)
        a = jnp.concatenate([x[:, here] for x in (a0, a1, a2, a3)], axis=0)
        rows = []
        for layer in range(LAYERS):
            merged = w_ref[layer, :, here].astype(jnp.float32) + jnp.dot(
                bt_ref[layer], a, preferred_element_type=jnp.float32
            )
            cot = g_ref[layer, :, here].astype(jnp.float32)
            rows.append(jnp.sum(merged * merged, axis=0, keepdims=True))
            rows.append(jnp.sum(cot * merged, axis=0, keepdims=True))
        sums = jnp.concatenate(rows, axis=0)
        s_ref[:, :, here] = jnp.broadcast_to(sums[None], (GROUPS, 2 * LAYERS, BLOCK))


def grads_kernel(
    me_ref, w_ref, g_ref, bz_ref, bt_ref, a0, a1, a2, a3, s_ref, mag_ref,
    ta_ref, self_ref, keep_ref, send_ref, gmag_ref, total,
):
    for start in range(0, w_ref.shape[2], BLOCK):
        here = pl.ds(start, BLOCK)
        a = jnp.concatenate([x[:, here] for x in (a0, a1, a2, a3)], axis=0)
        a_wide = a.astype(jnp.float32)
        sums = jnp.sum(s_ref[:, :, here], axis=0)
        term_a = None
        term_b = None
        for layer in range(LAYERS):
            squares = sums[2 * layer : 2 * layer + 1]
            inner = sums[2 * layer + 1 : 2 * layer + 2]
            norm = jnp.sqrt(squares + epsilon)
            scale = mag_ref[layer : layer + 1, here] / norm
            shrink = scale * inner / (norm * norm)
            gmag_ref[layer : layer + 1, here] = inner / norm
            merged = w_ref[layer, :, here].astype(jnp.float32) + jnp.dot(
                bt_ref[layer], a, preferred_element_type=jnp.float32
            )
            cot = g_ref[layer, :, here].astype(jnp.float32)
            grad = (scale * cot - shrink * merged).astype(jnp.bfloat16)
            az = jnp.where(layer_mask(layer, a_wide.shape), a_wide, 0.0).astype(jnp.bfloat16)
            part_a = jnp.dot(bz_ref[layer], grad, preferred_element_type=jnp.float32)
            part_b = lax.dot_general(
                az, grad, (((1,), (1,)), ((), ())), preferred_element_type=jnp.float32
            )
            term_a = part_a if term_a is None else term_a + part_a
            term_b = part_b if term_b is None else term_b + part_b
        ta_ref[:, :, here] = term_a.reshape(GROUPS, SLAB, BLOCK)
        term_b = term_b.reshape(total.shape)
        if start == 0:
            total[...] = term_b
        else:
            total[...] += term_b
    row, col = me_ref[0], me_ref[1]

    def sum_for(group):
        ky = (row // SIDE + SIDE - group // SIDE) % SIDE
        kx = (row % SIDE + SIDE - group % SIDE) % SIDE
        return total[ky * SIDE + kx]

    for swap in range(2):
        self_ref[swap] = sum_for(col_group(col, 1, 0, swap))
        for k in range(1, REACH + 1):
            keep_ref[k - 1, swap] = sum_for(col_group(col, 1, k, swap))
            send_ref[k - 1, swap] = sum_for(col_group(col, -1, k, 1 - swap))


def on_device(weight, cotangent, up, down, magnitude):
    layers, height, width = weight.shape
    me = jnp.stack([lax.axis_index("row"), lax.axis_index("col")]).astype(jnp.int32)
    params = pltpu.CompilerParams(vmem_limit_bytes=VMEM_BYTES)

    up = jnp.swapaxes(up, 1, 2)
    pair = jnp.stack([up, lax.ppermute(up, "col", SWAP_CORE)])
    mine = jnp.stack([lax.ppermute(pair, "col", z_apart(k)) for k in range(1, REACH + 1)])
    theirs = lax.ppermute(mine, "col", SWAP_CORE)

    near = [down] + [lax.ppermute(down, "row", x_shift(k)) for k in range(1, SIDE)]
    near = pl.pallas_call(
        stack_kernel,
        in_specs=[IN_VMEM] * SIDE,
        out_specs=IN_VMEM,
        out_shape=jax.ShapeDtypeStruct((SIDE * SLAB, width), down.dtype),
        compiler_params=params,
        cost_estimate=pl.CostEstimate(flops=10**10, bytes_accessed=10**6, transcendentals=0),
        name="stack",
    )(*near)
    downs = [near] + [lax.ppermute(near, "row", y_shift(k)) for k in range(1, SIDE)]

    sums, up_rows, up_columns = pl.pallas_call(
        sums_kernel,
        in_specs=[IN_SMEM] + [IN_VMEM] * 9,
        out_specs=[IN_VMEM] * 3,
        out_shape=[
            jax.ShapeDtypeStruct((GROUPS, 2 * layers, width), jnp.float32),
            jax.ShapeDtypeStruct((layers, DEPTH, height), jnp.bfloat16),
            jax.ShapeDtypeStruct((layers, height, DEPTH), jnp.bfloat16),
        ],
        scratch_shapes=[pltpu.VMEM((GROUPS, SLAB, height), jnp.float32)] * 2,
        compiler_params=params,
        name="column_sums",
    )(me, weight, cotangent, pair, mine, theirs, *downs)

    sums_all = lax.all_to_all(sums, "row", 0, 0)

    term_a, self_b, keep_b, send_b, mags = pl.pallas_call(
        grads_kernel,
        in_specs=[IN_SMEM] + [IN_VMEM] * 10,
        out_specs=[IN_VMEM] * 5,
        out_shape=[
            jax.ShapeDtypeStruct((GROUPS, SLAB, width), jnp.float32),
            jax.ShapeDtypeStruct((2, SLAB, height), jnp.float32),
            *[jax.ShapeDtypeStruct((REACH, 2, SLAB, height), jnp.float32)] * 2,
            jax.ShapeDtypeStruct((layers, width), jnp.float32),
        ],
        scratch_shapes=[pltpu.VMEM((GROUPS, SLAB, height), jnp.float32)],
        compiler_params=params,
        name="gradients",
    )(me, weight, cotangent, up_rows, up_columns, *downs, sums_all, magnitude)

    sum_core = keep_b + lax.ppermute(send_b, "col", SWAP_CORE)
    for k in range(1, REACH + 1):
        self_b = self_b + lax.ppermute(sum_core[k - 1], "col", z_apart(k))
    grad_b = self_b[0] + lax.ppermute(self_b[1], "col", SWAP_CORE)

    grad_a = jnp.sum(lax.all_to_all(term_a, "row", 0, 0), axis=0)
    grad_b = grad_b.reshape(layers, RANKS_HERE, height)
    return jnp.swapaxes(grad_b, 1, 2), grad_a.reshape(layers, RANKS_HERE, width), mags


def solution(mesh):
    in_specs = (
        P(None, "row", "col"),
        P(None, "row", "col"),
        P(None, "row", "col"),
        P(None, "row", "col"),
        P(None, "col"),
    )
    out_specs = (P(None, "row", "col"), P(None, "row", "col"), P(None, "col"))
    return jax.shard_map(
        on_device, mesh=mesh, in_specs=in_specs, out_specs=out_specs, check_vma=False
    )
```

time: 359 us -> 78.2 us (0.22)
  waiting for transfers between devices: 205 us -> 4.25 us
  blocking collectives: 104 us -> 12.5 us
  starting transfers between devices: 0.08 us -> 46.1 us
  matrix products: 15.1 us -> 0 us
  between operations: 15.5 us -> 0.8 us
  Pallas kernels: 0 us -> 10.7 us
  local copies, waits for them, and re-layouts: 9.66 us -> 2.06 us
  other arithmetic: 8.64 us -> 1.13 us
    unnamed x4 -> x0, waiting for transfers between devices: 205 us -> none
    psum x1 -> x0, blocking collectives: 58.1 us -> none  [on_device(): squares, inner = lax.psum((squares, inner), 'row')]
    all_gather x2 -> x0, blocking collectives: 46.3 us -> none  [the longest x1 26.3 us: on_device(): lax.all_gather(adapter_up_matrix, 'col', axis=2, tiled=True)]
    ppermute x0 -> x18, starting transfers between devices: none -> 42.5 us  [the longest x4 8.45 us: on_device(): self_b = self_b + lax.ppermute(sum_core[k - 1], 'col', z_apart(k))]
    dot_general x6 -> x0, matrix products: 15.1 us -> none  [the longest x2 7.14 us: on_device(): jnp.dot(left_here, right_here, preferred_element_type=jnp.float32)]
    all_to_all x0 -> x1, blocking collectives: none -> 12.5 us  [on_device(): sums_all = lax.all_to_all(sums, 'row', 0, 0)]
    pallas_call x0 -> x3, Pallas kernels: none -> 10.7 us  [the longest x1 6.98 us: on_device(): pl.pallas_call(grads_kernel, in_specs=[IN_SMEM] + [IN_VMEM] * 10, out_spe...]
    convert_element_type x1 -> x0, other arithmetic: 6.75 us -> none  [on_device(): grad_merged = (scale * cot_float - shrink * merged).astype(jnp.bfloat16)]
  transfers between devices with their start and end apart: 2 -> 19, of which waited for: 2 -> 3; matrix products, arithmetic and copies ran while one was open for 2% -> 2% of each run, Pallas kernels for 0% -> 0%
where the time goes in v2:
time: 78.2 us; the launch traced here: 77.6 us
  starting transfers between devices  46.1 us (59%)
  blocking collectives  12.5 us (16%)
  Pallas kernels  10.7 us (14%)
  waiting for transfers between devices  4.25 us (5%)
  local copies, waits for them, and re-layouts  2.06 us (3%)
  other arithmetic  1.13 us (1%)
  between operations  0.8 us (1%)
    all_to_all x1, blocking collectives, on_device(): sums_all = lax.all_to_all(sums, 'row', 0, 0)  12.5 us
    ppermute x4, starting transfers between devices, on_device(): self_b = self_b + lax.ppermute(sum_core[k - 1], 'col', z_apart(k))  8.45 us
    ppermute x4, starting transfers between devices, on_device(): lax.ppermute(pair, 'col', z_apart(k))  8.15 us
    pallas_call x1, Pallas kernels, on_device(): pl.pallas_call(grads_kernel, in_specs=[IN_SMEM] + [IN_VMEM] * 10, out_spe...  6.98 us
    ppermute x1, starting transfers between devices, on_device(): theirs = lax.ppermute(mine, 'col', SWAP_CORE)  6.06 us
    ppermute x1, starting transfers between devices, on_device(): grad_b = self_b[0] + lax.ppermute(self_b[1], 'col', SWAP_CORE)  4.58 us
    ppermute x1, starting transfers between devices, on_device(): sum_core = keep_b + lax.ppermute(send_b, 'col', SWAP_CORE)  4.37 us
    ppermute x3, starting transfers between devices, on_device(): lax.ppermute(near, 'row', y_shift(k))  3.85 us
  transfers between devices with their start and end apart: 19, of which 3 were waited for; matrix products, arithmetic and copies ran while one was open for 2% of the time, Pallas kernels for 0%

profile of v2, /device:TPU:1, one launch (start us, length us, event | category | flops | bytes accessed | tf_op | source)
XLA Modules:
  0.0 77.6 jit_solution(12659921896100935038)
XLA Ops:
  0.6 3.3 %collective-permute-start = (bf16[2,4,768]{2,1,0:T(4,128)(2,1)}, bf16[2,4,768]{2,1,0:T(4,128)(2,1)S(1)}, u32[]{:S(2)}, u32[]{:S(2)}) collective-permute-start(bf16[2,4,768]{2,1,0:T(4,128)(2,1)} %bitcast.34), channel_id=1, source_target_pairs={{0,1},{1,0},{2,3},{3,2},{4,5},{5,4},{6,7},{7,6},{8,9},{9,8},{10,11... | collective-permute-start | bytes 36872 | tf_op jit(solution)/shard_map/ppermute | solution.py:155
  4.0 1.0 %collective-permute-start.7 = (bf16[2,4,1792]{2,1,0:T(4,128)(2,1)}, bf16[2,4,1792]{2,1,0:T(4,128)(2,1)S(1)}, u32[]{:S(2)}, u32[]{:S(2)}) collective-permute-start(bf16[2,4,1792]{2,1,0:T(4,128)(2,1)} %d0.1), channel_id=1, source_target_pairs={{0,32},{16,48},{32,0},{48,16},{64,96},{80,112},{96,64},{112,80},{1... | collective-permute-start | bytes 86024 | tf_op jit(solution)/shard_map/ppermute | solution.py:159
  5.0 0.3 collective-permute-start.6
  5.3 2.4 %collective-permute-start.8 = (bf16[2,4,1792]{2,1,0:T(4,128)(2,1)}, bf16[2,4,1792]{2,1,0:T(4,128)(2,1)S(1)}, u32[]{:S(2)}, u32[]{:S(2)}) collective-permute-start(bf16[2,4,1792]{2,1,0:T(4,128)(2,1)} %d0.1), channel_id=1, source_target_pairs={{0,48},{16,0},{32,16},{48,32},{64,112},{80,64},{96,80},{112,96},{1... | collective-permute-start | bytes 86024 | tf_op jit(solution)/shard_map/ppermute | solution.py:159
  7.7 0.0 collective-permute-done
  7.7 0.0 slice-start
  7.7 0.0 slice-start.2
  7.7 0.9 %pad_maximum_fusion.1.pair = bf16[2,2,4,768]{3,2,1,0:T(4,128)(2,1)S(1)} fusion(bf16[1,2,4,768]{3,2,1,0:T(4,128)(2,1)S(1)} %bitcast.36, bf16[1,2,4,768]{3,2,1,0:T(4,128)(2,1)} %bitcast.35), kind=kLoop, calls=%fused_computation.9 | loop fusion | flops 12288 | bytes 49152 | tf_op jit(solution)/shard_map/stack | solution.py:155
  8.5 0.0 slice-start.1
  8.6 0.0 slice-start.3
  8.6 0.8 %collective-permute-start.4 = (bf16[2,2,4,768]{3,2,1,0:T(4,128)(2,1)S(1)}, bf16[2,2,4,768]{3,2,1,0:T(4,128)(2,1)S(1)}, u32[]{:S(2)}, u32[]{:S(2)}) collective-permute-start(bf16[2,2,4,768]{3,2,1,0:T(4,128)(2,1)S(1)} %pad_maximum_fusion.1.pair), channel_id=1, source_target_pairs={{0,8},{2,10},{4,12},{6,14},{8,0},{10,2},{12,4},{14,6},{16,24},{18,... | collective-permute-start | bytes 73736 | tf_op jit(solution)/shard_map/ppermute | solution.py:156
  9.4 6.5 %collective-permute-start.3 = (bf16[2,2,4,768]{3,2,1,0:T(4,128)(2,1)S(1)}, bf16[2,2,4,768]{3,2,1,0:T(4,128)(2,1)S(1)}, u32[]{:S(2)}, u32[]{:S(2)}) collective-permute-start(bf16[2,2,4,768]{3,2,1,0:T(4,128)(2,1)S(1)} %pad_maximum_fusion.1.pair), channel_id=1, source_target_pairs={{0,6},{2,8},{4,10},{6,12},{8,14},{10,0},{12,2},{14,4},{1,11},{3,13... | collective-permute-start | bytes 73736 | tf_op jit(solution)/shard_map/ppermute | solution.py:156
  15.9 0.0 collective-permute-done.7.d2
  15.9 0.3 collective-permute-start.2
  16.2 0.0 collective-permute-done.6.d1
  16.2 0.5 collective-permute-start.1
  16.7 0.0 collective-permute-done.8.d3
  16.7 0.0 copy-start.1
  16.7 0.7 copy-done.1
  17.5 2.8 %collective-permute-start.11 = (bf16[32,1792]{1,0:T(8,128)(2,1)S(1)}, bf16[32,1792]{1,0:T(8,128)(2,1)S(1)}, u32[]{:S(2)}, u32[]{:S(2)}) collective-permute-start(bf16[32,1792]{1,0:T(8,128)(2,1)S(1)} %stack.45.a0), channel_id=1, source_target_pairs={{0,192},{16,208},{32,224},{48,240},{64,0},{80,16},{96,32},{112,48}... | collective-permute-start | bytes 344072 | tf_op jit(solution)/shard_map/ppermute | solution.py:169
  20.3 0.0 collective-permute-done.4
  20.3 0.4 collective-permute-start.10
  20.7 0.0 collective-permute-done.3
  20.7 0.7 collective-permute-start.9
  21.4 0.0 collective-permute-done.2
  21.4 0.0 collective-permute-done.1
  21.4 0.1 pad_maximum_fusion.mine
  21.5 6.1 %collective-permute-start.5 = (bf16[4,2,2,4,768]{4,3,2,1,0:T(4,128)(2,1)S(1)}, bf16[4,2,2,4,768]{4,3,2,1,0:T(4,128)(2,1)S(1)}, u32[]{:S(2)}, u32[]{:S(2)}) collective-permute-start(bf16[4,2,2,4,768]{4,3,2,1,0:T(4,128)(2,1)S(1)} %pad_maximum_fusion.mine), channel_id=1, source_target_pairs={{0,1},{1,0},{2,3},{3,2},{4,5},{5,4},{6,7},{7,6},{8,9},{9,8},{10,11... | collective-permute-start | bytes 294920 | tf_op jit(solution)/shard_map/ppermute | solution.py:157
  27.5 0.1 pad_add_fusion.me_ref
  27.6 0.0 copy-start
  27.6 0.9 %collective-permute-done.5.theirs = bf16[4,2,2,4,768]{4,3,2,1,0:T(4,128)(2,1)S(1)} collective-permute-done((bf16[4,2,2,4,768]{4,3,2,1,0:T(4,128)(2,1)S(1)}, bf16[4,2,2,4,768]{4,3,2,1,0:T(4,128)(2,1)S(1)}, u32[]{:S(2)}, u32[]{:S(2)}) %collective-permute-start.5) | collective-permute-done | bytes 98336 | tf_op jit(solution)/shard_map/ppermute | solution.py:157
  28.5 0.0 collective-permute-done.11.a3
  28.5 0.0 collective-permute-done.10.a2
  28.5 0.0 collective-permute-done.9.a1
  28.5 0.0 slice-done
  28.5 0.0 slice-done.2
  28.5 0.0 slice-done.1
  28.5 0.0 slice-done.3
  28.6 3.7 %column_sums.1 = (f32[16,4,1792]{2,1,0:T(4,128)S(1)}, bf16[2,128,768]{2,1,0:T(8,128)(2,1)S(1)}, bf16[2,768,128]{2,1,0:T(8,128)(2,1)S(1)}) custom-call(s32[2]{0:T(128)S(1)} %pad_add_fusion.me_ref, bf16[2,768,1792]{2,1,0:T(8,128)(2,1)S(1)} %bitcast.26, bf16[2,768,1792]{2,1,0:T(8,128)(2,1)S(1)} %bitcast.28, bf16[2,2,4,768]{3,2,1,0:T(4,128)(2,1)S(1)} %pad_maximum_fusion.1.pair, ...), custom_call_target="tpu_custom_call" | custom-call | tf_op jit(solution)/shard_map/column_sums/pallas_call | solution.py:171
  32.3 12.5 %all_to_all.10.s_ref = f32[16,4,1792]{2,1,0:T(4,128)S(1)} all-to-all(f32[16,4,1792]{2,1,0:T(4,128)S(1)} %get-tuple-element.13), channel_id=1, replica_groups=mesh['row'=16,'col'=16] {'row'}, dimensions={0} | all-to-all | bytes 917504 | tf_op jit(solution)/shard_map/all_to_all | solution.py:185
  44.8 0.0 copy-done
  44.8 7.0 %gradients.1 = (f32[16,8,1792]{2,1,0:T(8,128)}, f32[2,8,768]{2,1,0:T(8,128)S(1)}, f32[4,2,8,768]{3,2,1,0:T(8,128)S(1)}, f32[4,2,8,768]{3,2,1,0:T(8,128)S(1)}, f32[2,1792]{1,0:T(2,128)}) custom-call(s32[2]{0:T(128)S(1)} %pad_add_fusion.me_ref, bf16[2,768,1792]{2,1,0:T(8,128)(2,1)S(1)} %bitcast.26, bf16[2,768,1792]{2,1,0:T(8,128)(2,1)S(1)} %bitcast.28, ...), custom_call_target="tpu_custom_call" | custom-call | tf_op jit(solution)/shard_map/gradients/pallas_call | solution.py:187
  51.8 4.4 %collective-permute-start.12 = (f32[4,2,8,768]{3,2,1,0:T(8,128)S(1)}, f32[4,2,8,768]{3,2,1,0:T(8,128)S(1)}, u32[]{:S(2)}, u32[]{:S(2)}) collective-permute-start(f32[4,2,8,768]{3,2,1,0:T(8,128)S(1)} %get-tuple-element.16), channel_id=1, source_target_pairs={{0,1},{1,0},{2,3},{3,2},{4,5},{5,4},{6,7},{7,6},{8,9},{9,8},{10,11... | collective-permute-start | bytes 589832 | tf_op jit(solution)/shard_map/ppermute | solution.py:202
  56.2 3.6 %all-to-all-start.1 = ((f32[16,8,1792]{2,1,0:T(8,128)}), f32[16,8,1792]{2,1,0:T(8,128)S(1)}, u32[]{:S(2)}, u32[]{:S(2)}) async-start(f32[16,8,1792]{2,1,0:T(8,128)} %get-tuple-element.17), calls=%async_computation.1 | async-start | bytes 1835008 | tf_op jit(solution)/shard_map/all_to_all | solution.py:207
  59.8 0.0 collective-permute-done.12
  59.9 2.3 %collective-permute-start.13 = (f32[2,8,768]{2,1,0:T(8,128)S(1)}, f32[2,8,768]{2,1,0:T(8,128)S(1)}, u32[]{:S(2)}, u32[]{:S(2)}) collective-permute-start(f32[2,8,768]{2,1,0:T(8,128)S(1)} %get-tuple-element.19), channel_id=1, source_target_pairs={{0,2},{2,4},{4,6},{6,8},{8,10},{10,12},{12,14},{14,0},{1,15},{3,1}... | collective-permute-start | bytes 147464 | tf_op jit(solution)/shard_map/ppermute | solution.py:204
  62.2 0.7 collective-permute-start.16
  62.9 3.1 %collective-permute-start.15 = (f32[2,8,768]{2,1,0:T(8,128)S(1)}, f32[2,8,768]{2,1,0:T(8,128)S(1)}, u32[]{:S(2)}, u32[]{:S(2)}) collective-permute-start(f32[2,8,768]{2,1,0:T(8,128)S(1)} %get-tuple-element.21), channel_id=1, source_target_pairs={{0,6},{2,8},{4,10},{6,12},{8,14},{10,0},{12,2},{14,4},{1,11},{3,13... | collective-permute-start | bytes 147464 | tf_op jit(solution)/shard_map/ppermute | solution.py:204
  65.9 2.4 %collective-permute-start.14 = (f32[2,8,768]{2,1,0:T(8,128)S(1)}, f32[2,8,768]{2,1,0:T(8,128)S(1)}, u32[]{:S(2)}, u32[]{:S(2)}) collective-permute-start(f32[2,8,768]{2,1,0:T(8,128)S(1)} %get-tuple-element.22), channel_id=1, source_target_pairs={{0,4},{2,6},{4,8},{6,10},{8,12},{10,14},{12,0},{14,2},{1,13},{3,15... | collective-permute-start | bytes 147464 | tf_op jit(solution)/shard_map/ppermute | solution.py:204
  68.3 0.0 collective-permute-done.13
  68.3 0.0 collective-permute-done.16
  68.3 0.0 collective-permute-done.15
  68.3 2.5 %collective-permute-done.14 = f32[2,8,768]{2,1,0:T(8,128)S(1)} collective-permute-done((f32[2,8,768]{2,1,0:T(8,128)S(1)}, f32[2,8,768]{2,1,0:T(8,128)S(1)}, u32[]{:S(2)}, u32[]{:S(2)}) %collective-permute-start.14) | collective-permute-done | bytes 49184 | tf_op jit(solution)/shard_map/ppermute | solution.py:204
  70.9 4.6 %collective-permute-start.17 = (f32[8,768]{1,0:T(8,128)S(1)}, f32[8,768]{1,0:T(8,128)S(1)}, u32[]{:S(2)}, u32[]{:S(2)}) collective-permute-start(f32[8,768]{1,0:T(8,128)S(1)} %slice_bitcast_fusion.4), channel_id=1, source_target_pairs={{0,1},{1,0},{2,3},{3,2},{4,5},{5,4},{6,7},{7,6},{8,9},{9,8},{10,11... | collective-permute-start | bytes 73736 | tf_op jit(solution)/shard_map/ppermute | solution.py:205
  75.4 0.8 %collective-permute-done.17 = f32[8,768]{1,0:T(8,128)S(1)} collective-permute-done((f32[8,768]{1,0:T(8,128)S(1)}, f32[8,768]{1,0:T(8,128)S(1)}, u32[]{:S(2)}, u32[]{:S(2)}) %collective-permute-start.17) | collective-permute-done | bytes 24608 | tf_op jit(solution)/shard_map/ppermute | solution.py:205
  76.3 0.6 reshape.12
  76.9 0.0 all-to-all-done.1
  76.9 0.1 reduce_sum.9
  77.0 0.6 reshape.13
  (8 shorter events, 0.1 us)
Async XLA Ops:
  0.6 7.0 %collective-permute-start = (bf16[2,4,768]{2,1,0:T(4,128)(2,1)}, bf16[2,4,768]{2,1,0:T(4,128)(2,1)S(1)}, u32[]{:S(2)}, u32[]{:S(2)}) collective-permute-start(bf16[2,4,768]{2,1,0:T(4,128)(2,1)} %bitcast.34), channel_id=1, source_target_pairs={{0,1},{1,0},{2,3},{3,2},{4,5},{5,4},{6,7},{7,6},{8,9},{9,8},{10,11... | collective-permute-start | bytes 36872 | tf_op jit(solution)/shard_map/ppermute | solution.py:155
  4.0 12.0 %collective-permute-start.7 = (bf16[2,4,1792]{2,1,0:T(4,128)(2,1)}, bf16[2,4,1792]{2,1,0:T(4,128)(2,1)S(1)}, u32[]{:S(2)}, u32[]{:S(2)}) collective-permute-start(bf16[2,4,1792]{2,1,0:T(4,128)(2,1)} %d0.1), channel_id=1, source_target_pairs={{0,32},{16,48},{32,0},{48,16},{64,96},{80,112},{96,64},{112,80},{1... | collective-permute-start | bytes 86024 | tf_op jit(solution)/shard_map/ppermute | solution.py:159
  5.0 11.2 %collective-permute-start.6 = (bf16[2,4,1792]{2,1,0:T(4,128)(2,1)}, bf16[2,4,1792]{2,1,0:T(4,128)(2,1)S(1)}, u32[]{:S(2)}, u32[]{:S(2)}) collective-permute-start(bf16[2,4,1792]{2,1,0:T(4,128)(2,1)} %d0.1), channel_id=1, source_target_pairs={{0,16},{16,32},{32,48},{48,0},{64,80},{80,96},{96,112},{112,64},{1... | collective-permute-start | bytes 86024 | tf_op jit(solution)/shard_map/ppermute | solution.py:159
  5.3 11.4 %collective-permute-start.8 = (bf16[2,4,1792]{2,1,0:T(4,128)(2,1)}, bf16[2,4,1792]{2,1,0:T(4,128)(2,1)S(1)}, u32[]{:S(2)}, u32[]{:S(2)}) collective-permute-start(bf16[2,4,1792]{2,1,0:T(4,128)(2,1)} %d0.1), channel_id=1, source_target_pairs={{0,48},{16,0},{32,16},{48,32},{64,112},{80,64},{96,80},{112,96},{1... | collective-permute-start | bytes 86024 | tf_op jit(solution)/shard_map/ppermute | solution.py:159
  7.7 20.8 %slice-start = ((s8[5505024]{0:T(1024)(128)(4,1)}), s8[4194304]{0:T(1024)(128)(4,1)S(1)}, s32[]{:S(2)}) async-start(s8[5505024]{0:T(1024)(128)(4,1)} %bitcast.25), calls=%async_computation.2 | async-start | bytes 8388608
  7.7 20.8 %slice-start.2 = ((s8[5505024]{0:T(1024)(128)(4,1)}), s8[4194304]{0:T(1024)(128)(4,1)S(1)}, s32[]{:S(2)}) async-start(s8[5505024]{0:T(1024)(128)(4,1)} %bitcast.27), calls=%async_computation.4 | async-start | bytes 8388608
  8.5 20.0 %slice-start.1 = ((s8[5505024]{0:T(1024)(128)(4,1)}), s8[1310720]{0:T(1024)(128)(4,1)S(1)}, s32[]{:S(2)}) async-start(s8[5505024]{0:T(1024)(128)(4,1)} %bitcast.25), calls=%async_computation.3 | async-start | bytes 2621440
  8.6 20.0 %slice-start.3 = ((s8[5505024]{0:T(1024)(128)(4,1)}), s8[1310720]{0:T(1024)(128)(4,1)S(1)}, s32[]{:S(2)}) async-start(s8[5505024]{0:T(1024)(128)(4,1)} %bitcast.27), calls=%async_computation.5 | async-start | bytes 2621440
  8.6 11.8 %collective-permute-start.4 = (bf16[2,2,4,768]{3,2,1,0:T(4,128)(2,1)S(1)}, bf16[2,2,4,768]{3,2,1,0:T(4,128)(2,1)S(1)}, u32[]{:S(2)}, u32[]{:S(2)}) collective-permute-start(bf16[2,2,4,768]{3,2,1,0:T(4,128)(2,1)S(1)} %pad_maximum_fusion.1.pair), channel_id=1, source_target_pairs={{0,8},{2,10},{4,12},{6,14},{8,0},{10,2},{12,4},{14,6},{16,24},{18,... | collective-permute-start | bytes 73736 | tf_op jit(solution)/shard_map/ppermute | solution.py:156
  9.4 11.3 %collective-permute-start.3 = (bf16[2,2,4,768]{3,2,1,0:T(4,128)(2,1)S(1)}, bf16[2,2,4,768]{3,2,1,0:T(4,128)(2,1)S(1)}, u32[]{:S(2)}, u32[]{:S(2)}) collective-permute-start(bf16[2,2,4,768]{3,2,1,0:T(4,128)(2,1)S(1)} %pad_maximum_fusion.1.pair), channel_id=1, source_target_pairs={{0,6},{2,8},{4,10},{6,12},{8,14},{10,0},{12,2},{14,4},{1,11},{3,13... | collective-permute-start | bytes 73736 | tf_op jit(solution)/shard_map/ppermute | solution.py:156
  15.9 5.5 %collective-permute-start.2 = (bf16[2,2,4,768]{3,2,1,0:T(4,128)(2,1)S(1)}, bf16[2,2,4,768]{3,2,1,0:T(4,128)(2,1)S(1)}, u32[]{:S(2)}, u32[]{:S(2)}) collective-permute-start(bf16[2,2,4,768]{3,2,1,0:T(4,128)(2,1)S(1)} %pad_maximum_fusion.1.pair), channel_id=1, source_target_pairs={{0,4},{2,6},{4,8},{6,10},{8,12},{10,14},{12,0},{14,2},{1,13},{3,15... | collective-permute-start | bytes 73736 | tf_op jit(solution)/shard_map/ppermute | solution.py:156
  16.2 5.2 %collective-permute-start.1 = (bf16[2,2,4,768]{3,2,1,0:T(4,128)(2,1)S(1)}, bf16[2,2,4,768]{3,2,1,0:T(4,128)(2,1)S(1)}, u32[]{:S(2)}, u32[]{:S(2)}) collective-permute-start(bf16[2,2,4,768]{3,2,1,0:T(4,128)(2,1)S(1)} %pad_maximum_fusion.1.pair), channel_id=1, source_target_pairs={{0,2},{2,4},{4,6},{6,8},{8,10},{10,12},{12,14},{14,0},{1,15},{3,1}... | collective-permute-start | bytes 73736 | tf_op jit(solution)/shard_map/ppermute | solution.py:156
  16.7 0.7 copy-start.1
  17.5 11.0 %collective-permute-start.11 = (bf16[32,1792]{1,0:T(8,128)(2,1)S(1)}, bf16[32,1792]{1,0:T(8,128)(2,1)S(1)}, u32[]{:S(2)}, u32[]{:S(2)}) collective-permute-start(bf16[32,1792]{1,0:T(8,128)(2,1)S(1)} %stack.45.a0), channel_id=1, source_target_pairs={{0,192},{16,208},{32,224},{48,240},{64,0},{80,16},{96,32},{112,48}... | collective-permute-start | bytes 344072 | tf_op jit(solution)/shard_map/ppermute | solution.py:169
  20.3 8.2 %collective-permute-start.10 = (bf16[32,1792]{1,0:T(8,128)(2,1)S(1)}, bf16[32,1792]{1,0:T(8,128)(2,1)S(1)}, u32[]{:S(2)}, u32[]{:S(2)}) collective-permute-start(bf16[32,1792]{1,0:T(8,128)(2,1)S(1)} %stack.45.a0), channel_id=1, source_target_pairs={{0,128},{16,144},{32,160},{48,176},{64,192},{80,208},{96,224},{112... | collective-permute-start | bytes 344072 | tf_op jit(solution)/shard_map/ppermute | solution.py:169
  20.7 7.8 %collective-permute-start.9 = (bf16[32,1792]{1,0:T(8,128)(2,1)S(1)}, bf16[32,1792]{1,0:T(8,128)(2,1)S(1)}, u32[]{:S(2)}, u32[]{:S(2)}) collective-permute-start(bf16[32,1792]{1,0:T(8,128)(2,1)S(1)} %stack.45.a0), channel_id=1, source_target_pairs={{0,64},{16,80},{32,96},{48,112},{64,128},{80,144},{96,160},{112,17... | collective-permute-start | bytes 344072 | tf_op jit(solution)/shard_map/ppermute | solution.py:169
  21.5 7.0 %collective-permute-start.5 = (bf16[4,2,2,4,768]{4,3,2,1,0:T(4,128)(2,1)S(1)}, bf16[4,2,2,4,768]{4,3,2,1,0:T(4,128)(2,1)S(1)}, u32[]{:S(2)}, u32[]{:S(2)}) collective-permute-start(bf16[4,2,2,4,768]{4,3,2,1,0:T(4,128)(2,1)S(1)} %pad_maximum_fusion.mine), channel_id=1, source_target_pairs={{0,1},{1,0},{2,3},{3,2},{4,5},{5,4},{6,7},{7,6},{8,9},{9,8},{10,11... | collective-permute-start | bytes 294920 | tf_op jit(solution)/shard_map/ppermute | solution.py:157
  27.6 17.2 %copy-start = (f32[2,1792]{1,0:T(2,128)S(1)}, f32[2,1792]{1,0:T(2,128)}, u32[]{:S(2)}) copy-start(f32[2,1792]{1,0:T(2,128)} %mag_ref.1) | copy-start | bytes 43012
  51.8 8.0 %collective-permute-start.12 = (f32[4,2,8,768]{3,2,1,0:T(8,128)S(1)}, f32[4,2,8,768]{3,2,1,0:T(8,128)S(1)}, u32[]{:S(2)}, u32[]{:S(2)}) collective-permute-start(f32[4,2,8,768]{3,2,1,0:T(8,128)S(1)} %get-tuple-element.16), channel_id=1, source_target_pairs={{0,1},{1,0},{2,3},{3,2},{4,5},{5,4},{6,7},{7,6},{8,9},{9,8},{10,11... | collective-permute-start | bytes 589832 | tf_op jit(solution)/shard_map/ppermute | solution.py:202
  56.2 20.8 %all-to-all-start.1 = ((f32[16,8,1792]{2,1,0:T(8,128)}), f32[16,8,1792]{2,1,0:T(8,128)S(1)}, u32[]{:S(2)}, u32[]{:S(2)}) async-start(f32[16,8,1792]{2,1,0:T(8,128)} %get-tuple-element.17), calls=%async_computation.1 | async-start | bytes 1835008 | tf_op jit(solution)/shard_map/all_to_all | solution.py:207
  59.9 8.5 %collective-permute-start.13 = (f32[2,8,768]{2,1,0:T(8,128)S(1)}, f32[2,8,768]{2,1,0:T(8,128)S(1)}, u32[]{:S(2)}, u32[]{:S(2)}) collective-permute-start(f32[2,8,768]{2,1,0:T(8,128)S(1)} %get-tuple-element.19), channel_id=1, source_target_pairs={{0,2},{2,4},{4,6},{6,8},{8,10},{10,12},{12,14},{14,0},{1,15},{3,1}... | collective-permute-start | bytes 147464 | tf_op jit(solution)/shard_map/ppermute | solution.py:204
  62.2 6.1 %collective-permute-start.16 = (f32[2,8,768]{2,1,0:T(8,128)S(1)}, f32[2,8,768]{2,1,0:T(8,128)S(1)}, u32[]{:S(2)}, u32[]{:S(2)}) collective-permute-start(f32[2,8,768]{2,1,0:T(8,128)S(1)} %get-tuple-element.20), channel_id=1, source_target_pairs={{0,8},{2,10},{4,12},{6,14},{8,0},{10,2},{12,4},{14,6},{16,24},{18,... | collective-permute-start | bytes 147464 | tf_op jit(solution)/shard_map/ppermute | solution.py:204
  62.9 5.5 %collective-permute-start.15 = (f32[2,8,768]{2,1,0:T(8,128)S(1)}, f32[2,8,768]{2,1,0:T(8,128)S(1)}, u32[]{:S(2)}, u32[]{:S(2)}) collective-permute-start(f32[2,8,768]{2,1,0:T(8,128)S(1)} %get-tuple-element.21), channel_id=1, source_target_pairs={{0,6},{2,8},{4,10},{6,12},{8,14},{10,0},{12,2},{14,4},{1,11},{3,13... | collective-permute-start | bytes 147464 | tf_op jit(solution)/shard_map/ppermute | solution.py:204
  65.9 4.9 %collective-permute-start.14 = (f32[2,8,768]{2,1,0:T(8,128)S(1)}, f32[2,8,768]{2,1,0:T(8,128)S(1)}, u32[]{:S(2)}, u32[]{:S(2)}) collective-permute-start(f32[2,8,768]{2,1,0:T(8,128)S(1)} %get-tuple-element.22), channel_id=1, source_target_pairs={{0,4},{2,6},{4,8},{6,10},{8,12},{10,14},{12,0},{14,2},{1,13},{3,15... | collective-permute-start | bytes 147464 | tf_op jit(solution)/shard_map/ppermute | solution.py:204
  70.9 5.4 %collective-permute-start.17 = (f32[8,768]{1,0:T(8,128)S(1)}, f32[8,768]{1,0:T(8,128)S(1)}, u32[]{:S(2)}, u32[]{:S(2)}) collective-permute-start(f32[8,768]{1,0:T(8,128)S(1)} %slice_bitcast_fusion.4), channel_id=1, source_target_pairs={{0,1},{1,0},{2,3},{3,2},{4,5},{5,4},{6,7},{7,6},{8,9},{9,8},{10,11... | collective-permute-start | bytes 73736 | tf_op jit(solution)/shard_map/ppermute | solution.py:205

commit v3 on v2

v3 whole, which is shorter than its diff:
```python
import jax
import jax.numpy as jnp
from jax import lax
from jax.experimental import pallas as pl
from jax.experimental.pallas import tpu as pltpu
from jax.sharding import PartitionSpec as P

epsilon = 1e-06
LAYERS = 2
GROUPS = 16
RANKS_HERE = 4
SLAB = LAYERS * RANKS_HERE
DEPTH = GROUPS * SLAB
SIDE = 4
RING = 8
REACH = RING // 2
BLOCK = 256
VMEM_BYTES = 20 * 1024 * 1024
IN_VMEM = pl.BlockSpec(memory_space=pltpu.VMEM)
ANYWHERE = pl.BlockSpec(memory_space=pl.ANY)
IN_SMEM = pl.BlockSpec(memory_space=pltpu.SMEM)

SWAP_CORE = [(i, i ^ 1) for i in range(GROUPS)]


def z_apart(k):
    ahead = [(2 * z, (z + k) % RING * 2) for z in range(RING)]
    behind = [(2 * z + 1, (z + RING - k) % RING * 2 + 1) for z in range(RING)]
    return ahead + behind


SEEN = [(1, 0), (1, 1), (2, 0), (2, 1), (3, 0), (3, 1), (REACH, 0), (0, 0)]


def row_shift(k, second):
    pairs = []
    for row in range(GROUPS):
        y, x = row // SIDE, row % SIDE
        for col in range(GROUPS):
            along_y = (col % 2 + second) % 2
            to = (y + k) % SIDE * SIDE + x if along_y else y * SIDE + (x + k) % SIDE
            pairs.append((row * GROUPS + col, to * GROUPS + col))
    return pairs


def col_group(col, core_sign, k, swap):
    core = col % 2
    step = core_sign * (1 - 2 * core) * k
    return (col // 2 + RING + step) % RING * 2 + (core + swap) % 2


def row_group(row, col, second, first):
    core = col % 2
    ky = second * (1 - core) + first * core
    kx = first * (1 - core) + second * core
    return (row // SIDE + SIDE - ky) % SIDE * SIDE + (row % SIDE + SIDE - kx) % SIDE


def row_place(row, col, group):
    core = col % 2
    ky = (row // SIDE + SIDE - group // SIDE) % SIDE
    kx = (row % SIDE + SIDE - group % SIDE) % SIDE
    return (ky * (1 - core) + kx * core) * SIDE + kx * (1 - core) + ky * core


def layer_mask(layer, shape):
    row = lax.broadcasted_iota(jnp.int32, shape, 0)
    return (row // RANKS_HERE) % LAYERS == layer


def stack_kernel(d0, d1, d2, d3, out_ref):
    rows = [d[layer].astype(jnp.float32) for d in (d0, d1, d2, d3) for layer in range(LAYERS)]
    out_ref[...] = jnp.concatenate(rows, axis=0).astype(jnp.bfloat16)


def sums_kernel(
    me_ref, w_ref, g_ref, pair, mine, theirs, a0, a1, a2, a3, s_ref, bz_ref, bt_ref, found, order
):
    row, col = me_ref[0], me_ref[1]

    def put(group, slab):
        for layer in range(LAYERS):
            found[group, layer * RANKS_HERE : (layer + 1) * RANKS_HERE, :] = slab[layer].astype(jnp.float32)

    for at, (k, swap) in enumerate(SEEN[:-1]):
        put(col_group(col, -1, k, swap), mine[at])
        put(col_group(col, 1, k, 1 - swap), theirs[at])
    for swap in range(2):
        put(col_group(col, 1, 0, swap), pair[swap])
    for second in range(SIDE):
        for first in range(SIDE):
            order[second * SIDE + first] = found[row_group(row, col, second, first)]
    here, there = (x[...].reshape(DEPTH, found.shape[2]) for x in (found, order))
    for layer in range(LAYERS):
        mask = layer_mask(layer, here.shape)
        span = pl.ds(layer * found.shape[2], found.shape[2])
        bz_ref[:, span] = jnp.where(mask, here, 0.0).astype(jnp.bfloat16)
        bt_ref[layer] = jnp.where(mask, there, 0.0).T.astype(jnp.bfloat16)

    for start in range(0, w_ref.shape[2], BLOCK):
        here = pl.ds(start, BLOCK)
        a = jnp.concatenate([x[:, here] for x in (a0, a1, a2, a3)], axis=0)
        rows = []
        for layer in range(LAYERS):
            merged = w_ref[layer, :, here].astype(jnp.float32) + jnp.dot(
                bt_ref[layer], a, preferred_element_type=jnp.float32
            )
            cot = g_ref[layer, :, here].astype(jnp.float32)
            rows.append(jnp.sum(merged * merged, axis=0, keepdims=True))
            rows.append(jnp.sum(cot * merged, axis=0, keepdims=True))
        sums = jnp.concatenate(rows, axis=0)
        s_ref[:, :, here] = jnp.broadcast_to(sums[None], (GROUPS, 2 * LAYERS, BLOCK))


def grads_kernel(
    me_ref, w_ref, g_ref, bz_ref, bt_ref, a0, a1, a2, a3, s_ref, mag_ref,
    ta_ref, keep_ref, send_ref, gmag_ref, total,
):
    for start in range(0, w_ref.shape[2], BLOCK):
        here = pl.ds(start, BLOCK)
        a = jnp.concatenate([x[:, here] for x in (a0, a1, a2, a3)], axis=0)
        a_wide = a.astype(jnp.float32)
        sums = jnp.sum(s_ref[:, :, here], axis=0)
        grads = []
        factors = []
        for layer in range(LAYERS):
            squares = sums[2 * layer : 2 * layer + 1]
            inner = sums[2 * layer + 1 : 2 * layer + 2]
            norm = jnp.sqrt(squares + epsilon)
            scale = mag_ref[layer : layer + 1, here] / norm
            shrink = scale * inner / (norm * norm)
            gmag_ref[layer : layer + 1, here] = inner / norm
            merged = w_ref[layer, :, here].astype(jnp.float32) + jnp.dot(
                bt_ref[layer], a, preferred_element_type=jnp.float32
            )
            cot = g_ref[layer, :, here].astype(jnp.float32)
            grad = (scale * cot - shrink * merged).astype(jnp.bfloat16)
            az = jnp.where(layer_mask(layer, a_wide.shape), a_wide, 0.0).astype(jnp.bfloat16)
            grads.append(grad)
            factors.append(az)
        term_a = jnp.dot(
            bz_ref[...], jnp.concatenate(grads, axis=0), preferred_element_type=jnp.float32
        )
        ta_ref[:, :, here] = term_a.reshape(GROUPS, SLAB, BLOCK)
        term_b = lax.dot_general(
            jnp.concatenate(factors, axis=1),
            jnp.concatenate(grads, axis=1),
            (((1,), (1,)), ((), ())),
            preferred_element_type=jnp.float32,
        )
        term_b = term_b.reshape(total.shape)
        if start == 0:
            total[...] = term_b
        else:
            total[...] += term_b
    row, col = me_ref[0], me_ref[1]

    def sum_for(group):
        return total[row_place(row, col, group)]

    for at, (k, swap) in enumerate(SEEN):
        keep_ref[at] = sum_for(col_group(col, 1, k, swap))
        send_ref[at] = sum_for(col_group(col, -1, k, 1 - swap))


def combine_kernel(keep_ref, got_ref, one_ref, two_ref, three_ref, four_ref, here_ref):
    for k, ref in enumerate((one_ref, two_ref, three_ref)):
        ref[...] = keep_ref[2 * k : 2 * k + 2] + got_ref[2 * k : 2 * k + 2]
    four_ref[...] = keep_ref[6] + got_ref[6]
    here_ref[...] = keep_ref[7] + got_ref[7]


def finish_kernel(parts_ref, here_ref, got_ref, other_ref, ga_ref, gb_ref):
    sum_a = jnp.sum(parts_ref[...], axis=0)
    sum_b = here_ref[...] + got_ref[0] + other_ref[...]
    for layer in range(LAYERS):
        rows = slice(layer * RANKS_HERE, (layer + 1) * RANKS_HERE)
        ga_ref[layer] = sum_a[rows]
        gb_ref[layer] = sum_b[rows]


def on_device(weight, cotangent, up, down, magnitude):
    layers, height, width = weight.shape
    me = jnp.stack([lax.axis_index("row"), lax.axis_index("col")]).astype(jnp.int32)
    params = pltpu.CompilerParams(vmem_limit_bytes=VMEM_BYTES)

    up = jnp.swapaxes(up, 1, 2)
    pair = jnp.stack([up, lax.ppermute(up, "col", SWAP_CORE)])
    two = lax.ppermute(pair, "col", z_apart(2))
    one, three = (lax.ppermute(pair, "col", z_apart(k)) for k in (1, 3))
    four = lax.ppermute(two[0], "col", z_apart(2))
    mine = jnp.concatenate([one, two, three, four[None]])
    theirs = lax.ppermute(mine, "col", SWAP_CORE)

    near = [down] + [lax.ppermute(down, ("row", "col"), row_shift(k, 0)) for k in range(1, SIDE)]
    near = pl.pallas_call(
        stack_kernel,
        in_specs=[IN_VMEM] * SIDE,
        out_specs=IN_VMEM,
        out_shape=jax.ShapeDtypeStruct((SIDE * SLAB, width), down.dtype),
        compiler_params=params,
        cost_estimate=pl.CostEstimate(flops=10**10, bytes_accessed=10**6, transcendentals=0),
        name="stack",
    )(*near)
    downs = [near] + [lax.ppermute(near, ("row", "col"), row_shift(k, 1)) for k in range(1, SIDE)]

    sums, up_rows, up_columns = pl.pallas_call(
        sums_kernel,
        in_specs=[IN_SMEM] + [IN_VMEM] * 9,
        out_specs=[IN_VMEM] * 3,
        out_shape=[
            jax.ShapeDtypeStruct((GROUPS, 2 * layers, width), jnp.float32),
            jax.ShapeDtypeStruct((DEPTH, layers * height), jnp.bfloat16),
            jax.ShapeDtypeStruct((layers, height, DEPTH), jnp.bfloat16),
        ],
        scratch_shapes=[pltpu.VMEM((GROUPS, SLAB, height), jnp.float32)] * 2,
        compiler_params=params,
        name="column_sums",
    )(me, weight, cotangent, pair, mine, theirs, *downs)

    sums_all = lax.all_to_all(sums, "row", 0, 0)

    term_a, keep_b, send_b, mags = pl.pallas_call(
        grads_kernel,
        in_specs=[IN_SMEM] + [IN_VMEM] * 10,
        out_specs=[IN_VMEM] * 4,
        out_shape=[
            jax.ShapeDtypeStruct((GROUPS, SLAB, width), jnp.float32),
            *[jax.ShapeDtypeStruct((len(SEEN), SLAB, height), jnp.float32)] * 2,
            jax.ShapeDtypeStruct((layers, width), jnp.float32),
        ],
        scratch_shapes=[pltpu.VMEM((GROUPS, SLAB, height), jnp.float32)],
        compiler_params=params,
        name="gradients",
    )(me, weight, cotangent, up_rows, up_columns, *downs, sums_all, magnitude)

    pair_of = jax.ShapeDtypeStruct((2, SLAB, height), jnp.float32)
    one_of = jax.ShapeDtypeStruct((SLAB, height), jnp.float32)
    one, two, three, four, here_b = pl.pallas_call(
        combine_kernel,
        in_specs=[IN_VMEM] * 2,
        out_specs=[IN_VMEM] * 5,
        out_shape=[pair_of, pair_of, pair_of, one_of, one_of],
        compiler_params=params,
        name="combine",
    )(keep_b, lax.ppermute(send_b, "col", SWAP_CORE))
    parts_a = lax.all_to_all(term_a, "row", 0, 0)
    four = lax.ppermute(four, "col", z_apart(2))
    three, one = (lax.ppermute(x, "col", z_apart(k)) for x, k in ((three, 3), (one, 1)))
    two = lax.ppermute(two.at[0].add(four), "col", z_apart(2))
    got = one + two + three
    other = lax.ppermute(got[1], "col", SWAP_CORE)

    grad_a, grad_b = pl.pallas_call(
        finish_kernel,
        in_specs=[IN_VMEM] * 4,
        out_specs=[IN_VMEM] * 2,
        out_shape=[
            jax.ShapeDtypeStruct((layers, RANKS_HERE, width), jnp.float32),
            jax.ShapeDtypeStruct((layers, RANKS_HERE, height), jnp.float32),
        ],
        compiler_params=params,
        name="finish",
    )(parts_a, here_b, got, other)
    return jnp.swapaxes(grad_b, 1, 2), grad_a, mags


def solution(mesh):
    in_specs = (
        P(None, "row", "col"),
        P(None, "row", "col"),
        P(None, "row", "col"),
        P(None, "row", "col"),
        P(None, "col"),
    )
    out_specs = (P(None, "row", "col"), P(None, "row", "col"), P(None, "col"))
    return jax.shard_map(
        on_device, mesh=mesh, in_specs=in_specs, out_specs=out_specs, check_vma=False
    )
```

time: 78.2 us -> 76.5 us (0.978)
  starting transfers between devices: 46.1 us -> 43.3 us
  waiting for transfers between devices: 4.25 us -> 6.36 us
  local copies, waits for them, and re-layouts: 2.06 us -> 0.94 us
    all_to_all x1, waiting for transfers between devices: 0.01 us -> 2.37 us  [on_device(): parts_a = lax.all_to_all(term_a, 'row', 0, 0)]
    ppermute x1, starting transfers between devices: 6.06 us -> 4.61 us  [on_device(): theirs = lax.ppermute(mine, 'col', SWAP_CORE)]
    ppermute x16, starting transfers between devices: 33.1 us -> 31.7 us  [the longest x3 5.59 us: on_device(): lax.ppermute(down, ('row', 'col'), row_shift(k, 0))]
    ppermute x16, waiting for transfers between devices: 3.38 us -> 2.1 us  [the longest x1 1.11 us: on_device(): two = lax.ppermute(two.at[0].add(four), 'col', z_apart(2))]
    reshape x2 -> x0, local copies, waits for them, and re-layouts: 1.26 us -> none  [the longest x1 0.64 us: on_device(): grad_a.reshape(layers, RANKS_HERE, width)]
    ppermute x1, waiting for transfers between devices: 0.01 us -> 1.04 us  [on_device(): pair = jnp.stack([up, lax.ppermute(up, 'col', SWAP_CORE)])]
  transfers between devices with their start and end apart: 19 -> 19, of which waited for: 3 -> 6; matrix products, arithmetic and copies ran while one was open for 2% -> 0% of each run, Pallas kernels for 0% -> 0%
where the time goes in v3:
time: 76.5 us; the launch traced here: 76.2 us
  starting transfers between devices  43.3 us (57%)
  blocking collectives  13 us (17%)
  Pallas kernels  11 us (14%)
  waiting for transfers between devices  6.36 us (8%)
  local copies, waits for them, and re-layouts  0.94 us (1%)
  other arithmetic  0.88 us (1%)
  between operations  0.79 us (1%)
    all_to_all x1, blocking collectives, on_device(): sums_all = lax.all_to_all(sums, 'row', 0, 0)  13 us
    pallas_call x1, Pallas kernels, on_device(): pl.pallas_call(grads_kernel, in_specs=[IN_SMEM] + [IN_VMEM] * 10, out_spe...  6.51 us
    ppermute x3, starting transfers between devices, on_device(): lax.ppermute(down, ('row', 'col'), row_shift(k, 0))  5.59 us
    ppermute x1, starting transfers between devices, on_device(): theirs = lax.ppermute(mine, 'col', SWAP_CORE)  4.61 us
    ppermute x1, starting transfers between devices, on_device(): two = lax.ppermute(pair, 'col', z_apart(2))  4.36 us
    ppermute x1, starting transfers between devices, on_device(): lax.ppermute(send_b, 'col', SWAP_CORE)  4.17 us
    ppermute x1, starting transfers between devices, on_device(): other = lax.ppermute(got[1], 'col', SWAP_CORE)  3.88 us
    ppermute x1, starting transfers between devices, on_device(): four = lax.ppermute(four, 'col', z_apart(2))  3.88 us
  transfers between devices with their start and end apart: 19, of which 6 were waited for; matrix products, arithmetic and copies ran while one was open for 0% of the time, Pallas kernels for 0%

profile of v3, /device:TPU:1, one launch (start us, length us, event | category | flops | bytes accessed | tf_op | source)
XLA Modules:
  0.0 76.2 jit_solution(6550952416813828668)
XLA Ops:
  0.6 3.3 %collective-permute-start = (bf16[2,4,768]{2,1,0:T(4,128)(2,1)}, bf16[2,4,768]{2,1,0:T(4,128)(2,1)S(1)}, u32[]{:S(2)}, u32[]{:S(2)}) collective-permute-start(bf16[2,4,768]{2,1,0:T(4,128)(2,1)} %bitcast.20), channel_id=1, source_target_pairs={{0,1},{1,0},{2,3},{3,2},{4,5},{5,4},{6,7},{7,6},{8,9},{9,8},{10,11... | collective-permute-start | bytes 36872 | tf_op jit(solution)/shard_map/ppermute | solution.py:188
  4.0 1.0 %collective-permute-done = bf16[2,4,768]{2,1,0:T(4,128)(2,1)S(1)} collective-permute-done((bf16[2,4,768]{2,1,0:T(4,128)(2,1)}, bf16[2,4,768]{2,1,0:T(4,128)(2,1)S(1)}, u32[]{:S(2)}, u32[]{:S(2)}) %collective-permute-start) | collective-permute-done | bytes 12320 | tf_op jit(solution)/shard_map/ppermute | solution.py:188
  5.0 0.7 pad_maximum_fusion.1.pair
  5.7 4.4 %collective-permute-start.2 = (bf16[2,2,4,768]{3,2,1,0:T(4,128)(2,1)S(1)}, bf16[2,2,4,768]{3,2,1,0:T(4,128)(2,1)S(1)}, u32[]{:S(2)}, u32[]{:S(2)}) collective-permute-start(bf16[2,2,4,768]{3,2,1,0:T(4,128)(2,1)S(1)} %pad_maximum_fusion.1.pair), channel_id=1, source_target_pairs={{0,4},{2,6},{4,8},{6,10},{8,12},{10,14},{12,0},{14,2},{1,13},{3,15... | collective-permute-start | bytes 73736 | tf_op jit(solution)/shard_map/ppermute | solution.py:189
  10.1 2.9 %collective-permute-start.7 = (bf16[2,4,1792]{2,1,0:T(4,128)(2,1)}, bf16[2,4,1792]{2,1,0:T(4,128)(2,1)S(1)}, u32[]{:S(2)}, u32[]{:S(2)}) collective-permute-start(bf16[2,4,1792]{2,1,0:T(4,128)(2,1)} %d0.1), channel_id=1, source_target_pairs={{0,32},{1,129},{2,34},{3,131},{4,36},{5,133},{6,38},{7,135},{8,40}... | collective-permute-start | bytes 86024 | tf_op jit(solution)/shard_map/ppermute | solution.py:195
  13.0 0.4 collective-permute-start.6
  13.4 2.3 %collective-permute-start.8 = (bf16[2,4,1792]{2,1,0:T(4,128)(2,1)}, bf16[2,4,1792]{2,1,0:T(4,128)(2,1)S(1)}, u32[]{:S(2)}, u32[]{:S(2)}) collective-permute-start(bf16[2,4,1792]{2,1,0:T(4,128)(2,1)} %d0.1), channel_id=1, source_target_pairs={{0,48},{1,193},{2,50},{3,195},{4,52},{5,197},{6,54},{7,199},{8,56}... | collective-permute-start | bytes 86024 | tf_op jit(solution)/shard_map/ppermute | solution.py:195
  15.7 0.7 collective-permute-start.3
  16.4 0.0 collective-permute-done.2
  16.4 0.6 collective-permute-start.1
  17.0 0.0 slice-start
  17.0 0.0 slice-start.2
  17.0 0.0 slice-start.1
  17.0 0.0 slice-start.3
  17.0 0.0 collective-permute-done.7.d2
  17.0 0.1 collective-permute-start.4
  17.1 0.0 collective-permute-done.6.d1
  17.2 0.0 collective-permute-done.8.d3
  17.2 0.0 copy-start.1
  17.2 0.9 %copy-done.1 = bf16[2,4,1792]{2,1,0:T(4,128)(2,1)S(1)} copy-done((bf16[2,4,1792]{2,1,0:T(4,128)(2,1)S(1)}, bf16[2,4,1792]{2,1,0:T(4,128)(2,1)}, u32[]{:S(2)}) %copy-start.1) | copy-done | bytes 28696
  18.1 2.9 %collective-permute-start.11 = (bf16[32,1792]{1,0:T(8,128)(2,1)S(1)}, bf16[32,1792]{1,0:T(8,128)(2,1)S(1)}, u32[]{:S(2)}, u32[]{:S(2)}) collective-permute-start(bf16[32,1792]{1,0:T(8,128)(2,1)S(1)} %stack.25.a0), channel_id=1, source_target_pairs={{0,192},{1,49},{2,194},{3,51},{4,196},{5,53},{6,198},{7,55},{8,200... | collective-permute-start | bytes 344072 | tf_op jit(solution)/shard_map/ppermute | solution.py:205
  21.0 0.5 collective-permute-start.10
  21.5 0.0 collective-permute-done.3
  21.5 0.2 collective-permute-start.9
  21.8 0.0 collective-permute-done.1
  21.8 0.0 collective-permute-done.4
  21.8 0.1 pad_maximum_fusion.mine
  21.9 4.6 %collective-permute-start.5 = (bf16[7,2,4,768]{3,2,1,0:T(4,128)(2,1)S(1)}, bf16[7,2,4,768]{3,2,1,0:T(4,128)(2,1)S(1)}, u32[]{:S(2)}, u32[]{:S(2)}) collective-permute-start(bf16[7,2,4,768]{3,2,1,0:T(4,128)(2,1)S(1)} %pad_maximum_fusion.mine), channel_id=1, source_target_pairs={{0,1},{1,0},{2,3},{3,2},{4,5},{5,4},{6,7},{7,6},{8,9},{9,8},{10,11... | collective-permute-start | bytes 258056 | tf_op jit(solution)/shard_map/ppermute | solution.py:193
  26.5 0.1 pad_add_fusion.me_ref
  26.5 0.0 copy-start
  26.5 0.9 %collective-permute-done.5.theirs = bf16[7,2,4,768]{3,2,1,0:T(4,128)(2,1)S(1)} collective-permute-done((bf16[7,2,4,768]{3,2,1,0:T(4,128)(2,1)S(1)}, bf16[7,2,4,768]{3,2,1,0:T(4,128)(2,1)S(1)}, u32[]{:S(2)}, u32[]{:S(2)}) %collective-permute-start.5) | collective-permute-done | bytes 86048 | tf_op jit(solution)/shard_map/ppermute | solution.py:193
  27.4 0.0 collective-permute-done.11.a3
  27.4 0.0 collective-permute-done.10.a2
  27.4 0.0 collective-permute-done.9.a1
  27.4 0.0 slice-done
  27.4 0.0 slice-done.2
  27.4 0.0 slice-done.1
  27.4 0.0 slice-done.3
  27.5 3.7 %column_sums.1 = (f32[16,4,1792]{2,1,0:T(4,128)S(1)}, bf16[128,1536]{1,0:T(8,128)(2,1)S(1)}, bf16[2,768,128]{2,1,0:T(8,128)(2,1)S(1)}) custom-call(s32[2]{0:T(128)S(1)} %pad_add_fusion.me_ref, bf16[2,768,1792]{2,1,0:T(8,128)(2,1)S(1)} %bitcast.17, bf16[2,768,1792]{2,1,0:T(8,128)(2,1)S(1)} %bitcast.19, bf16[2,2,4,768]{3,2,1,0:T(4,128)(2,1)S(1)} %pad_maximum_fusion.1.pair, ...), custom_call_target="tpu_custom_call" | custom-call | tf_op jit(solution)/shard_map/column_sums/pallas_call | solution.py:207
  31.2 13.0 %all_to_all.10.s_ref = f32[16,4,1792]{2,1,0:T(4,128)S(1)} all-to-all(f32[16,4,1792]{2,1,0:T(4,128)S(1)} %get-tuple-element.31), channel_id=1, replica_groups=mesh['row'=16,'col'=16] {'row'}, dimensions={0} | all-to-all | bytes 917504 | tf_op jit(solution)/shard_map/all_to_all | solution.py:221
  44.2 0.0 copy-done
  44.2 6.5 %gradients.1 = (f32[16,8,1792]{2,1,0:T(8,128)}, f32[8,8,768]{2,1,0:T(8,128)S(1)}, f32[8,8,768]{2,1,0:T(8,128)S(1)}, f32[2,1792]{1,0:T(2,128)}) custom-call(s32[2]{0:T(128)S(1)} %pad_add_fusion.me_ref, bf16[2,768,1792]{2,1,0:T(8,128)(2,1)S(1)} %bitcast.17, bf16[2,768,1792]{2,1,0:T(8,128)(2,1)S(1)} %bitcast.19, ...), custom_call_target="tpu_custom_call" | custom-call | tf_op jit(solution)/shard_map/gradients/pallas_call | solution.py:223
  50.7 4.2 %collective-permute-start.12 = (f32[8,8,768]{2,1,0:T(8,128)S(1)}, f32[8,8,768]{2,1,0:T(8,128)S(1)}, u32[]{:S(2)}, u32[]{:S(2)}) collective-permute-start(f32[8,8,768]{2,1,0:T(8,128)S(1)} %get-tuple-element.34), channel_id=1, source_target_pairs={{0,1},{1,0},{2,3},{3,2},{4,5},{5,4},{6,7},{7,6},{8,9},{9,8},{10,11... | collective-permute-start | bytes 589832 | tf_op jit(solution)/shard_map/ppermute | solution.py:246
  54.9 3.6 %all-to-all-start.1 = ((f32[16,8,1792]{2,1,0:T(8,128)}), f32[16,8,1792]{2,1,0:T(8,128)S(1)}, u32[]{:S(2)}, u32[]{:S(2)}) async-start(f32[16,8,1792]{2,1,0:T(8,128)} %get-tuple-element.32), calls=%async_computation.1 | async-start | bytes 1835008 | tf_op jit(solution)/shard_map/all_to_all | solution.py:247
  58.5 0.0 collective-permute-done.12.got_ref
  58.5 3.9 %collective-permute-start.14 = (f32[8,768]{1,0:T(8,128)S(1)}, f32[8,768]{1,0:T(8,128)S(1)}, u32[]{:S(2)}, u32[]{:S(2)}) collective-permute-start(f32[8,768]{1,0:T(8,128)S(1)} %get-tuple-element.38), channel_id=1, source_target_pairs={{0,4},{2,6},{4,8},{6,10},{8,12},{10,14},{12,0},{14,2},{1,13},{3,15... | collective-permute-start | bytes 73736 | tf_op jit(solution)/shard_map/ppermute | solution.py:248
  62.4 0.0 collective-permute-start.13
  62.4 1.2 %collective-permute-start.16 = (f32[2,8,768]{2,1,0:T(8,128)S(1)}, f32[2,8,768]{2,1,0:T(8,128)S(1)}, u32[]{:S(2)}, u32[]{:S(2)}) collective-permute-start(f32[2,8,768]{2,1,0:T(8,128)S(1)} %get-tuple-element.39), channel_id=1, source_target_pairs={{0,6},{2,8},{4,10},{6,12},{8,14},{10,0},{12,2},{14,4},{1,11},{3,13... | collective-permute-start | bytes 147464 | tf_op jit(solution)/shard_map/ppermute | solution.py:249
  63.6 0.0 collective-permute-done.14
  63.7 3.6 %collective-permute-start.15 = (f32[2,8,768]{2,1,0:T(8,128)S(1)}, f32[2,8,768]{2,1,0:T(8,128)S(1)}, u32[]{:S(2)}, u32[]{:S(2)}) collective-permute-start(f32[2,8,768]{2,1,0:T(8,128)S(1)} %fusion), channel_id=1, source_target_pairs={{0,4},{2,6},{4,8},{6,10},{8,12},{10,14},{12,0},{14,2},{1,13},{3,15... | collective-permute-start | bytes 147464 | tf_op jit(solution)/shard_map/ppermute | solution.py:250
  67.2 0.0 collective-permute-done.13
  67.2 0.1 collective-permute-done.16
  67.3 1.1 %collective-permute-done.15 = f32[2,8,768]{2,1,0:T(8,128)S(1)} collective-permute-done((f32[2,8,768]{2,1,0:T(8,128)S(1)}, f32[2,8,768]{2,1,0:T(8,128)S(1)}, u32[]{:S(2)}, u32[]{:S(2)}) %collective-permute-start.15) | collective-permute-done | bytes 49184 | tf_op jit(solution)/shard_map/ppermute | solution.py:250
  68.4 3.9 %collective-permute-start.17 = (f32[8,768]{1,0:T(8,128)S(1)}, f32[8,768]{1,0:T(8,128)S(1)}, u32[]{:S(2)}, u32[]{:S(2)}) collective-permute-start(f32[8,768]{1,0:T(8,128)S(1)} %slice_bitcast_fusion), channel_id=1, source_target_pairs={{0,1},{1,0},{2,3},{3,2},{4,5},{5,4},{6,7},{7,6},{8,9},{9,8},{10,11... | collective-permute-start | bytes 73736 | tf_op jit(solution)/shard_map/ppermute | solution.py:252
  72.3 0.8 %collective-permute-done.17.other_ref = f32[8,768]{1,0:T(8,128)S(1)} collective-permute-done((f32[8,768]{1,0:T(8,128)S(1)}, f32[8,768]{1,0:T(8,128)S(1)}, u32[]{:S(2)}, u32[]{:S(2)}) %collective-permute-start.17) | collective-permute-done | bytes 24608 | tf_op jit(solution)/shard_map/ppermute | solution.py:252
  73.1 2.4 %all-to-all-done.1.parts_ref = f32[16,8,1792]{2,1,0:T(8,128)S(1)} async-done(((f32[16,8,1792]{2,1,0:T(8,128)}), f32[16,8,1792]{2,1,0:T(8,128)S(1)}, u32[]{:S(2)}, u32[]{:S(2)}) %all-to-all-start.1) | async-done | bytes 917536 | tf_op jit(solution)/shard_map/all_to_all | solution.py:247
  75.5 0.7 finish.1
  (8 shorter events, 0.1 us)
Async XLA Ops:
  0.6 4.4 %collective-permute-start = (bf16[2,4,768]{2,1,0:T(4,128)(2,1)}, bf16[2,4,768]{2,1,0:T(4,128)(2,1)S(1)}, u32[]{:S(2)}, u32[]{:S(2)}) collective-permute-start(bf16[2,4,768]{2,1,0:T(4,128)(2,1)} %bitcast.20), channel_id=1, source_target_pairs={{0,1},{1,0},{2,3},{3,2},{4,5},{5,4},{6,7},{7,6},{8,9},{9,8},{10,11... | collective-permute-start | bytes 36872 | tf_op jit(solution)/shard_map/ppermute | solution.py:188
  5.7 10.7 %collective-permute-start.2 = (bf16[2,2,4,768]{3,2,1,0:T(4,128)(2,1)S(1)}, bf16[2,2,4,768]{3,2,1,0:T(4,128)(2,1)S(1)}, u32[]{:S(2)}, u32[]{:S(2)}) collective-permute-start(bf16[2,2,4,768]{3,2,1,0:T(4,128)(2,1)S(1)} %pad_maximum_fusion.1.pair), channel_id=1, source_target_pairs={{0,4},{2,6},{4,8},{6,10},{8,12},{10,14},{12,0},{14,2},{1,13},{3,15... | collective-permute-start | bytes 73736 | tf_op jit(solution)/shard_map/ppermute | solution.py:189
  10.1 6.9 %collective-permute-start.7 = (bf16[2,4,1792]{2,1,0:T(4,128)(2,1)}, bf16[2,4,1792]{2,1,0:T(4,128)(2,1)S(1)}, u32[]{:S(2)}, u32[]{:S(2)}) collective-permute-start(bf16[2,4,1792]{2,1,0:T(4,128)(2,1)} %d0.1), channel_id=1, source_target_pairs={{0,32},{1,129},{2,34},{3,131},{4,36},{5,133},{6,38},{7,135},{8,40}... | collective-permute-start | bytes 86024 | tf_op jit(solution)/shard_map/ppermute | solution.py:195
  13.0 4.1 %collective-permute-start.6 = (bf16[2,4,1792]{2,1,0:T(4,128)(2,1)}, bf16[2,4,1792]{2,1,0:T(4,128)(2,1)S(1)}, u32[]{:S(2)}, u32[]{:S(2)}) collective-permute-start(bf16[2,4,1792]{2,1,0:T(4,128)(2,1)} %d0.1), channel_id=1, source_target_pairs={{0,16},{1,65},{2,18},{3,67},{4,20},{5,69},{6,22},{7,71},{8,24},{9,... | collective-permute-start | bytes 86024 | tf_op jit(solution)/shard_map/ppermute | solution.py:195
  13.4 3.7 %collective-permute-start.8 = (bf16[2,4,1792]{2,1,0:T(4,128)(2,1)}, bf16[2,4,1792]{2,1,0:T(4,128)(2,1)S(1)}, u32[]{:S(2)}, u32[]{:S(2)}) collective-permute-start(bf16[2,4,1792]{2,1,0:T(4,128)(2,1)} %d0.1), channel_id=1, source_target_pairs={{0,48},{1,193},{2,50},{3,195},{4,52},{5,197},{6,54},{7,199},{8,56}... | collective-permute-start | bytes 86024 | tf_op jit(solution)/shard_map/ppermute | solution.py:195
  15.7 5.9 %collective-permute-start.3 = (bf16[2,2,4,768]{3,2,1,0:T(4,128)(2,1)S(1)}, bf16[2,2,4,768]{3,2,1,0:T(4,128)(2,1)S(1)}, u32[]{:S(2)}, u32[]{:S(2)}) collective-permute-start(bf16[2,2,4,768]{3,2,1,0:T(4,128)(2,1)S(1)} %pad_maximum_fusion.1.pair), channel_id=1, source_target_pairs={{0,6},{2,8},{4,10},{6,12},{8,14},{10,0},{12,2},{14,4},{1,11},{3,13... | collective-permute-start | bytes 73736 | tf_op jit(solution)/shard_map/ppermute | solution.py:190
  16.4 5.4 %collective-permute-start.1 = (bf16[2,2,4,768]{3,2,1,0:T(4,128)(2,1)S(1)}, bf16[2,2,4,768]{3,2,1,0:T(4,128)(2,1)S(1)}, u32[]{:S(2)}, u32[]{:S(2)}) collective-permute-start(bf16[2,2,4,768]{3,2,1,0:T(4,128)(2,1)S(1)} %pad_maximum_fusion.1.pair), channel_id=1, source_target_pairs={{0,2},{2,4},{4,6},{6,8},{8,10},{10,12},{12,14},{14,0},{1,15},{3,1}... | collective-permute-start | bytes 73736 | tf_op jit(solution)/shard_map/ppermute | solution.py:190
  17.0 10.4 %slice-start = ((s8[5505024]{0:T(1024)(128)(4,1)}), s8[4194304]{0:T(1024)(128)(4,1)S(1)}, s32[]{:S(2)}) async-start(s8[5505024]{0:T(1024)(128)(4,1)} %bitcast.16), calls=%async_computation.2 | async-start | bytes 8388608
  17.0 10.5 %slice-start.2 = ((s8[5505024]{0:T(1024)(128)(4,1)}), s8[4194304]{0:T(1024)(128)(4,1)S(1)}, s32[]{:S(2)}) async-start(s8[5505024]{0:T(1024)(128)(4,1)} %bitcast.18), calls=%async_computation.4 | async-start | bytes 8388608
  17.0 10.5 %slice-start.1 = ((s8[5505024]{0:T(1024)(128)(4,1)}), s8[1310720]{0:T(1024)(128)(4,1)S(1)}, s32[]{:S(2)}) async-start(s8[5505024]{0:T(1024)(128)(4,1)} %bitcast.16), calls=%async_computation.3 | async-start | bytes 2621440
  17.0 10.4 %slice-start.3 = ((s8[5505024]{0:T(1024)(128)(4,1)}), s8[1310720]{0:T(1024)(128)(4,1)S(1)}, s32[]{:S(2)}) async-start(s8[5505024]{0:T(1024)(128)(4,1)} %bitcast.18), calls=%async_computation.5 | async-start | bytes 2621440
  17.0 4.8 %collective-permute-start.4 = (bf16[2,4,768]{2,1,0:T(4,128)(2,1)S(1)}, bf16[2,4,768]{2,1,0:T(4,128)(2,1)S(1)}, u32[]{:S(2)}, u32[]{:S(2)}) collective-permute-start(bf16[2,4,768]{2,1,0:T(4,128)(2,1)S(1)} %slice_bitcast_fusion.1), channel_id=1, source_target_pairs={{0,4},{2,6},{4,8},{6,10},{8,12},{10,14},{12,0},{14,2},{1,13},{3,15... | collective-permute-start | bytes 36872 | tf_op jit(solution)/shard_map/ppermute | solution.py:191
  17.2 0.9 %copy-start.1 = (bf16[2,4,1792]{2,1,0:T(4,128)(2,1)S(1)}, bf16[2,4,1792]{2,1,0:T(4,128)(2,1)}, u32[]{:S(2)}) copy-start(bf16[2,4,1792]{2,1,0:T(4,128)(2,1)} %d0.1) | copy-start | bytes 86020
  18.1 9.3 %collective-permute-start.11 = (bf16[32,1792]{1,0:T(8,128)(2,1)S(1)}, bf16[32,1792]{1,0:T(8,128)(2,1)S(1)}, u32[]{:S(2)}, u32[]{:S(2)}) collective-permute-start(bf16[32,1792]{1,0:T(8,128)(2,1)S(1)} %stack.25.a0), channel_id=1, source_target_pairs={{0,192},{1,49},{2,194},{3,51},{4,196},{5,53},{6,198},{7,55},{8,200... | collective-permute-start | bytes 344072 | tf_op jit(solution)/shard_map/ppermute | solution.py:205
  21.0 6.4 %collective-permute-start.10 = (bf16[32,1792]{1,0:T(8,128)(2,1)S(1)}, bf16[32,1792]{1,0:T(8,128)(2,1)S(1)}, u32[]{:S(2)}, u32[]{:S(2)}) collective-permute-start(bf16[32,1792]{1,0:T(8,128)(2,1)S(1)} %stack.25.a0), channel_id=1, source_target_pairs={{0,128},{1,33},{2,130},{3,35},{4,132},{5,37},{6,134},{7,39},{8,136... | collective-permute-start | bytes 344072 | tf_op jit(solution)/shard_map/ppermute | solution.py:205
  21.5 5.9 %collective-permute-start.9 = (bf16[32,1792]{1,0:T(8,128)(2,1)S(1)}, bf16[32,1792]{1,0:T(8,128)(2,1)S(1)}, u32[]{:S(2)}, u32[]{:S(2)}) collective-permute-start(bf16[32,1792]{1,0:T(8,128)(2,1)S(1)} %stack.25.a0), channel_id=1, source_target_pairs={{0,64},{1,17},{2,66},{3,19},{4,68},{5,21},{6,70},{7,23},{8,72},{9,... | collective-permute-start | bytes 344072 | tf_op jit(solution)/shard_map/ppermute | solution.py:205
  21.9 5.5 %collective-permute-start.5 = (bf16[7,2,4,768]{3,2,1,0:T(4,128)(2,1)S(1)}, bf16[7,2,4,768]{3,2,1,0:T(4,128)(2,1)S(1)}, u32[]{:S(2)}, u32[]{:S(2)}) collective-permute-start(bf16[7,2,4,768]{3,2,1,0:T(4,128)(2,1)S(1)} %pad_maximum_fusion.mine), channel_id=1, source_target_pairs={{0,1},{1,0},{2,3},{3,2},{4,5},{5,4},{6,7},{7,6},{8,9},{9,8},{10,11... | collective-permute-start | bytes 258056 | tf_op jit(solution)/shard_map/ppermute | solution.py:193
  26.5 17.6 %copy-start = (f32[2,1792]{1,0:T(2,128)S(1)}, f32[2,1792]{1,0:T(2,128)}, u32[]{:S(2)}) copy-start(f32[2,1792]{1,0:T(2,128)} %mag_ref.1) | copy-start | bytes 43012
  50.7 7.8 %collective-permute-start.12 = (f32[8,8,768]{2,1,0:T(8,128)S(1)}, f32[8,8,768]{2,1,0:T(8,128)S(1)}, u32[]{:S(2)}, u32[]{:S(2)}) collective-permute-start(f32[8,8,768]{2,1,0:T(8,128)S(1)} %get-tuple-element.34), channel_id=1, source_target_pairs={{0,1},{1,0},{2,3},{3,2},{4,5},{5,4},{6,7},{7,6},{8,9},{9,8},{10,11... | collective-permute-start | bytes 589832 | tf_op jit(solution)/shard_map/ppermute | solution.py:246
  54.9 20.7 %all-to-all-start.1 = ((f32[16,8,1792]{2,1,0:T(8,128)}), f32[16,8,1792]{2,1,0:T(8,128)S(1)}, u32[]{:S(2)}, u32[]{:S(2)}) async-start(f32[16,8,1792]{2,1,0:T(8,128)} %get-tuple-element.32), calls=%async_computation.1 | async-start | bytes 1835008 | tf_op jit(solution)/shard_map/all_to_all | solution.py:247
  58.5 5.1 %collective-permute-start.14 = (f32[8,768]{1,0:T(8,128)S(1)}, f32[8,768]{1,0:T(8,128)S(1)}, u32[]{:S(2)}, u32[]{:S(2)}) collective-permute-start(f32[8,768]{1,0:T(8,128)S(1)} %get-tuple-element.38), channel_id=1, source_target_pairs={{0,4},{2,6},{4,8},{6,10},{8,12},{10,14},{12,0},{14,2},{1,13},{3,15... | collective-permute-start | bytes 73736 | tf_op jit(solution)/shard_map/ppermute | solution.py:248
  62.4 4.8 %collective-permute-start.13 = (f32[2,8,768]{2,1,0:T(8,128)S(1)}, f32[2,8,768]{2,1,0:T(8,128)S(1)}, u32[]{:S(2)}, u32[]{:S(2)}) collective-permute-start(f32[2,8,768]{2,1,0:T(8,128)S(1)} %get-tuple-element.36), channel_id=1, source_target_pairs={{0,2},{2,4},{4,6},{6,8},{8,10},{10,12},{12,14},{14,0},{1,15},{3,1}... | collective-permute-start | bytes 147464 | tf_op jit(solution)/shard_map/ppermute | solution.py:249
  62.4 4.8 %collective-permute-start.16 = (f32[2,8,768]{2,1,0:T(8,128)S(1)}, f32[2,8,768]{2,1,0:T(8,128)S(1)}, u32[]{:S(2)}, u32[]{:S(2)}) collective-permute-start(f32[2,8,768]{2,1,0:T(8,128)S(1)} %get-tuple-element.39), channel_id=1, source_target_pairs={{0,6},{2,8},{4,10},{6,12},{8,14},{10,0},{12,2},{14,4},{1,11},{3,13... | collective-permute-start | bytes 147464 | tf_op jit(solution)/shard_map/ppermute | solution.py:249
  63.7 4.7 %collective-permute-start.15 = (f32[2,8,768]{2,1,0:T(8,128)S(1)}, f32[2,8,768]{2,1,0:T(8,128)S(1)}, u32[]{:S(2)}, u32[]{:S(2)}) collective-permute-start(f32[2,8,768]{2,1,0:T(8,128)S(1)} %fusion), channel_id=1, source_target_pairs={{0,4},{2,6},{4,8},{6,10},{8,12},{10,14},{12,0},{14,2},{1,13},{3,15... | collective-permute-start | bytes 147464 | tf_op jit(solution)/shard_map/ppermute | solution.py:250
  68.4 4.7 %collective-permute-start.17 = (f32[8,768]{1,0:T(8,128)S(1)}, f32[8,768]{1,0:T(8,128)S(1)}, u32[]{:S(2)}, u32[]{:S(2)}) collective-permute-start(f32[8,768]{1,0:T(8,128)S(1)} %slice_bitcast_fusion), channel_id=1, source_target_pairs={{0,1},{1,0},{2,3},{3,2},{4,5},{5,4},{6,7},{7,6},{8,9},{9,8},{10,11... | collective-permute-start | bytes 73736 | tf_op jit(solution)/shard_map/ppermute | solution.py:252

commit v4 on v3

--- a/solution.py
+++ b/solution.py
@@ -68,14 +68,24 @@
     return (row // RANKS_HERE) % LAYERS == layer
 
 
+def fetch_kernel(up_hbm, other_ref, down_hbm, pair_ref, down_ref, sems):
+    copies = [
+        pltpu.make_async_copy(up_hbm, pair_ref.at[0], sems.at[0]),
+        pltpu.make_async_copy(down_hbm, down_ref, sems.at[1]),
+    ]
+    for copy in copies:
+        copy.start()
+    pair_ref[1] = other_ref[...]
+    for copy in copies:
+        copy.wait()
+
+
 def stack_kernel(d0, d1, d2, d3, out_ref):
     rows = [d[layer].astype(jnp.float32) for d in (d0, d1, d2, d3) for layer in range(LAYERS)]
     out_ref[...] = jnp.concatenate(rows, axis=0).astype(jnp.bfloat16)
 
 
-def sums_kernel(
-    me_ref, w_ref, g_ref, pair, mine, theirs, a0, a1, a2, a3, s_ref, bz_ref, bt_ref, found, order
-):
+def prepare_kernel(me_ref, pair, mine, theirs, bz_ref, bt_ref, found, order):
     row, col = me_ref[0], me_ref[1]
 
     def put(group, slab):
@@ -97,6 +107,8 @@
         bz_ref[:, span] = jnp.where(mask, here, 0.0).astype(jnp.bfloat16)
         bt_ref[layer] = jnp.where(mask, there, 0.0).T.astype(jnp.bfloat16)
 
+
+def sums_kernel(w_ref, g_ref, bt_ref, a0, a1, a2, a3, s_ref):
     for start in range(0, w_ref.shape[2], BLOCK):
         here = pl.ds(start, BLOCK)
         a = jnp.concatenate([x[:, here] for x in (a0, a1, a2, a3)], axis=0)
@@ -179,20 +191,35 @@
         gb_ref[layer] = sum_b[rows]
 
 
+def in_hbm(x):
+    return pltpu.with_memory_space_constraint(x, pltpu.HBM)
+
+
 def on_device(weight, cotangent, up, down, magnitude):
     layers, height, width = weight.shape
     me = jnp.stack([lax.axis_index("row"), lax.axis_index("col")]).astype(jnp.int32)
     params = pltpu.CompilerParams(vmem_limit_bytes=VMEM_BYTES)
 
     up = jnp.swapaxes(up, 1, 2)
-    pair = jnp.stack([up, lax.ppermute(up, "col", SWAP_CORE)])
+    pair, own = pl.pallas_call(
+        fetch_kernel,
+        in_specs=[ANYWHERE, IN_VMEM, ANYWHERE],
+        out_specs=[IN_VMEM] * 2,
+        out_shape=[
+            jax.ShapeDtypeStruct((2, *up.shape), up.dtype),
+            jax.ShapeDtypeStruct(down.shape, down.dtype),
+        ],
+        scratch_shapes=[pltpu.SemaphoreType.DMA((2,))],
+        compiler_params=params,
+        name="fetch",
+    )(in_hbm(up), lax.ppermute(up, "col", SWAP_CORE), in_hbm(down))
     two = lax.ppermute(pair, "col", z_apart(2))
     one, three = (lax.ppermute(pair, "col", z_apart(k)) for k in (1, 3))
     four = lax.ppermute(two[0], "col", z_apart(2))
     mine = jnp.concatenate([one, two, three, four[None]])
     theirs = lax.ppermute(mine, "col", SWAP_CORE)
 
-    near = [down] + [lax.ppermute(down, ("row", "col"), row_shift(k, 0)) for k in range(1, SIDE)]
+    near = [own] + [lax.ppermute(down, ("row", "col"), row_shift(k, 0)) for k in range(1, SIDE)]
     near = pl.pallas_call(
         stack_kernel,
         in_specs=[IN_VMEM] * SIDE,
@@ -204,19 +231,27 @@
     )(*near)
     downs = [near] + [lax.ppermute(near, ("row", "col"), row_shift(k, 1)) for k in range(1, SIDE)]
 
-    sums, up_rows, up_columns = pl.pallas_call(
-        sums_kernel,
-        in_specs=[IN_SMEM] + [IN_VMEM] * 9,
-        out_specs=[IN_VMEM] * 3,
+    up_rows, up_columns = pl.pallas_call(
+        prepare_kernel,
+        in_specs=[IN_SMEM] + [IN_VMEM] * 3,
+        out_specs=[IN_VMEM] * 2,
         out_shape=[
-            jax.ShapeDtypeStruct((GROUPS, 2 * layers, width), jnp.float32),
             jax.ShapeDtypeStruct((DEPTH, layers * height), jnp.bfloat16),
             jax.ShapeDtypeStruct((layers, height, DEPTH), jnp.bfloat16),
         ],
         scratch_shapes=[pltpu.VMEM((GROUPS, SLAB, height), jnp.float32)] * 2,
         compiler_params=params,
+        name="prepare",
+    )(me, pair, mine, theirs)
+
+    sums = pl.pallas_call(
+        sums_kernel,
+        in_specs=[IN_VMEM] * 7,
+        out_specs=IN_VMEM,
+        out_shape=jax.ShapeDtypeStruct((GROUPS, 2 * layers, width), jnp.float32),
+        compiler_params=params,
         name="column_sums",
-    )(me, weight, cotangent, pair, mine, theirs, *downs)
+    )(weight, cotangent, up_columns, *downs)
 
     sums_all = lax.all_to_all(sums, "row", 0, 0)
 

time: 76.5 us -> 74.6 us (0.975)
  starting transfers between devices: 43.3 us -> 37.3 us
  waiting for transfers between devices: 6.36 us -> 9.52 us
  blocking collectives: 13 us -> 14.9 us
  local copies, waits for them, and re-layouts: 0.94 us -> 0.02 us
    ppermute x1, starting transfers between devices: 4.17 us -> 2.11 us  [on_device(): lax.ppermute(send_b, 'col', SWAP_CORE)]
    all_to_all x1, blocking collectives: 13 us -> 14.9 us  [on_device(): sums_all = lax.all_to_all(sums, 'row', 0, 0)]
    ppermute x3, waiting for transfers between devices: 0.05 us -> 1.41 us  [on_device(): lax.ppermute(down, ('row', 'col'), row_shift(k, 0))]
    ppermute x1, starting transfers between devices: 4.61 us -> 3.39 us  [on_device(): theirs = lax.ppermute(mine, 'col', SWAP_CORE)]
    ppermute x3, starting transfers between devices: 5.59 us -> 4.38 us  [on_device(): lax.ppermute(down, ('row', 'col'), row_shift(k, 0))]
    ppermute x1, starting transfers between devices: 3.88 us -> 2.69 us  [on_device(): four = lax.ppermute(four, 'col', z_apart(2))]
    unnamed x12 -> x6, local copies, waits for them, and re-layouts: 0.93 us -> 0.01 us
    ppermute x2, waiting for transfers between devices: 0.07 us -> 0.98 us  [on_device(): lax.ppermute(x, 'col', z_apart(k))]
  transfers between devices with their start and end apart: 19 -> 19, of which waited for: 6 -> 7; matrix products, arithmetic and copies ran while one was open for 0% -> 0% of each run, Pallas kernels for 0% -> 1%
where the time goes in v4:
time: 74.6 us; the launch traced here: 74.3 us
  starting transfers between devices  37.3 us (50%)
  blocking collectives  14.9 us (20%)
  Pallas kernels  11.7 us (16%)
  waiting for transfers between devices  9.52 us (13%)
  between operations  0.79 us (1%)
    all_to_all x1, blocking collectives, on_device(): sums_all = lax.all_to_all(sums, 'row', 0, 0)  14.9 us
    pallas_call x1, Pallas kernels, on_device(): pl.pallas_call(grads_kernel, in_specs=[IN_SMEM] + [IN_VMEM] * 10, out_spe...  6.51 us
    ppermute x3, starting transfers between devices, on_device(): lax.ppermute(down, ('row', 'col'), row_shift(k, 0))  4.38 us
    ppermute x1, starting transfers between devices, on_device(): two = lax.ppermute(pair, 'col', z_apart(2))  4.36 us
    ppermute x3, starting transfers between devices, on_device(): lax.ppermute(near, ('row', 'col'), row_shift(k, 1))  3.98 us
    all_to_all x1, starting transfers between devices, on_device(): parts_a = lax.all_to_all(term_a, 'row', 0, 0)  3.63 us
    ppermute x1, starting transfers between devices, on_device(): theirs = lax.ppermute(mine, 'col', SWAP_CORE)  3.39 us
    ppermute x1, starting transfers between devices, on_device(): lax.ppermute(up, 'col', SWAP_CORE)  3.33 us
  transfers between devices with their start and end apart: 19, of which 7 were waited for; matrix products, arithmetic and copies ran while one was open for 0% of the time, Pallas kernels for 1%

profile of v4, /device:TPU:1, one launch (start us, length us, event | category | flops | bytes accessed | tf_op | source)
XLA Modules:
  0.0 74.3 jit_solution(7053258129456794915)
XLA Ops:
  0.6 3.3 %collective-permute-start = (bf16[2,4,768]{2,1,0:T(4,128)(2,1)}, bf16[2,4,768]{2,1,0:T(4,128)(2,1)S(1)}, u32[]{:S(2)}, u32[]{:S(2)}) collective-permute-start(bf16[2,4,768]{2,1,0:T(4,128)(2,1)} %bitcast.13), channel_id=1, source_target_pairs={{0,1},{1,0},{2,3},{3,2},{4,5},{5,4},{6,7},{7,6},{8,9},{9,8},{10,11... | collective-permute-start | bytes 36872 | tf_op jit(solution)/shard_map/ppermute | solution.py:215
  4.0 1.0 %collective-permute-done.other_ref = bf16[2,4,768]{2,1,0:T(4,128)(2,1)S(1)} collective-permute-done((bf16[2,4,768]{2,1,0:T(4,128)(2,1)}, bf16[2,4,768]{2,1,0:T(4,128)(2,1)S(1)}, u32[]{:S(2)}, u32[]{:S(2)}) %collective-permute-start) | collective-permute-done | bytes 12320 | tf_op jit(solution)/shard_map/ppermute | solution.py:215
  5.0 0.8 %fetch.1 = (bf16[2,2,4,768]{3,2,1,0:T(4,128)(2,1)S(1)}, bf16[2,4,1792]{2,1,0:T(4,128)(2,1)S(1)}) custom-call(bf16[2,4,768]{2,1,0:T(4,128)(2,1)} %bitcast.14, bf16[2,4,768]{2,1,0:T(4,128)(2,1)S(1)} %collective-permute-done.other_ref, bf16[2,4,1792]{2,1,0:T(4,128)(2,1)} %down_hbm.1), custom_call_target="tpu_custom_call" | custom-call | tf_op jit(solution)/shard_map/fetch/pallas_call | solution.py:204
  5.8 4.4 %collective-permute-start.2 = (bf16[2,2,4,768]{3,2,1,0:T(4,128)(2,1)S(1)}, bf16[2,2,4,768]{3,2,1,0:T(4,128)(2,1)S(1)}, u32[]{:S(2)}, u32[]{:S(2)}) collective-permute-start(bf16[2,2,4,768]{3,2,1,0:T(4,128)(2,1)S(1)} %get-tuple-element.30.pair), channel_id=1, source_target_pairs={{0,4},{2,6},{4,8},{6,10},{8,12},{10,14},{12,0},{14,2},{1,13},{3,15... | collective-permute-start | bytes 73736 | tf_op jit(solution)/shard_map/ppermute | solution.py:216
  10.2 1.3 %collective-permute-start.6 = (bf16[2,4,1792]{2,1,0:T(4,128)(2,1)}, bf16[2,4,1792]{2,1,0:T(4,128)(2,1)S(1)}, u32[]{:S(2)}, u32[]{:S(2)}) collective-permute-start(bf16[2,4,1792]{2,1,0:T(4,128)(2,1)} %down_hbm.1), channel_id=1, source_target_pairs={{0,16},{1,65},{2,18},{3,67},{4,20},{5,69},{6,22},{7,71},{8,24},{9,... | collective-permute-start | bytes 86024 | tf_op jit(solution)/shard_map/ppermute | solution.py:222
  11.4 1.4 %collective-permute-start.8 = (bf16[2,4,1792]{2,1,0:T(4,128)(2,1)}, bf16[2,4,1792]{2,1,0:T(4,128)(2,1)S(1)}, u32[]{:S(2)}, u32[]{:S(2)}) collective-permute-start(bf16[2,4,1792]{2,1,0:T(4,128)(2,1)} %down_hbm.1), channel_id=1, source_target_pairs={{0,48},{1,193},{2,50},{3,195},{4,52},{5,197},{6,54},{7,199},{8,56}... | collective-permute-start | bytes 86024 | tf_op jit(solution)/shard_map/ppermute | solution.py:222
  12.9 1.6 %collective-permute-start.7 = (bf16[2,4,1792]{2,1,0:T(4,128)(2,1)}, bf16[2,4,1792]{2,1,0:T(4,128)(2,1)S(1)}, u32[]{:S(2)}, u32[]{:S(2)}) collective-permute-start(bf16[2,4,1792]{2,1,0:T(4,128)(2,1)} %down_hbm.1), channel_id=1, source_target_pairs={{0,32},{1,129},{2,34},{3,131},{4,36},{5,133},{6,38},{7,135},{8,40}... | collective-permute-start | bytes 86024 | tf_op jit(solution)/shard_map/ppermute | solution.py:222
  14.5 0.7 collective-permute-start.3
  15.3 0.0 collective-permute-done.2
  15.3 0.5 collective-permute-start.1
  15.8 0.0 collective-permute-done.6.d1
  15.8 0.1 collective-permute-start.4
  15.9 0.0 collective-permute-done.8.d3
  15.9 1.4 %collective-permute-done.7.d2 = bf16[2,4,1792]{2,1,0:T(4,128)(2,1)S(1)} collective-permute-done((bf16[2,4,1792]{2,1,0:T(4,128)(2,1)}, bf16[2,4,1792]{2,1,0:T(4,128)(2,1)S(1)}, u32[]{:S(2)}, u32[]{:S(2)}) %collective-permute-start.7) | collective-permute-done | bytes 28704 | tf_op jit(solution)/shard_map/ppermute | solution.py:222
  17.3 0.0 copy-start
  17.3 0.0 copy-start.1
  17.4 2.9 %collective-permute-start.11 = (bf16[32,1792]{1,0:T(8,128)(2,1)S(1)}, bf16[32,1792]{1,0:T(8,128)(2,1)S(1)}, u32[]{:S(2)}, u32[]{:S(2)}) collective-permute-start(bf16[32,1792]{1,0:T(8,128)(2,1)S(1)} %stack.13.a0), channel_id=1, source_target_pairs={{0,192},{1,49},{2,194},{3,51},{4,196},{5,53},{6,198},{7,55},{8,200... | collective-permute-start | bytes 344072 | tf_op jit(solution)/shard_map/ppermute | solution.py:232
  20.2 0.4 collective-permute-start.10
  20.6 0.0 collective-permute-done.3
  20.6 0.8 %collective-permute-start.9 = (bf16[32,1792]{1,0:T(8,128)(2,1)S(1)}, bf16[32,1792]{1,0:T(8,128)(2,1)S(1)}, u32[]{:S(2)}, u32[]{:S(2)}) collective-permute-start(bf16[32,1792]{1,0:T(8,128)(2,1)S(1)} %stack.13.a0), channel_id=1, source_target_pairs={{0,64},{1,17},{2,66},{3,19},{4,68},{5,21},{6,70},{7,23},{8,72},{9,... | collective-permute-start | bytes 344072 | tf_op jit(solution)/shard_map/ppermute | solution.py:232
  21.3 0.0 collective-permute-done.1
  21.3 0.0 collective-permute-done.4
  21.4 0.1 pad_maximum_fusion.mine
  21.4 3.4 %collective-permute-start.5 = (bf16[7,2,4,768]{3,2,1,0:T(4,128)(2,1)S(1)}, bf16[7,2,4,768]{3,2,1,0:T(4,128)(2,1)S(1)}, u32[]{:S(2)}, u32[]{:S(2)}) collective-permute-start(bf16[7,2,4,768]{3,2,1,0:T(4,128)(2,1)S(1)} %pad_maximum_fusion.mine), channel_id=1, source_target_pairs={{0,1},{1,0},{2,3},{3,2},{4,5},{5,4},{6,7},{7,6},{8,9},{9,8},{10,11... | collective-permute-start | bytes 258056 | tf_op jit(solution)/shard_map/ppermute | solution.py:220
  24.8 0.1 pad_add_fusion.me_ref
  24.9 0.9 %collective-permute-done.5.theirs = bf16[7,2,4,768]{3,2,1,0:T(4,128)(2,1)S(1)} collective-permute-done((bf16[7,2,4,768]{3,2,1,0:T(4,128)(2,1)S(1)}, bf16[7,2,4,768]{3,2,1,0:T(4,128)(2,1)S(1)}, u32[]{:S(2)}, u32[]{:S(2)}) %collective-permute-start.5) | collective-permute-done | bytes 86048 | tf_op jit(solution)/shard_map/ppermute | solution.py:220
  25.7 0.9 %prepare.1 = (bf16[128,1536]{1,0:T(8,128)(2,1)S(1)}, bf16[2,768,128]{2,1,0:T(8,128)(2,1)S(1)}) custom-call(s32[2]{0:T(128)S(1)} %pad_add_fusion.me_ref, bf16[2,2,4,768]{3,2,1,0:T(4,128)(2,1)S(1)} %get-tuple-element.30.pair, bf16[7,2,4,768]{3,2,1,0:T(4,128)(2,1)S(1)} %pad_maximum_fusion.mine, bf16[7,2,4,768]{3,2,1,0:T(4,128)(2,1)S(1)} %collective-permute-done.5.theirs), custom_call_target="tpu_custom_call" | custom-call | tf_op jit(solution)/shard_map/prepare/pallas_call | solution.py:234
  26.6 0.0 collective-permute-done.11.a3
  26.6 0.0 collective-permute-done.10.a2
  26.6 0.0 collective-permute-done.9.a1
  26.6 0.0 copy-done
  26.7 0.0 copy-done.1
  26.7 0.0 copy-start.2
  26.7 2.8 %column_sums.1 = f32[16,4,1792]{2,1,0:T(4,128)S(1)} custom-call(bf16[2,768,1792]{2,1,0:T(8,128)(2,1)S(1)} %copy-done, bf16[2,768,1792]{2,1,0:T(8,128)(2,1)S(1)} %copy-done.1, bf16[2,768,128]{2,1,0:T(8,128)(2,1)S(1)} %get-tuple-element.32.bt_ref, bf16[32,1792]{1,0:T(8,128)(2,1)S(1)} %stack.13.a0, bf16[32,1792]{1,0:T(8,128)(2,1)S(1)} %collective-permute-done.9.a1, ...), custom_call_target="tpu_custom_call" | custom-call | tf_op jit(solution)/shard_map/column_sums/pallas_call | solution.py:247
  29.5 14.9 %all_to_all.10.s_ref = f32[16,4,1792]{2,1,0:T(4,128)S(1)} all-to-all(f32[16,4,1792]{2,1,0:T(4,128)S(1)} %column_sums.1), channel_id=1, replica_groups=mesh['row'=16,'col'=16] {'row'}, dimensions={0} | all-to-all | bytes 917504 | tf_op jit(solution)/shard_map/all_to_all | solution.py:256
  44.4 0.0 copy-done.2
  44.4 6.5 %gradients.1 = (f32[16,8,1792]{2,1,0:T(8,128)}, f32[8,8,768]{2,1,0:T(8,128)S(1)}, f32[8,8,768]{2,1,0:T(8,128)S(1)}, f32[2,1792]{1,0:T(2,128)}) custom-call(s32[2]{0:T(128)S(1)} %pad_add_fusion.me_ref, bf16[2,768,1792]{2,1,0:T(8,128)(2,1)S(1)} %copy-done, bf16[2,768,1792]{2,1,0:T(8,128)(2,1)S(1)} %copy-done.1, ...), custom_call_target="tpu_custom_call" | custom-call | tf_op jit(solution)/shard_map/gradients/pallas_call | solution.py:258
  50.9 2.1 %collective-permute-start.12 = (f32[8,8,768]{2,1,0:T(8,128)S(1)}, f32[8,8,768]{2,1,0:T(8,128)S(1)}, u32[]{:S(2)}, u32[]{:S(2)}) collective-permute-start(f32[8,8,768]{2,1,0:T(8,128)S(1)} %get-tuple-element.36), channel_id=1, source_target_pairs={{0,1},{1,0},{2,3},{3,2},{4,5},{5,4},{6,7},{7,6},{8,9},{9,8},{10,11... | collective-permute-start | bytes 589832 | tf_op jit(solution)/shard_map/ppermute | solution.py:281
  53.0 3.6 %all-to-all-start.1 = ((f32[16,8,1792]{2,1,0:T(8,128)}), f32[16,8,1792]{2,1,0:T(8,128)S(1)}, u32[]{:S(2)}, u32[]{:S(2)}) async-start(f32[16,8,1792]{2,1,0:T(8,128)} %get-tuple-element.34), calls=%async_computation.1 | async-start | bytes 1835008 | tf_op jit(solution)/shard_map/all_to_all | solution.py:282
  56.6 0.0 collective-permute-done.12.got_ref
  56.7 2.7 %collective-permute-start.14 = (f32[8,768]{1,0:T(8,128)S(1)}, f32[8,768]{1,0:T(8,128)S(1)}, u32[]{:S(2)}, u32[]{:S(2)}) collective-permute-start(f32[8,768]{1,0:T(8,128)S(1)} %get-tuple-element.40), channel_id=1, source_target_pairs={{0,4},{2,6},{4,8},{6,10},{8,12},{10,14},{12,0},{14,2},{1,13},{3,15... | collective-permute-start | bytes 73736 | tf_op jit(solution)/shard_map/ppermute | solution.py:283
  59.4 0.7 collective-permute-start.13
  60.1 1.0 %collective-permute-start.16 = (f32[2,8,768]{2,1,0:T(8,128)S(1)}, f32[2,8,768]{2,1,0:T(8,128)S(1)}, u32[]{:S(2)}, u32[]{:S(2)}) collective-permute-start(f32[2,8,768]{2,1,0:T(8,128)S(1)} %get-tuple-element.41), channel_id=1, source_target_pairs={{0,6},{2,8},{4,10},{6,12},{8,14},{10,0},{12,2},{14,4},{1,11},{3,13... | collective-permute-start | bytes 147464 | tf_op jit(solution)/shard_map/ppermute | solution.py:284
  61.1 0.0 collective-permute-done.14
  61.1 3.1 %collective-permute-start.15 = (f32[2,8,768]{2,1,0:T(8,128)S(1)}, f32[2,8,768]{2,1,0:T(8,128)S(1)}, u32[]{:S(2)}, u32[]{:S(2)}) collective-permute-start(f32[2,8,768]{2,1,0:T(8,128)S(1)} %fusion), channel_id=1, source_target_pairs={{0,4},{2,6},{4,8},{6,10},{8,12},{10,14},{12,0},{14,2},{1,13},{3,15... | collective-permute-start | bytes 147464 | tf_op jit(solution)/shard_map/ppermute | solution.py:285
  64.2 0.0 collective-permute-done.13
  64.2 1.0 %collective-permute-done.16 = f32[2,8,768]{2,1,0:T(8,128)S(1)} collective-permute-done((f32[2,8,768]{2,1,0:T(8,128)S(1)}, f32[2,8,768]{2,1,0:T(8,128)S(1)}, u32[]{:S(2)}, u32[]{:S(2)}) %collective-permute-start.16) | collective-permute-done | bytes 49184 | tf_op jit(solution)/shard_map/ppermute | solution.py:284
  65.1 1.1 %collective-permute-done.15 = f32[2,8,768]{2,1,0:T(8,128)S(1)} collective-permute-done((f32[2,8,768]{2,1,0:T(8,128)S(1)}, f32[2,8,768]{2,1,0:T(8,128)S(1)}, u32[]{:S(2)}, u32[]{:S(2)}) %collective-permute-start.15) | collective-permute-done | bytes 49184 | tf_op jit(solution)/shard_map/ppermute | solution.py:285
  66.3 3.3 %collective-permute-start.17 = (f32[8,768]{1,0:T(8,128)S(1)}, f32[8,768]{1,0:T(8,128)S(1)}, u32[]{:S(2)}, u32[]{:S(2)}) collective-permute-start(f32[8,768]{1,0:T(8,128)S(1)} %slice_bitcast_fusion), channel_id=1, source_target_pairs={{0,1},{1,0},{2,3},{3,2},{4,5},{5,4},{6,7},{7,6},{8,9},{9,8},{10,11... | collective-permute-start | bytes 73736 | tf_op jit(solution)/shard_map/ppermute | solution.py:287
  69.6 0.8 %collective-permute-done.17.other_ref = f32[8,768]{1,0:T(8,128)S(1)} collective-permute-done((f32[8,768]{1,0:T(8,128)S(1)}, f32[8,768]{1,0:T(8,128)S(1)}, u32[]{:S(2)}, u32[]{:S(2)}) %collective-permute-start.17) | collective-permute-done | bytes 24608 | tf_op jit(solution)/shard_map/ppermute | solution.py:287
  70.4 3.2 %all-to-all-done.1.parts_ref = f32[16,8,1792]{2,1,0:T(8,128)S(1)} async-done(((f32[16,8,1792]{2,1,0:T(8,128)}), f32[16,8,1792]{2,1,0:T(8,128)S(1)}, u32[]{:S(2)}, u32[]{:S(2)}) %all-to-all-start.1) | async-done | bytes 917536 | tf_op jit(solution)/shard_map/all_to_all | solution.py:282
  73.7 0.7 finish.1
  (6 shorter events, 0.1 us)
Async XLA Ops:
  0.6 4.4 %collective-permute-start = (bf16[2,4,768]{2,1,0:T(4,128)(2,1)}, bf16[2,4,768]{2,1,0:T(4,128)(2,1)S(1)}, u32[]{:S(2)}, u32[]{:S(2)}) collective-permute-start(bf16[2,4,768]{2,1,0:T(4,128)(2,1)} %bitcast.13), channel_id=1, source_target_pairs={{0,1},{1,0},{2,3},{3,2},{4,5},{5,4},{6,7},{7,6},{8,9},{9,8},{10,11... | collective-permute-start | bytes 36872 | tf_op jit(solution)/shard_map/ppermute | solution.py:215
  5.8 9.5 %collective-permute-start.2 = (bf16[2,2,4,768]{3,2,1,0:T(4,128)(2,1)S(1)}, bf16[2,2,4,768]{3,2,1,0:T(4,128)(2,1)S(1)}, u32[]{:S(2)}, u32[]{:S(2)}) collective-permute-start(bf16[2,2,4,768]{3,2,1,0:T(4,128)(2,1)S(1)} %get-tuple-element.30.pair), channel_id=1, source_target_pairs={{0,4},{2,6},{4,8},{6,10},{8,12},{10,14},{12,0},{14,2},{1,13},{3,15... | collective-permute-start | bytes 73736 | tf_op jit(solution)/shard_map/ppermute | solution.py:216
  10.2 5.7 %collective-permute-start.6 = (bf16[2,4,1792]{2,1,0:T(4,128)(2,1)}, bf16[2,4,1792]{2,1,0:T(4,128)(2,1)S(1)}, u32[]{:S(2)}, u32[]{:S(2)}) collective-permute-start(bf16[2,4,1792]{2,1,0:T(4,128)(2,1)} %down_hbm.1), channel_id=1, source_target_pairs={{0,16},{1,65},{2,18},{3,67},{4,20},{5,69},{6,22},{7,71},{8,24},{9,... | collective-permute-start | bytes 86024 | tf_op jit(solution)/shard_map/ppermute | solution.py:222
  11.4 4.5 %collective-permute-start.8 = (bf16[2,4,1792]{2,1,0:T(4,128)(2,1)}, bf16[2,4,1792]{2,1,0:T(4,128)(2,1)S(1)}, u32[]{:S(2)}, u32[]{:S(2)}) collective-permute-start(bf16[2,4,1792]{2,1,0:T(4,128)(2,1)} %down_hbm.1), channel_id=1, source_target_pairs={{0,48},{1,193},{2,50},{3,195},{4,52},{5,197},{6,54},{7,199},{8,56}... | collective-permute-start | bytes 86024 | tf_op jit(solution)/shard_map/ppermute | solution.py:222
  12.9 4.4 %collective-permute-start.7 = (bf16[2,4,1792]{2,1,0:T(4,128)(2,1)}, bf16[2,4,1792]{2,1,0:T(4,128)(2,1)S(1)}, u32[]{:S(2)}, u32[]{:S(2)}) collective-permute-start(bf16[2,4,1792]{2,1,0:T(4,128)(2,1)} %down_hbm.1), channel_id=1, source_target_pairs={{0,32},{1,129},{2,34},{3,131},{4,36},{5,133},{6,38},{7,135},{8,40}... | collective-permute-start | bytes 86024 | tf_op jit(solution)/shard_map/ppermute | solution.py:222
  14.5 6.0 %collective-permute-start.3 = (bf16[2,2,4,768]{3,2,1,0:T(4,128)(2,1)S(1)}, bf16[2,2,4,768]{3,2,1,0:T(4,128)(2,1)S(1)}, u32[]{:S(2)}, u32[]{:S(2)}) collective-permute-start(bf16[2,2,4,768]{3,2,1,0:T(4,128)(2,1)S(1)} %get-tuple-element.30.pair), channel_id=1, source_target_pairs={{0,6},{2,8},{4,10},{6,12},{8,14},{10,0},{12,2},{14,4},{1,11},{3,13... | collective-permute-start | bytes 73736 | tf_op jit(solution)/shard_map/ppermute | solution.py:217
  15.3 6.1 %collective-permute-start.1 = (bf16[2,2,4,768]{3,2,1,0:T(4,128)(2,1)S(1)}, bf16[2,2,4,768]{3,2,1,0:T(4,128)(2,1)S(1)}, u32[]{:S(2)}, u32[]{:S(2)}) collective-permute-start(bf16[2,2,4,768]{3,2,1,0:T(4,128)(2,1)S(1)} %get-tuple-element.30.pair), channel_id=1, source_target_pairs={{0,2},{2,4},{4,6},{6,8},{8,10},{10,12},{12,14},{14,0},{1,15},{3,1}... | collective-permute-start | bytes 73736 | tf_op jit(solution)/shard_map/ppermute | solution.py:217
  15.8 5.5 %collective-permute-start.4 = (bf16[2,4,768]{2,1,0:T(4,128)(2,1)S(1)}, bf16[2,4,768]{2,1,0:T(4,128)(2,1)S(1)}, u32[]{:S(2)}, u32[]{:S(2)}) collective-permute-start(bf16[2,4,768]{2,1,0:T(4,128)(2,1)S(1)} %slice_bitcast_fusion.1), channel_id=1, source_target_pairs={{0,4},{2,6},{4,8},{6,10},{8,12},{10,14},{12,0},{14,2},{1,13},{3,15... | collective-permute-start | bytes 36872 | tf_op jit(solution)/shard_map/ppermute | solution.py:218
  17.3 9.3 %copy-start = (bf16[2,768,1792]{2,1,0:T(8,128)(2,1)S(1)}, bf16[2,768,1792]{2,1,0:T(8,128)(2,1)}, u32[]{:S(2)}) copy-start(bf16[2,768,1792]{2,1,0:T(8,128)(2,1)} %w_ref.3) | copy-start | bytes 16515076
  17.3 9.3 %copy-start.1 = (bf16[2,768,1792]{2,1,0:T(8,128)(2,1)S(1)}, bf16[2,768,1792]{2,1,0:T(8,128)(2,1)}, u32[]{:S(2)}) copy-start(bf16[2,768,1792]{2,1,0:T(8,128)(2,1)} %g_ref.3) | copy-start | bytes 16515076
  17.4 9.2 %collective-permute-start.11 = (bf16[32,1792]{1,0:T(8,128)(2,1)S(1)}, bf16[32,1792]{1,0:T(8,128)(2,1)S(1)}, u32[]{:S(2)}, u32[]{:S(2)}) collective-permute-start(bf16[32,1792]{1,0:T(8,128)(2,1)S(1)} %stack.13.a0), channel_id=1, source_target_pairs={{0,192},{1,49},{2,194},{3,51},{4,196},{5,53},{6,198},{7,55},{8,200... | collective-permute-start | bytes 344072 | tf_op jit(solution)/shard_map/ppermute | solution.py:232
  20.2 6.4 %collective-permute-start.10 = (bf16[32,1792]{1,0:T(8,128)(2,1)S(1)}, bf16[32,1792]{1,0:T(8,128)(2,1)S(1)}, u32[]{:S(2)}, u32[]{:S(2)}) collective-permute-start(bf16[32,1792]{1,0:T(8,128)(2,1)S(1)} %stack.13.a0), channel_id=1, source_target_pairs={{0,128},{1,33},{2,130},{3,35},{4,132},{5,37},{6,134},{7,39},{8,136... | collective-permute-start | bytes 344072 | tf_op jit(solution)/shard_map/ppermute | solution.py:232
  20.6 6.0 %collective-permute-start.9 = (bf16[32,1792]{1,0:T(8,128)(2,1)S(1)}, bf16[32,1792]{1,0:T(8,128)(2,1)S(1)}, u32[]{:S(2)}, u32[]{:S(2)}) collective-permute-start(bf16[32,1792]{1,0:T(8,128)(2,1)S(1)} %stack.13.a0), channel_id=1, source_target_pairs={{0,64},{1,17},{2,66},{3,19},{4,68},{5,21},{6,70},{7,23},{8,72},{9,... | collective-permute-start | bytes 344072 | tf_op jit(solution)/shard_map/ppermute | solution.py:232
  21.4 4.3 %collective-permute-start.5 = (bf16[7,2,4,768]{3,2,1,0:T(4,128)(2,1)S(1)}, bf16[7,2,4,768]{3,2,1,0:T(4,128)(2,1)S(1)}, u32[]{:S(2)}, u32[]{:S(2)}) collective-permute-start(bf16[7,2,4,768]{3,2,1,0:T(4,128)(2,1)S(1)} %pad_maximum_fusion.mine), channel_id=1, source_target_pairs={{0,1},{1,0},{2,3},{3,2},{4,5},{5,4},{6,7},{7,6},{8,9},{9,8},{10,11... | collective-permute-start | bytes 258056 | tf_op jit(solution)/shard_map/ppermute | solution.py:220
  26.7 17.7 %copy-start.2 = (f32[2,1792]{1,0:T(2,128)S(1)}, f32[2,1792]{1,0:T(2,128)}, u32[]{:S(2)}) copy-start(f32[2,1792]{1,0:T(2,128)} %mag_ref.1) | copy-start | bytes 43012
  50.9 5.8 %collective-permute-start.12 = (f32[8,8,768]{2,1,0:T(8,128)S(1)}, f32[8,8,768]{2,1,0:T(8,128)S(1)}, u32[]{:S(2)}, u32[]{:S(2)}) collective-permute-start(f32[8,8,768]{2,1,0:T(8,128)S(1)} %get-tuple-element.36), channel_id=1, source_target_pairs={{0,1},{1,0},{2,3},{3,2},{4,5},{5,4},{6,7},{7,6},{8,9},{9,8},{10,11... | collective-permute-start | bytes 589832 | tf_op jit(solution)/shard_map/ppermute | solution.py:281
  53.0 20.7 %all-to-all-start.1 = ((f32[16,8,1792]{2,1,0:T(8,128)}), f32[16,8,1792]{2,1,0:T(8,128)S(1)}, u32[]{:S(2)}, u32[]{:S(2)}) async-start(f32[16,8,1792]{2,1,0:T(8,128)} %get-tuple-element.34), calls=%async_computation.1 | async-start | bytes 1835008 | tf_op jit(solution)/shard_map/all_to_all | solution.py:282
  56.7 4.4 %collective-permute-start.14 = (f32[8,768]{1,0:T(8,128)S(1)}, f32[8,768]{1,0:T(8,128)S(1)}, u32[]{:S(2)}, u32[]{:S(2)}) collective-permute-start(f32[8,768]{1,0:T(8,128)S(1)} %get-tuple-element.40), channel_id=1, source_target_pairs={{0,4},{2,6},{4,8},{6,10},{8,12},{10,14},{12,0},{14,2},{1,13},{3,15... | collective-permute-start | bytes 73736 | tf_op jit(solution)/shard_map/ppermute | solution.py:283
  59.4 4.8 %collective-permute-start.13 = (f32[2,8,768]{2,1,0:T(8,128)S(1)}, f32[2,8,768]{2,1,0:T(8,128)S(1)}, u32[]{:S(2)}, u32[]{:S(2)}) collective-permute-start(f32[2,8,768]{2,1,0:T(8,128)S(1)} %get-tuple-element.38), channel_id=1, source_target_pairs={{0,2},{2,4},{4,6},{6,8},{8,10},{10,12},{12,14},{14,0},{1,15},{3,1}... | collective-permute-start | bytes 147464 | tf_op jit(solution)/shard_map/ppermute | solution.py:284
  60.1 5.0 %collective-permute-start.16 = (f32[2,8,768]{2,1,0:T(8,128)S(1)}, f32[2,8,768]{2,1,0:T(8,128)S(1)}, u32[]{:S(2)}, u32[]{:S(2)}) collective-permute-start(f32[2,8,768]{2,1,0:T(8,128)S(1)} %get-tuple-element.41), channel_id=1, source_target_pairs={{0,6},{2,8},{4,10},{6,12},{8,14},{10,0},{12,2},{14,4},{1,11},{3,13... | collective-permute-start | bytes 147464 | tf_op jit(solution)/shard_map/ppermute | solution.py:284
  61.1 5.2 %collective-permute-start.15 = (f32[2,8,768]{2,1,0:T(8,128)S(1)}, f32[2,8,768]{2,1,0:T(8,128)S(1)}, u32[]{:S(2)}, u32[]{:S(2)}) collective-permute-start(f32[2,8,768]{2,1,0:T(8,128)S(1)} %fusion), channel_id=1, source_target_pairs={{0,4},{2,6},{4,8},{6,10},{8,12},{10,14},{12,0},{14,2},{1,13},{3,15... | collective-permute-start | bytes 147464 | tf_op jit(solution)/shard_map/ppermute | solution.py:285
  66.3 4.1 %collective-permute-start.17 = (f32[8,768]{1,0:T(8,128)S(1)}, f32[8,768]{1,0:T(8,128)S(1)}, u32[]{:S(2)}, u32[]{:S(2)}) collective-permute-start(f32[8,768]{1,0:T(8,128)S(1)} %slice_bitcast_fusion), channel_id=1, source_target_pairs={{0,1},{1,0},{2,3},{3,2},{4,5},{5,4},{6,7},{7,6},{8,9},{9,8},{10,11... | collective-permute-start | bytes 73736 | tf_op jit(solution)/shard_map/ppermute | solution.py:287

commit v5 on v4

--- a/solution.py
+++ b/solution.py
@@ -68,14 +68,13 @@
     return (row // RANKS_HERE) % LAYERS == layer
 
 
-def fetch_kernel(up_hbm, other_ref, down_hbm, pair_ref, down_ref, sems):
+def fetch_kernel(up_hbm, down_hbm, up_ref, down_ref, sems):
     copies = [
-        pltpu.make_async_copy(up_hbm, pair_ref.at[0], sems.at[0]),
+        pltpu.make_async_copy(up_hbm, up_ref, sems.at[0]),
         pltpu.make_async_copy(down_hbm, down_ref, sems.at[1]),
     ]
     for copy in copies:
         copy.start()
-    pair_ref[1] = other_ref[...]
     for copy in copies:
         copy.wait()
 
@@ -154,12 +153,11 @@
             bz_ref[...], jnp.concatenate(grads, axis=0), preferred_element_type=jnp.float32
         )
         ta_ref[:, :, here] = term_a.reshape(GROUPS, SLAB, BLOCK)
-        term_b = lax.dot_general(
-            jnp.concatenate(factors, axis=1),
-            jnp.concatenate(grads, axis=1),
-            (((1,), (1,)), ((), ())),
-            preferred_element_type=jnp.float32,
-        )
+        part_b = [
+            lax.dot_general(f, g, (((1,), (1,)), ((), ())), preferred_element_type=jnp.float32)
+            for f, g in zip(factors, grads)
+        ]
+        term_b = part_b[0] + part_b[1]
         term_b = term_b.reshape(total.shape)
         if start == 0:
             total[...] = term_b
@@ -201,18 +199,20 @@
     params = pltpu.CompilerParams(vmem_limit_bytes=VMEM_BYTES)
 
     up = jnp.swapaxes(up, 1, 2)
-    pair, own = pl.pallas_call(
+    other = lax.ppermute(up, "col", SWAP_CORE)
+    up, own = pl.pallas_call(
         fetch_kernel,
-        in_specs=[ANYWHERE, IN_VMEM, ANYWHERE],
+        in_specs=[ANYWHERE] * 2,
         out_specs=[IN_VMEM] * 2,
         out_shape=[
-            jax.ShapeDtypeStruct((2, *up.shape), up.dtype),
+            jax.ShapeDtypeStruct(up.shape, up.dtype),
             jax.ShapeDtypeStruct(down.shape, down.dtype),
         ],
         scratch_shapes=[pltpu.SemaphoreType.DMA((2,))],
         compiler_params=params,
         name="fetch",
-    )(in_hbm(up), lax.ppermute(up, "col", SWAP_CORE), in_hbm(down))
+    )(in_hbm(up), in_hbm(down))
+    pair = jnp.stack([up, other])
     two = lax.ppermute(pair, "col", z_apart(2))
     one, three = (lax.ppermute(pair, "col", z_apart(k)) for k in (1, 3))
     four = lax.ppermute(two[0], "col", z_apart(2))

time: 74.6 us -> 73.7 us (0.988)
  waiting for transfers between devices: 9.52 us -> 8.74 us
    ppermute x1, waiting for transfers between devices: 1.04 us -> 0.26 us  [on_device(): other = lax.ppermute(up, 'col', SWAP_CORE)]
  transfers between devices with their start and end apart: 19 -> 19, of which waited for: 7 -> 7; matrix products, arithmetic and copies ran while one was open for 0% -> 0% of each run, Pallas kernels for 1% -> 2%
where the time goes in v5:
time: 73.7 us; the launch traced here: 73.4 us
  starting transfers between devices  37.3 us (51%)
  blocking collectives  14.9 us (20%)
  Pallas kernels  11.5 us (16%)
  waiting for transfers between devices  8.74 us (12%)
  between operations  0.79 us (1%)
    all_to_all x1, blocking collectives, on_device(): sums_all = lax.all_to_all(sums, 'row', 0, 0)  14.9 us
    pallas_call x1, Pallas kernels, on_device(): pl.pallas_call(grads_kernel, in_specs=[IN_SMEM] + [IN_VMEM] * 10, out_spe...  6.3 us
    ppermute x3, starting transfers between devices, on_device(): lax.ppermute(down, ('row', 'col'), row_shift(k, 0))  4.38 us
    ppermute x1, starting transfers between devices, on_device(): two = lax.ppermute(pair, 'col', z_apart(2))  4.36 us
    ppermute x3, starting transfers between devices, on_device(): lax.ppermute(near, ('row', 'col'), row_shift(k, 1))  3.98 us
    all_to_all x1, starting transfers between devices, on_device(): parts_a = lax.all_to_all(term_a, 'row', 0, 0)  3.63 us
    ppermute x1, starting transfers between devices, on_device(): theirs = lax.ppermute(mine, 'col', SWAP_CORE)  3.39 us
    ppermute x1, starting transfers between devices, on_device(): other = lax.ppermute(up, 'col', SWAP_CORE)  3.33 us
  transfers between devices with their start and end apart: 19, of which 7 were waited for; matrix products, arithmetic and copies ran while one was open for 0% of the time, Pallas kernels for 2%

profile of v5, /device:TPU:1, one launch (start us, length us, event | category | flops | bytes accessed | tf_op | source)
XLA Modules:
  0.0 73.4 jit_solution(1529242453782997854)
XLA Ops:
  0.6 3.3 %collective-permute-start = (bf16[2,4,768]{2,1,0:T(4,128)(2,1)}, bf16[2,4,768]{2,1,0:T(4,128)(2,1)S(1)}, u32[]{:S(2)}, u32[]{:S(2)}) collective-permute-start(bf16[2,4,768]{2,1,0:T(4,128)(2,1)} %bitcast.16), channel_id=1, source_target_pairs={{0,1},{1,0},{2,3},{3,2},{4,5},{5,4},{6,7},{7,6},{8,9},{9,8},{10,11... | collective-permute-start | bytes 36872 | tf_op jit(solution)/shard_map/ppermute | solution.py:202
  4.0 0.8 %fetch.1 = (bf16[2,4,768]{2,1,0:T(4,128)(2,1)S(1)}, bf16[2,4,1792]{2,1,0:T(4,128)(2,1)S(1)}) custom-call(bf16[2,4,768]{2,1,0:T(4,128)(2,1)} %bitcast.17, bf16[2,4,1792]{2,1,0:T(4,128)(2,1)} %down_hbm.1), custom_call_target="tpu_custom_call" | custom-call | tf_op jit(solution)/shard_map/fetch/pallas_call | solution.py:203
  4.7 0.3 collective-permute-done
  5.0 4.4 %collective-permute-start.2 = (bf16[2,2,4,768]{3,2,1,0:T(4,128)(2,1)S(1)}, bf16[2,2,4,768]{3,2,1,0:T(4,128)(2,1)S(1)}, u32[]{:S(2)}, u32[]{:S(2)}) collective-permute-start(bf16[2,2,4,768]{3,2,1,0:T(4,128)(2,1)S(1)} %pad_maximum_fusion.1.pair), channel_id=1, source_target_pairs={{0,4},{2,6},{4,8},{6,10},{8,12},{10,14},{12,0},{14,2},{1,13},{3,15... | collective-permute-start | bytes 73736 | tf_op jit(solution)/shard_map/ppermute | solution.py:216
  9.4 1.3 %collective-permute-start.6 = (bf16[2,4,1792]{2,1,0:T(4,128)(2,1)}, bf16[2,4,1792]{2,1,0:T(4,128)(2,1)S(1)}, u32[]{:S(2)}, u32[]{:S(2)}) collective-permute-start(bf16[2,4,1792]{2,1,0:T(4,128)(2,1)} %down_hbm.1), channel_id=1, source_target_pairs={{0,16},{1,65},{2,18},{3,67},{4,20},{5,69},{6,22},{7,71},{8,24},{9,... | collective-permute-start | bytes 86024 | tf_op jit(solution)/shard_map/ppermute | solution.py:222
  10.7 1.4 %collective-permute-start.8 = (bf16[2,4,1792]{2,1,0:T(4,128)(2,1)}, bf16[2,4,1792]{2,1,0:T(4,128)(2,1)S(1)}, u32[]{:S(2)}, u32[]{:S(2)}) collective-permute-start(bf16[2,4,1792]{2,1,0:T(4,128)(2,1)} %down_hbm.1), channel_id=1, source_target_pairs={{0,48},{1,193},{2,50},{3,195},{4,52},{5,197},{6,54},{7,199},{8,56}... | collective-permute-start | bytes 86024 | tf_op jit(solution)/shard_map/ppermute | solution.py:222
  12.1 1.6 %collective-permute-start.7 = (bf16[2,4,1792]{2,1,0:T(4,128)(2,1)}, bf16[2,4,1792]{2,1,0:T(4,128)(2,1)S(1)}, u32[]{:S(2)}, u32[]{:S(2)}) collective-permute-start(bf16[2,4,1792]{2,1,0:T(4,128)(2,1)} %down_hbm.1), channel_id=1, source_target_pairs={{0,32},{1,129},{2,34},{3,131},{4,36},{5,133},{6,38},{7,135},{8,40}... | collective-permute-start | bytes 86024 | tf_op jit(solution)/shard_map/ppermute | solution.py:222
  13.8 0.7 collective-permute-start.3
  14.5 0.0 collective-permute-done.2
  14.5 0.5 collective-permute-start.1
  15.0 0.0 collective-permute-done.6.d1
  15.1 0.1 collective-permute-start.4
  15.1 0.0 collective-permute-done.8.d3
  15.2 1.4 %collective-permute-done.7.d2 = bf16[2,4,1792]{2,1,0:T(4,128)(2,1)S(1)} collective-permute-done((bf16[2,4,1792]{2,1,0:T(4,128)(2,1)}, bf16[2,4,1792]{2,1,0:T(4,128)(2,1)S(1)}, u32[]{:S(2)}, u32[]{:S(2)}) %collective-permute-start.7) | collective-permute-done | bytes 28704 | tf_op jit(solution)/shard_map/ppermute | solution.py:222
  16.6 0.0 copy-start
  16.6 0.0 copy-start.1
  16.6 2.9 %collective-permute-start.11 = (bf16[32,1792]{1,0:T(8,128)(2,1)S(1)}, bf16[32,1792]{1,0:T(8,128)(2,1)S(1)}, u32[]{:S(2)}, u32[]{:S(2)}) collective-permute-start(bf16[32,1792]{1,0:T(8,128)(2,1)S(1)} %stack.25.a0), channel_id=1, source_target_pairs={{0,192},{1,49},{2,194},{3,51},{4,196},{5,53},{6,198},{7,55},{8,200... | collective-permute-start | bytes 344072 | tf_op jit(solution)/shard_map/ppermute | solution.py:232
  19.5 0.4 collective-permute-start.10
  19.8 0.0 collective-permute-done.3
  19.8 0.8 %collective-permute-start.9 = (bf16[32,1792]{1,0:T(8,128)(2,1)S(1)}, bf16[32,1792]{1,0:T(8,128)(2,1)S(1)}, u32[]{:S(2)}, u32[]{:S(2)}) collective-permute-start(bf16[32,1792]{1,0:T(8,128)(2,1)S(1)} %stack.25.a0), channel_id=1, source_target_pairs={{0,64},{1,17},{2,66},{3,19},{4,68},{5,21},{6,70},{7,23},{8,72},{9,... | collective-permute-start | bytes 344072 | tf_op jit(solution)/shard_map/ppermute | solution.py:232
  20.6 0.0 collective-permute-done.1
  20.6 0.0 collective-permute-done.4
  20.6 0.1 pad_maximum_fusion.mine
  20.7 3.4 %collective-permute-start.5 = (bf16[7,2,4,768]{3,2,1,0:T(4,128)(2,1)S(1)}, bf16[7,2,4,768]{3,2,1,0:T(4,128)(2,1)S(1)}, u32[]{:S(2)}, u32[]{:S(2)}) collective-permute-start(bf16[7,2,4,768]{3,2,1,0:T(4,128)(2,1)S(1)} %pad_maximum_fusion.mine), channel_id=1, source_target_pairs={{0,1},{1,0},{2,3},{3,2},{4,5},{5,4},{6,7},{7,6},{8,9},{9,8},{10,11... | collective-permute-start | bytes 258056 | tf_op jit(solution)/shard_map/ppermute | solution.py:220
  24.1 0.1 pad_add_fusion.me_ref
  24.1 0.9 %collective-permute-done.5.theirs = bf16[7,2,4,768]{3,2,1,0:T(4,128)(2,1)S(1)} collective-permute-done((bf16[7,2,4,768]{3,2,1,0:T(4,128)(2,1)S(1)}, bf16[7,2,4,768]{3,2,1,0:T(4,128)(2,1)S(1)}, u32[]{:S(2)}, u32[]{:S(2)}) %collective-permute-start.5) | collective-permute-done | bytes 86048 | tf_op jit(solution)/shard_map/ppermute | solution.py:220
  25.0 0.9 %prepare.1 = (bf16[128,1536]{1,0:T(8,128)(2,1)S(1)}, bf16[2,768,128]{2,1,0:T(8,128)(2,1)S(1)}) custom-call(s32[2]{0:T(128)S(1)} %pad_add_fusion.me_ref, bf16[2,2,4,768]{3,2,1,0:T(4,128)(2,1)S(1)} %pad_maximum_fusion.1.pair, bf16[7,2,4,768]{3,2,1,0:T(4,128)(2,1)S(1)} %pad_maximum_fusion.mine, bf16[7,2,4,768]{3,2,1,0:T(4,128)(2,1)S(1)} %collective-permute-done.5.theirs), custom_call_target="tpu_custom_call" | custom-call | tf_op jit(solution)/shard_map/prepare/pallas_call | solution.py:234
  25.8 0.0 collective-permute-done.11.a3
  25.9 0.0 collective-permute-done.10.a2
  25.9 0.0 collective-permute-done.9.a1
  25.9 0.0 copy-done
  25.9 0.0 copy-done.1
  25.9 0.0 copy-start.2
  25.9 2.8 %column_sums.1 = f32[16,4,1792]{2,1,0:T(4,128)S(1)} custom-call(bf16[2,768,1792]{2,1,0:T(8,128)(2,1)S(1)} %copy-done, bf16[2,768,1792]{2,1,0:T(8,128)(2,1)S(1)} %copy-done.1, bf16[2,768,128]{2,1,0:T(8,128)(2,1)S(1)} %get-tuple-element.32.bt_ref, bf16[32,1792]{1,0:T(8,128)(2,1)S(1)} %stack.25.a0, bf16[32,1792]{1,0:T(8,128)(2,1)S(1)} %collective-permute-done.9.a1, ...), custom_call_target="tpu_custom_call" | custom-call | tf_op jit(solution)/shard_map/column_sums/pallas_call | solution.py:247
  28.8 14.9 %all_to_all.10.s_ref = f32[16,4,1792]{2,1,0:T(4,128)S(1)} all-to-all(f32[16,4,1792]{2,1,0:T(4,128)S(1)} %column_sums.1), channel_id=1, replica_groups=mesh['row'=16,'col'=16] {'row'}, dimensions={0} | all-to-all | bytes 917504 | tf_op jit(solution)/shard_map/all_to_all | solution.py:256
  43.6 0.0 copy-done.2
  43.6 6.3 %gradients.1 = (f32[16,8,1792]{2,1,0:T(8,128)}, f32[8,8,768]{2,1,0:T(8,128)S(1)}, f32[8,8,768]{2,1,0:T(8,128)S(1)}, f32[2,1792]{1,0:T(2,128)}) custom-call(s32[2]{0:T(128)S(1)} %pad_add_fusion.me_ref, bf16[2,768,1792]{2,1,0:T(8,128)(2,1)S(1)} %copy-done, bf16[2,768,1792]{2,1,0:T(8,128)(2,1)S(1)} %copy-done.1, ...), custom_call_target="tpu_custom_call" | custom-call | tf_op jit(solution)/shard_map/gradients/pallas_call | solution.py:258
  49.9 2.1 %collective-permute-start.12 = (f32[8,8,768]{2,1,0:T(8,128)S(1)}, f32[8,8,768]{2,1,0:T(8,128)S(1)}, u32[]{:S(2)}, u32[]{:S(2)}) collective-permute-start(f32[8,8,768]{2,1,0:T(8,128)S(1)} %get-tuple-element.36), channel_id=1, source_target_pairs={{0,1},{1,0},{2,3},{3,2},{4,5},{5,4},{6,7},{7,6},{8,9},{9,8},{10,11... | collective-permute-start | bytes 589832 | tf_op jit(solution)/shard_map/ppermute | solution.py:281
  52.1 3.6 %all-to-all-start.1 = ((f32[16,8,1792]{2,1,0:T(8,128)}), f32[16,8,1792]{2,1,0:T(8,128)S(1)}, u32[]{:S(2)}, u32[]{:S(2)}) async-start(f32[16,8,1792]{2,1,0:T(8,128)} %get-tuple-element.34), calls=%async_computation.1 | async-start | bytes 1835008 | tf_op jit(solution)/shard_map/all_to_all | solution.py:282
  55.7 0.0 collective-permute-done.12.got_ref
  55.7 2.7 %collective-permute-start.14 = (f32[8,768]{1,0:T(8,128)S(1)}, f32[8,768]{1,0:T(8,128)S(1)}, u32[]{:S(2)}, u32[]{:S(2)}) collective-permute-start(f32[8,768]{1,0:T(8,128)S(1)} %get-tuple-element.40), channel_id=1, source_target_pairs={{0,4},{2,6},{4,8},{6,10},{8,12},{10,14},{12,0},{14,2},{1,13},{3,15... | collective-permute-start | bytes 73736 | tf_op jit(solution)/shard_map/ppermute | solution.py:283
  58.4 0.7 collective-permute-start.13
  59.1 1.0 %collective-permute-start.16 = (f32[2,8,768]{2,1,0:T(8,128)S(1)}, f32[2,8,768]{2,1,0:T(8,128)S(1)}, u32[]{:S(2)}, u32[]{:S(2)}) collective-permute-start(f32[2,8,768]{2,1,0:T(8,128)S(1)} %get-tuple-element.41), channel_id=1, source_target_pairs={{0,6},{2,8},{4,10},{6,12},{8,14},{10,0},{12,2},{14,4},{1,11},{3,13... | collective-permute-start | bytes 147464 | tf_op jit(solution)/shard_map/ppermute | solution.py:284
  60.1 0.0 collective-permute-done.14
  60.1 3.1 %collective-permute-start.15 = (f32[2,8,768]{2,1,0:T(8,128)S(1)}, f32[2,8,768]{2,1,0:T(8,128)S(1)}, u32[]{:S(2)}, u32[]{:S(2)}) collective-permute-start(f32[2,8,768]{2,1,0:T(8,128)S(1)} %fusion), channel_id=1, source_target_pairs={{0,4},{2,6},{4,8},{6,10},{8,12},{10,14},{12,0},{14,2},{1,13},{3,15... | collective-permute-start | bytes 147464 | tf_op jit(solution)/shard_map/ppermute | solution.py:285
  63.2 0.0 collective-permute-done.13
  63.2 1.0 %collective-permute-done.16 = f32[2,8,768]{2,1,0:T(8,128)S(1)} collective-permute-done((f32[2,8,768]{2,1,0:T(8,128)S(1)}, f32[2,8,768]{2,1,0:T(8,128)S(1)}, u32[]{:S(2)}, u32[]{:S(2)}) %collective-permute-start.16) | collective-permute-done | bytes 49184 | tf_op jit(solution)/shard_map/ppermute | solution.py:284
  64.2 1.1 %collective-permute-done.15 = f32[2,8,768]{2,1,0:T(8,128)S(1)} collective-permute-done((f32[2,8,768]{2,1,0:T(8,128)S(1)}, f32[2,8,768]{2,1,0:T(8,128)S(1)}, u32[]{:S(2)}, u32[]{:S(2)}) %collective-permute-start.15) | collective-permute-done | bytes 49184 | tf_op jit(solution)/shard_map/ppermute | solution.py:285
  65.3 3.3 %collective-permute-start.17 = (f32[8,768]{1,0:T(8,128)S(1)}, f32[8,768]{1,0:T(8,128)S(1)}, u32[]{:S(2)}, u32[]{:S(2)}) collective-permute-start(f32[8,768]{1,0:T(8,128)S(1)} %slice_bitcast_fusion), channel_id=1, source_target_pairs={{0,1},{1,0},{2,3},{3,2},{4,5},{5,4},{6,7},{7,6},{8,9},{9,8},{10,11... | collective-permute-start | bytes 73736 | tf_op jit(solution)/shard_map/ppermute | solution.py:287
  68.6 0.8 %collective-permute-done.17.other_ref = f32[8,768]{1,0:T(8,128)S(1)} collective-permute-done((f32[8,768]{1,0:T(8,128)S(1)}, f32[8,768]{1,0:T(8,128)S(1)}, u32[]{:S(2)}, u32[]{:S(2)}) %collective-permute-start.17) | collective-permute-done | bytes 24608 | tf_op jit(solution)/shard_map/ppermute | solution.py:287
  69.5 3.2 %all-to-all-done.1.parts_ref = f32[16,8,1792]{2,1,0:T(8,128)S(1)} async-done(((f32[16,8,1792]{2,1,0:T(8,128)}), f32[16,8,1792]{2,1,0:T(8,128)S(1)}, u32[]{:S(2)}, u32[]{:S(2)}) %all-to-all-start.1) | async-done | bytes 917536 | tf_op jit(solution)/shard_map/all_to_all | solution.py:282
  72.7 0.7 finish.1
  (7 shorter events, 0.1 us)
Async XLA Ops:
  0.6 4.4 %collective-permute-start = (bf16[2,4,768]{2,1,0:T(4,128)(2,1)}, bf16[2,4,768]{2,1,0:T(4,128)(2,1)S(1)}, u32[]{:S(2)}, u32[]{:S(2)}) collective-permute-start(bf16[2,4,768]{2,1,0:T(4,128)(2,1)} %bitcast.16), channel_id=1, source_target_pairs={{0,1},{1,0},{2,3},{3,2},{4,5},{5,4},{6,7},{7,6},{8,9},{9,8},{10,11... | collective-permute-start | bytes 36872 | tf_op jit(solution)/shard_map/ppermute | solution.py:202
  5.0 9.5 %collective-permute-start.2 = (bf16[2,2,4,768]{3,2,1,0:T(4,128)(2,1)S(1)}, bf16[2,2,4,768]{3,2,1,0:T(4,128)(2,1)S(1)}, u32[]{:S(2)}, u32[]{:S(2)}) collective-permute-start(bf16[2,2,4,768]{3,2,1,0:T(4,128)(2,1)S(1)} %pad_maximum_fusion.1.pair), channel_id=1, source_target_pairs={{0,4},{2,6},{4,8},{6,10},{8,12},{10,14},{12,0},{14,2},{1,13},{3,15... | collective-permute-start | bytes 73736 | tf_op jit(solution)/shard_map/ppermute | solution.py:216
  9.4 5.7 %collective-permute-start.6 = (bf16[2,4,1792]{2,1,0:T(4,128)(2,1)}, bf16[2,4,1792]{2,1,0:T(4,128)(2,1)S(1)}, u32[]{:S(2)}, u32[]{:S(2)}) collective-permute-start(bf16[2,4,1792]{2,1,0:T(4,128)(2,1)} %down_hbm.1), channel_id=1, source_target_pairs={{0,16},{1,65},{2,18},{3,67},{4,20},{5,69},{6,22},{7,71},{8,24},{9,... | collective-permute-start | bytes 86024 | tf_op jit(solution)/shard_map/ppermute | solution.py:222
  10.7 4.5 %collective-permute-start.8 = (bf16[2,4,1792]{2,1,0:T(4,128)(2,1)}, bf16[2,4,1792]{2,1,0:T(4,128)(2,1)S(1)}, u32[]{:S(2)}, u32[]{:S(2)}) collective-permute-start(bf16[2,4,1792]{2,1,0:T(4,128)(2,1)} %down_hbm.1), channel_id=1, source_target_pairs={{0,48},{1,193},{2,50},{3,195},{4,52},{5,197},{6,54},{7,199},{8,56}... | collective-permute-start | bytes 86024 | tf_op jit(solution)/shard_map/ppermute | solution.py:222
  12.1 4.4 %collective-permute-start.7 = (bf16[2,4,1792]{2,1,0:T(4,128)(2,1)}, bf16[2,4,1792]{2,1,0:T(4,128)(2,1)S(1)}, u32[]{:S(2)}, u32[]{:S(2)}) collective-permute-start(bf16[2,4,1792]{2,1,0:T(4,128)(2,1)} %down_hbm.1), channel_id=1, source_target_pairs={{0,32},{1,129},{2,34},{3,131},{4,36},{5,133},{6,38},{7,135},{8,40}... | collective-permute-start | bytes 86024 | tf_op jit(solution)/shard_map/ppermute | solution.py:222
  13.8 6.0 %collective-permute-start.3 = (bf16[2,2,4,768]{3,2,1,0:T(4,128)(2,1)S(1)}, bf16[2,2,4,768]{3,2,1,0:T(4,128)(2,1)S(1)}, u32[]{:S(2)}, u32[]{:S(2)}) collective-permute-start(bf16[2,2,4,768]{3,2,1,0:T(4,128)(2,1)S(1)} %pad_maximum_fusion.1.pair), channel_id=1, source_target_pairs={{0,6},{2,8},{4,10},{6,12},{8,14},{10,0},{12,2},{14,4},{1,11},{3,13... | collective-permute-start | bytes 73736 | tf_op jit(solution)/shard_map/ppermute | solution.py:217
  14.5 6.1 %collective-permute-start.1 = (bf16[2,2,4,768]{3,2,1,0:T(4,128)(2,1)S(1)}, bf16[2,2,4,768]{3,2,1,0:T(4,128)(2,1)S(1)}, u32[]{:S(2)}, u32[]{:S(2)}) collective-permute-start(bf16[2,2,4,768]{3,2,1,0:T(4,128)(2,1)S(1)} %pad_maximum_fusion.1.pair), channel_id=1, source_target_pairs={{0,2},{2,4},{4,6},{6,8},{8,10},{10,12},{12,14},{14,0},{1,15},{3,1}... | collective-permute-start | bytes 73736 | tf_op jit(solution)/shard_map/ppermute | solution.py:217
  15.1 5.5 %collective-permute-start.4 = (bf16[2,4,768]{2,1,0:T(4,128)(2,1)S(1)}, bf16[2,4,768]{2,1,0:T(4,128)(2,1)S(1)}, u32[]{:S(2)}, u32[]{:S(2)}) collective-permute-start(bf16[2,4,768]{2,1,0:T(4,128)(2,1)S(1)} %slice_bitcast_fusion.1), channel_id=1, source_target_pairs={{0,4},{2,6},{4,8},{6,10},{8,12},{10,14},{12,0},{14,2},{1,13},{3,15... | collective-permute-start | bytes 36872 | tf_op jit(solution)/shard_map/ppermute | solution.py:218
  16.6 9.3 %copy-start = (bf16[2,768,1792]{2,1,0:T(8,128)(2,1)S(1)}, bf16[2,768,1792]{2,1,0:T(8,128)(2,1)}, u32[]{:S(2)}) copy-start(bf16[2,768,1792]{2,1,0:T(8,128)(2,1)} %w_ref.3) | copy-start | bytes 16515076
  16.6 9.3 %copy-start.1 = (bf16[2,768,1792]{2,1,0:T(8,128)(2,1)S(1)}, bf16[2,768,1792]{2,1,0:T(8,128)(2,1)}, u32[]{:S(2)}) copy-start(bf16[2,768,1792]{2,1,0:T(8,128)(2,1)} %g_ref.3) | copy-start | bytes 16515076
  16.6 9.2 %collective-permute-start.11 = (bf16[32,1792]{1,0:T(8,128)(2,1)S(1)}, bf16[32,1792]{1,0:T(8,128)(2,1)S(1)}, u32[]{:S(2)}, u32[]{:S(2)}) collective-permute-start(bf16[32,1792]{1,0:T(8,128)(2,1)S(1)} %stack.25.a0), channel_id=1, source_target_pairs={{0,192},{1,49},{2,194},{3,51},{4,196},{5,53},{6,198},{7,55},{8,200... | collective-permute-start | bytes 344072 | tf_op jit(solution)/shard_map/ppermute | solution.py:232
  19.5 6.4 %collective-permute-start.10 = (bf16[32,1792]{1,0:T(8,128)(2,1)S(1)}, bf16[32,1792]{1,0:T(8,128)(2,1)S(1)}, u32[]{:S(2)}, u32[]{:S(2)}) collective-permute-start(bf16[32,1792]{1,0:T(8,128)(2,1)S(1)} %stack.25.a0), channel_id=1, source_target_pairs={{0,128},{1,33},{2,130},{3,35},{4,132},{5,37},{6,134},{7,39},{8,136... | collective-permute-start | bytes 344072 | tf_op jit(solution)/shard_map/ppermute | solution.py:232
  19.8 6.0 %collective-permute-start.9 = (bf16[32,1792]{1,0:T(8,128)(2,1)S(1)}, bf16[32,1792]{1,0:T(8,128)(2,1)S(1)}, u32[]{:S(2)}, u32[]{:S(2)}) collective-permute-start(bf16[32,1792]{1,0:T(8,128)(2,1)S(1)} %stack.25.a0), channel_id=1, source_target_pairs={{0,64},{1,17},{2,66},{3,19},{4,68},{5,21},{6,70},{7,23},{8,72},{9,... | collective-permute-start | bytes 344072 | tf_op jit(solution)/shard_map/ppermute | solution.py:232
  20.7 4.3 %collective-permute-start.5 = (bf16[7,2,4,768]{3,2,1,0:T(4,128)(2,1)S(1)}, bf16[7,2,4,768]{3,2,1,0:T(4,128)(2,1)S(1)}, u32[]{:S(2)}, u32[]{:S(2)}) collective-permute-start(bf16[7,2,4,768]{3,2,1,0:T(4,128)(2,1)S(1)} %pad_maximum_fusion.mine), channel_id=1, source_target_pairs={{0,1},{1,0},{2,3},{3,2},{4,5},{5,4},{6,7},{7,6},{8,9},{9,8},{10,11... | collective-permute-start | bytes 258056 | tf_op jit(solution)/shard_map/ppermute | solution.py:220
  25.9 17.7 %copy-start.2 = (f32[2,1792]{1,0:T(2,128)S(1)}, f32[2,1792]{1,0:T(2,128)}, u32[]{:S(2)}) copy-start(f32[2,1792]{1,0:T(2,128)} %mag_ref.1) | copy-start | bytes 43012
  49.9 5.8 %collective-permute-start.12 = (f32[8,8,768]{2,1,0:T(8,128)S(1)}, f32[8,8,768]{2,1,0:T(8,128)S(1)}, u32[]{:S(2)}, u32[]{:S(2)}) collective-permute-start(f32[8,8,768]{2,1,0:T(8,128)S(1)} %get-tuple-element.36), channel_id=1, source_target_pairs={{0,1},{1,0},{2,3},{3,2},{4,5},{5,4},{6,7},{7,6},{8,9},{9,8},{10,11... | collective-permute-start | bytes 589832 | tf_op jit(solution)/shard_map/ppermute | solution.py:281
  52.1 20.7 %all-to-all-start.1 = ((f32[16,8,1792]{2,1,0:T(8,128)}), f32[16,8,1792]{2,1,0:T(8,128)S(1)}, u32[]{:S(2)}, u32[]{:S(2)}) async-start(f32[16,8,1792]{2,1,0:T(8,128)} %get-tuple-element.34), calls=%async_computation.1 | async-start | bytes 1835008 | tf_op jit(solution)/shard_map/all_to_all | solution.py:282
  55.7 4.4 %collective-permute-start.14 = (f32[8,768]{1,0:T(8,128)S(1)}, f32[8,768]{1,0:T(8,128)S(1)}, u32[]{:S(2)}, u32[]{:S(2)}) collective-permute-start(f32[8,768]{1,0:T(8,128)S(1)} %get-tuple-element.40), channel_id=1, source_target_pairs={{0,4},{2,6},{4,8},{6,10},{8,12},{10,14},{12,0},{14,2},{1,13},{3,15... | collective-permute-start | bytes 73736 | tf_op jit(solution)/shard_map/ppermute | solution.py:283
  58.4 4.8 %collective-permute-start.13 = (f32[2,8,768]{2,1,0:T(8,128)S(1)}, f32[2,8,768]{2,1,0:T(8,128)S(1)}, u32[]{:S(2)}, u32[]{:S(2)}) collective-permute-start(f32[2,8,768]{2,1,0:T(8,128)S(1)} %get-tuple-element.38), channel_id=1, source_target_pairs={{0,2},{2,4},{4,6},{6,8},{8,10},{10,12},{12,14},{14,0},{1,15},{3,1}... | collective-permute-start | bytes 147464 | tf_op jit(solution)/shard_map/ppermute | solution.py:284
  59.1 5.0 %collective-permute-start.16 = (f32[2,8,768]{2,1,0:T(8,128)S(1)}, f32[2,8,768]{2,1,0:T(8,128)S(1)}, u32[]{:S(2)}, u32[]{:S(2)}) collective-permute-start(f32[2,8,768]{2,1,0:T(8,128)S(1)} %get-tuple-element.41), channel_id=1, source_target_pairs={{0,6},{2,8},{4,10},{6,12},{8,14},{10,0},{12,2},{14,4},{1,11},{3,13... | collective-permute-start | bytes 147464 | tf_op jit(solution)/shard_map/ppermute | solution.py:284
  60.1 5.2 %collective-permute-start.15 = (f32[2,8,768]{2,1,0:T(8,128)S(1)}, f32[2,8,768]{2,1,0:T(8,128)S(1)}, u32[]{:S(2)}, u32[]{:S(2)}) collective-permute-start(f32[2,8,768]{2,1,0:T(8,128)S(1)} %fusion), channel_id=1, source_target_pairs={{0,4},{2,6},{4,8},{6,10},{8,12},{10,14},{12,0},{14,2},{1,13},{3,15... | collective-permute-start | bytes 147464 | tf_op jit(solution)/shard_map/ppermute | solution.py:285
  65.3 4.1 %collective-permute-start.17 = (f32[8,768]{1,0:T(8,128)S(1)}, f32[8,768]{1,0:T(8,128)S(1)}, u32[]{:S(2)}, u32[]{:S(2)}) collective-permute-start(f32[8,768]{1,0:T(8,128)S(1)} %slice_bitcast_fusion), channel_id=1, source_target_pairs={{0,1},{1,0},{2,3},{3,2},{4,5},{5,4},{6,7},{7,6},{8,9},{9,8},{10,11... | collective-permute-start | bytes 73736 | tf_op jit(solution)/shard_map/ppermute | solution.py:287

commit v6 on v5

--- a/solution.py
+++ b/solution.py
@@ -15,7 +15,7 @@
 RING = 8
 REACH = RING // 2
 BLOCK = 256
-VMEM_BYTES = 20 * 1024 * 1024
+VMEM_BYTES = 28 * 1024 * 1024
 IN_VMEM = pl.BlockSpec(memory_space=pltpu.VMEM)
 ANYWHERE = pl.BlockSpec(memory_space=pl.ANY)
 IN_SMEM = pl.BlockSpec(memory_space=pltpu.SMEM)
@@ -37,7 +37,7 @@
     for row in range(GROUPS):
         y, x = row // SIDE, row % SIDE
         for col in range(GROUPS):
-            along_y = (col % 2 + second) % 2
+            along_y = (col + 1 + second) % 2
             to = (y + k) % SIDE * SIDE + x if along_y else y * SIDE + (x + k) % SIDE
             pairs.append((row * GROUPS + col, to * GROUPS + col))
     return pairs
@@ -50,14 +50,14 @@
 
 
 def row_group(row, col, second, first):
-    core = col % 2
+    core = 1 - col % 2
     ky = second * (1 - core) + first * core
     kx = first * (1 - core) + second * core
     return (row // SIDE + SIDE - ky) % SIDE * SIDE + (row % SIDE + SIDE - kx) % SIDE
 
 
 def row_place(row, col, group):
-    core = col % 2
+    core = 1 - col % 2
     ky = (row // SIDE + SIDE - group // SIDE) % SIDE
     kx = (row % SIDE + SIDE - group % SIDE) % SIDE
     return (ky * (1 - core) + kx * core) * SIDE + kx * (1 - core) + ky * core
@@ -107,7 +107,7 @@
         bt_ref[layer] = jnp.where(mask, there, 0.0).T.astype(jnp.bfloat16)
 
 
-def sums_kernel(w_ref, g_ref, bt_ref, a0, a1, a2, a3, s_ref):
+def sums_kernel(w_ref, g_ref, bt_ref, a0, a1, a2, a3, s_ref, kept_ref, rest_ref):
     for start in range(0, w_ref.shape[2], BLOCK):
         here = pl.ds(start, BLOCK)
         a = jnp.concatenate([x[:, here] for x in (a0, a1, a2, a3)], axis=0)
@@ -116,6 +116,10 @@
             merged = w_ref[layer, :, here].astype(jnp.float32) + jnp.dot(
                 bt_ref[layer], a, preferred_element_type=jnp.float32
             )
+            if layer == 0:
+                kept_ref[:, here] = merged
+            else:
+                rest_ref[:, here] = w_ref[layer, :, here]
             cot = g_ref[layer, :, here].astype(jnp.float32)
             rows.append(jnp.sum(merged * merged, axis=0, keepdims=True))
             rows.append(jnp.sum(cot * merged, axis=0, keepdims=True))
@@ -124,10 +128,10 @@
 
 
 def grads_kernel(
-    me_ref, w_ref, g_ref, bz_ref, bt_ref, a0, a1, a2, a3, s_ref, mag_ref,
+    me_ref, kept_ref, rest_ref, g_ref, bz_ref, bt_ref, a0, a1, a2, a3, s_ref, mag_ref,
     ta_ref, keep_ref, send_ref, gmag_ref, total,
 ):
-    for start in range(0, w_ref.shape[2], BLOCK):
+    for start in range(0, g_ref.shape[2], BLOCK):
         here = pl.ds(start, BLOCK)
         a = jnp.concatenate([x[:, here] for x in (a0, a1, a2, a3)], axis=0)
         a_wide = a.astype(jnp.float32)
@@ -141,9 +145,12 @@
             scale = mag_ref[layer : layer + 1, here] / norm
             shrink = scale * inner / (norm * norm)
             gmag_ref[layer : layer + 1, here] = inner / norm
-            merged = w_ref[layer, :, here].astype(jnp.float32) + jnp.dot(
-                bt_ref[layer], a, preferred_element_type=jnp.float32
-            )
+            if layer == 0:
+                merged = kept_ref[:, here]
+            else:
+                merged = rest_ref[:, here].astype(jnp.float32) + jnp.dot(
+                    bt_ref[layer], a, preferred_element_type=jnp.float32
+                )
             cot = g_ref[layer, :, here].astype(jnp.float32)
             grad = (scale * cot - shrink * merged).astype(jnp.bfloat16)
             az = jnp.where(layer_mask(layer, a_wide.shape), a_wide, 0.0).astype(jnp.bfloat16)
@@ -244,11 +251,15 @@
         name="prepare",
     )(me, pair, mine, theirs)
 
-    sums = pl.pallas_call(
+    sums, kept, rest = pl.pallas_call(
         sums_kernel,
         in_specs=[IN_VMEM] * 7,
-        out_specs=IN_VMEM,
-        out_shape=jax.ShapeDtypeStruct((GROUPS, 2 * layers, width), jnp.float32),
+        out_specs=[IN_VMEM] * 3,
+        out_shape=[
+            jax.ShapeDtypeStruct((GROUPS, 2 * layers, width), jnp.float32),
+            jax.ShapeDtypeStruct((height, width), jnp.float32),
+            jax.ShapeDtypeStruct((height, width), weight.dtype),
+        ],
         compiler_params=params,
         name="column_sums",
     )(weight, cotangent, up_columns, *downs)
@@ -257,7 +268,7 @@
 
     term_a, keep_b, send_b, mags = pl.pallas_call(
         grads_kernel,
-        in_specs=[IN_SMEM] + [IN_VMEM] * 10,
+        in_specs=[IN_SMEM] + [IN_VMEM] * 11,
         out_specs=[IN_VMEM] * 4,
         out_shape=[
             jax.ShapeDtypeStruct((GROUPS, SLAB, width), jnp.float32),
@@ -267,7 +278,7 @@
         scratch_shapes=[pltpu.VMEM((GROUPS, SLAB, height), jnp.float32)],
         compiler_params=params,
         name="gradients",
-    )(me, weight, cotangent, up_rows, up_columns, *downs, sums_all, magnitude)
+    )(me, kept, rest, cotangent, up_rows, up_columns, *downs, sums_all, magnitude)
 
     pair_of = jax.ShapeDtypeStruct((2, SLAB, height), jnp.float32)
     one_of = jax.ShapeDtypeStruct((SLAB, height), jnp.float32)

time: 73.7 us -> 72.9 us (0.989)
  no operation moved by 1% of the time
where the time goes in v6:
time: 72.9 us; the launch traced here: 72.6 us
  starting transfers between devices  37.2 us (51%)
  blocking collectives  14.6 us (20%)
  Pallas kernels  10.9 us (15%)
  waiting for transfers between devices  8.86 us (12%)
  between operations  0.79 us (1%)
    all_to_all x1, blocking collectives, on_device(): sums_all = lax.all_to_all(sums, 'row', 0, 0)  14.6 us
    pallas_call x1, Pallas kernels, on_device(): pl.pallas_call(grads_kernel, in_specs=[IN_SMEM] + [IN_VMEM] * 11, out_spe...  5.77 us
    ppermute x1, starting transfers between devices, on_device(): two = lax.ppermute(pair, 'col', z_apart(2))  4.36 us
    ppermute x3, starting transfers between devices, on_device(): lax.ppermute(down, ('row', 'col'), row_shift(k, 0))  4.21 us
    ppermute x3, starting transfers between devices, on_device(): lax.ppermute(near, ('row', 'col'), row_shift(k, 1))  4.15 us
    all_to_all x1, starting transfers between devices, on_device(): parts_a = lax.all_to_all(term_a, 'row', 0, 0)  3.63 us
    ppermute x1, starting transfers between devices, on_device(): theirs = lax.ppermute(mine, 'col', SWAP_CORE)  3.45 us
    ppermute x1, starting transfers between devices, on_device(): other = lax.ppermute(got[1], 'col', SWAP_CORE)  3.35 us
  transfers between devices with their start and end apart: 19, of which 7 were waited for; matrix products, arithmetic and copies ran while one was open for 0% of the time, Pallas kernels for 2%

profile of v6, /device:TPU:1, one launch (start us, length us, event | category | flops | bytes accessed | tf_op | source)
XLA Modules:
  0.0 72.6 jit_solution(14479250055749957969)
XLA Ops:
  0.6 3.3 %collective-permute-start = (bf16[2,4,768]{2,1,0:T(4,128)(2,1)}, bf16[2,4,768]{2,1,0:T(4,128)(2,1)S(1)}, u32[]{:S(2)}, u32[]{:S(2)}) collective-permute-start(bf16[2,4,768]{2,1,0:T(4,128)(2,1)} %bitcast.16), channel_id=1, source_target_pairs={{0,1},{1,0},{2,3},{3,2},{4,5},{5,4},{6,7},{7,6},{8,9},{9,8},{10,11... | collective-permute-start | bytes 36872 | tf_op jit(solution)/shard_map/ppermute | solution.py:209
  4.0 0.8 %fetch.1 = (bf16[2,4,768]{2,1,0:T(4,128)(2,1)S(1)}, bf16[2,4,1792]{2,1,0:T(4,128)(2,1)S(1)}) custom-call(bf16[2,4,768]{2,1,0:T(4,128)(2,1)} %bitcast.17, bf16[2,4,1792]{2,1,0:T(4,128)(2,1)} %down_hbm.1), custom_call_target="tpu_custom_call" | custom-call | tf_op jit(solution)/shard_map/fetch/pallas_call | solution.py:210
  4.7 0.3 collective-permute-done
  5.0 4.4 %collective-permute-start.2 = (bf16[2,2,4,768]{3,2,1,0:T(4,128)(2,1)S(1)}, bf16[2,2,4,768]{3,2,1,0:T(4,128)(2,1)S(1)}, u32[]{:S(2)}, u32[]{:S(2)}) collective-permute-start(bf16[2,2,4,768]{3,2,1,0:T(4,128)(2,1)S(1)} %pad_maximum_fusion.1.pair), channel_id=1, source_target_pairs={{0,4},{2,6},{4,8},{6,10},{8,12},{10,14},{12,0},{14,2},{1,13},{3,15... | collective-permute-start | bytes 73736 | tf_op jit(solution)/shard_map/ppermute | solution.py:223
  9.4 1.2 %collective-permute-start.6 = (bf16[2,4,1792]{2,1,0:T(4,128)(2,1)}, bf16[2,4,1792]{2,1,0:T(4,128)(2,1)S(1)}, u32[]{:S(2)}, u32[]{:S(2)}) collective-permute-start(bf16[2,4,1792]{2,1,0:T(4,128)(2,1)} %down_hbm.1), channel_id=1, source_target_pairs={{0,64},{1,17},{2,66},{3,19},{4,68},{5,21},{6,70},{7,23},{8,72},{9,... | collective-permute-start | bytes 86024 | tf_op jit(solution)/shard_map/ppermute | solution.py:229
  10.6 1.5 %collective-permute-start.8 = (bf16[2,4,1792]{2,1,0:T(4,128)(2,1)}, bf16[2,4,1792]{2,1,0:T(4,128)(2,1)S(1)}, u32[]{:S(2)}, u32[]{:S(2)}) collective-permute-start(bf16[2,4,1792]{2,1,0:T(4,128)(2,1)} %down_hbm.1), channel_id=1, source_target_pairs={{0,192},{1,49},{2,194},{3,51},{4,196},{5,53},{6,198},{7,55},{8,200... | collective-permute-start | bytes 86024 | tf_op jit(solution)/shard_map/ppermute | solution.py:229
  12.1 1.5 %collective-permute-start.7 = (bf16[2,4,1792]{2,1,0:T(4,128)(2,1)}, bf16[2,4,1792]{2,1,0:T(4,128)(2,1)S(1)}, u32[]{:S(2)}, u32[]{:S(2)}) collective-permute-start(bf16[2,4,1792]{2,1,0:T(4,128)(2,1)} %down_hbm.1), channel_id=1, source_target_pairs={{0,128},{1,33},{2,130},{3,35},{4,132},{5,37},{6,134},{7,39},{8,136... | collective-permute-start | bytes 86024 | tf_op jit(solution)/shard_map/ppermute | solution.py:229
  13.6 0.7 collective-permute-start.3
  14.3 0.0 collective-permute-done.2
  14.3 0.5 collective-permute-start.1
  14.9 0.0 collective-permute-done.6.d1
  14.9 0.1 collective-permute-start.4
  15.0 0.0 collective-permute-done.8.d3
  15.0 1.5 %collective-permute-done.7.d2 = bf16[2,4,1792]{2,1,0:T(4,128)(2,1)S(1)} collective-permute-done((bf16[2,4,1792]{2,1,0:T(4,128)(2,1)}, bf16[2,4,1792]{2,1,0:T(4,128)(2,1)S(1)}, u32[]{:S(2)}, u32[]{:S(2)}) %collective-permute-start.7) | collective-permute-done | bytes 28704 | tf_op jit(solution)/shard_map/ppermute | solution.py:229
  16.5 0.0 copy-start
  16.5 0.0 copy-start.1
  16.5 3.0 %collective-permute-start.11 = (bf16[32,1792]{1,0:T(8,128)(2,1)S(1)}, bf16[32,1792]{1,0:T(8,128)(2,1)S(1)}, u32[]{:S(2)}, u32[]{:S(2)}) collective-permute-start(bf16[32,1792]{1,0:T(8,128)(2,1)S(1)} %stack.25.a0), channel_id=1, source_target_pairs={{0,48},{1,193},{2,50},{3,195},{4,52},{5,197},{6,54},{7,199},{8,56}... | collective-permute-start | bytes 344072 | tf_op jit(solution)/shard_map/ppermute | solution.py:239
  19.5 0.4 collective-permute-start.10
  19.9 0.0 collective-permute-done.3
  19.9 0.8 %collective-permute-start.9 = (bf16[32,1792]{1,0:T(8,128)(2,1)S(1)}, bf16[32,1792]{1,0:T(8,128)(2,1)S(1)}, u32[]{:S(2)}, u32[]{:S(2)}) collective-permute-start(bf16[32,1792]{1,0:T(8,128)(2,1)S(1)} %stack.25.a0), channel_id=1, source_target_pairs={{0,16},{1,65},{2,18},{3,67},{4,20},{5,69},{6,22},{7,71},{8,24},{9,... | collective-permute-start | bytes 344072 | tf_op jit(solution)/shard_map/ppermute | solution.py:239
  20.7 0.0 collective-permute-done.1
  20.7 0.0 collective-permute-done.4
  20.7 0.1 pad_maximum_fusion.mine
  20.8 3.4 %collective-permute-start.5 = (bf16[7,2,4,768]{3,2,1,0:T(4,128)(2,1)S(1)}, bf16[7,2,4,768]{3,2,1,0:T(4,128)(2,1)S(1)}, u32[]{:S(2)}, u32[]{:S(2)}) collective-permute-start(bf16[7,2,4,768]{3,2,1,0:T(4,128)(2,1)S(1)} %pad_maximum_fusion.mine), channel_id=1, source_target_pairs={{0,1},{1,0},{2,3},{3,2},{4,5},{5,4},{6,7},{7,6},{8,9},{9,8},{10,11... | collective-permute-start | bytes 258056 | tf_op jit(solution)/shard_map/ppermute | solution.py:227
  24.2 0.1 pad_add_fusion.me_ref
  24.3 0.9 %collective-permute-done.5.theirs = bf16[7,2,4,768]{3,2,1,0:T(4,128)(2,1)S(1)} collective-permute-done((bf16[7,2,4,768]{3,2,1,0:T(4,128)(2,1)S(1)}, bf16[7,2,4,768]{3,2,1,0:T(4,128)(2,1)S(1)}, u32[]{:S(2)}, u32[]{:S(2)}) %collective-permute-start.5) | collective-permute-done | bytes 86048 | tf_op jit(solution)/shard_map/ppermute | solution.py:227
  25.1 0.9 %prepare.1 = (bf16[128,1536]{1,0:T(8,128)(2,1)S(1)}, bf16[2,768,128]{2,1,0:T(8,128)(2,1)S(1)}) custom-call(s32[2]{0:T(128)S(1)} %pad_add_fusion.me_ref, bf16[2,2,4,768]{3,2,1,0:T(4,128)(2,1)S(1)} %pad_maximum_fusion.1.pair, bf16[7,2,4,768]{3,2,1,0:T(4,128)(2,1)S(1)} %pad_maximum_fusion.mine, bf16[7,2,4,768]{3,2,1,0:T(4,128)(2,1)S(1)} %collective-permute-done.5.theirs), custom_call_target="tpu_custom_call" | custom-call | tf_op jit(solution)/shard_map/prepare/pallas_call | solution.py:241
  26.0 0.0 collective-permute-done.11.a3
  26.0 0.0 collective-permute-done.10.a2
  26.0 0.0 collective-permute-done.9.a1
  26.0 0.0 copy-done
  26.1 0.0 copy-done.1
  26.1 0.0 copy-start.2
  26.1 2.8 %column_sums.1 = (f32[16,4,1792]{2,1,0:T(4,128)S(1)}, f32[768,1792]{1,0:T(8,128)S(1)}, bf16[768,1792]{1,0:T(8,128)(2,1)S(1)}) custom-call(bf16[2,768,1792]{2,1,0:T(8,128)(2,1)S(1)} %copy-done.1, bf16[2,768,1792]{2,1,0:T(8,128)(2,1)S(1)} %copy-done, bf16[2,768,128]{2,1,0:T(8,128)(2,1)S(1)} %get-tuple-element.34.bt_ref, bf16[32,1792]{1,0:T(8,128)(2,1)S(1)} %stack.25.a0, ...), custom_call_target="tpu_custom_call" | custom-call | tf_op jit(solution)/shard_map/column_sums/pallas_call | solution.py:254
  28.9 14.6 %all_to_all.10.s_ref = f32[16,4,1792]{2,1,0:T(4,128)S(1)} all-to-all(f32[16,4,1792]{2,1,0:T(4,128)S(1)} %get-tuple-element.39), channel_id=1, replica_groups=mesh['row'=16,'col'=16] {'row'}, dimensions={0} | all-to-all | bytes 917504 | tf_op jit(solution)/shard_map/all_to_all | solution.py:267
  43.5 0.0 copy-done.2
  43.5 5.8 %gradients.1 = (f32[16,8,1792]{2,1,0:T(8,128)}, f32[8,8,768]{2,1,0:T(8,128)S(1)}, f32[8,8,768]{2,1,0:T(8,128)S(1)}, f32[2,1792]{1,0:T(2,128)}) custom-call(s32[2]{0:T(128)S(1)} %pad_add_fusion.me_ref, f32[768,1792]{1,0:T(8,128)S(1)} %get-tuple-element.36.kept_ref, bf16[768,1792]{1,0:T(8,128)(2,1)S(1)} %get-tuple-element.37.rest_ref, ...), custom_call_target="tpu_custom_call" | custom-call | tf_op jit(solution)/shard_map/gradients/pallas_call | solution.py:269
  49.2 2.0 %collective-permute-start.12 = (f32[8,8,768]{2,1,0:T(8,128)S(1)}, f32[8,8,768]{2,1,0:T(8,128)S(1)}, u32[]{:S(2)}, u32[]{:S(2)}) collective-permute-start(f32[8,8,768]{2,1,0:T(8,128)S(1)} %get-tuple-element.42), channel_id=1, source_target_pairs={{0,1},{1,0},{2,3},{3,2},{4,5},{5,4},{6,7},{7,6},{8,9},{9,8},{10,11... | collective-permute-start | bytes 589832 | tf_op jit(solution)/shard_map/ppermute | solution.py:292
  51.3 3.6 %all-to-all-start.1 = ((f32[16,8,1792]{2,1,0:T(8,128)}), f32[16,8,1792]{2,1,0:T(8,128)S(1)}, u32[]{:S(2)}, u32[]{:S(2)}) async-start(f32[16,8,1792]{2,1,0:T(8,128)} %get-tuple-element.40), calls=%async_computation.1 | async-start | bytes 1835008 | tf_op jit(solution)/shard_map/all_to_all | solution.py:293
  54.9 0.0 collective-permute-done.12.got_ref
  55.0 2.6 %collective-permute-start.14 = (f32[8,768]{1,0:T(8,128)S(1)}, f32[8,768]{1,0:T(8,128)S(1)}, u32[]{:S(2)}, u32[]{:S(2)}) collective-permute-start(f32[8,768]{1,0:T(8,128)S(1)} %get-tuple-element.46), channel_id=1, source_target_pairs={{0,4},{2,6},{4,8},{6,10},{8,12},{10,14},{12,0},{14,2},{1,13},{3,15... | collective-permute-start | bytes 73736 | tf_op jit(solution)/shard_map/ppermute | solution.py:294
  57.6 0.7 collective-permute-start.13
  58.3 1.2 %collective-permute-start.16 = (f32[2,8,768]{2,1,0:T(8,128)S(1)}, f32[2,8,768]{2,1,0:T(8,128)S(1)}, u32[]{:S(2)}, u32[]{:S(2)}) collective-permute-start(f32[2,8,768]{2,1,0:T(8,128)S(1)} %get-tuple-element.47), channel_id=1, source_target_pairs={{0,6},{2,8},{4,10},{6,12},{8,14},{10,0},{12,2},{14,4},{1,11},{3,13... | collective-permute-start | bytes 147464 | tf_op jit(solution)/shard_map/ppermute | solution.py:295
  59.5 0.0 collective-permute-done.14
  59.5 2.9 %collective-permute-start.15 = (f32[2,8,768]{2,1,0:T(8,128)S(1)}, f32[2,8,768]{2,1,0:T(8,128)S(1)}, u32[]{:S(2)}, u32[]{:S(2)}) collective-permute-start(f32[2,8,768]{2,1,0:T(8,128)S(1)} %fusion), channel_id=1, source_target_pairs={{0,4},{2,6},{4,8},{6,10},{8,12},{10,14},{12,0},{14,2},{1,13},{3,15... | collective-permute-start | bytes 147464 | tf_op jit(solution)/shard_map/ppermute | solution.py:296
  62.4 0.0 collective-permute-done.13
  62.4 1.0 %collective-permute-done.16 = f32[2,8,768]{2,1,0:T(8,128)S(1)} collective-permute-done((f32[2,8,768]{2,1,0:T(8,128)S(1)}, f32[2,8,768]{2,1,0:T(8,128)S(1)}, u32[]{:S(2)}, u32[]{:S(2)}) %collective-permute-start.16) | collective-permute-done | bytes 49184 | tf_op jit(solution)/shard_map/ppermute | solution.py:295
  63.3 1.1 %collective-permute-done.15 = f32[2,8,768]{2,1,0:T(8,128)S(1)} collective-permute-done((f32[2,8,768]{2,1,0:T(8,128)S(1)}, f32[2,8,768]{2,1,0:T(8,128)S(1)}, u32[]{:S(2)}, u32[]{:S(2)}) %collective-permute-start.15) | collective-permute-done | bytes 49184 | tf_op jit(solution)/shard_map/ppermute | solution.py:296
  64.5 3.3 %collective-permute-start.17 = (f32[8,768]{1,0:T(8,128)S(1)}, f32[8,768]{1,0:T(8,128)S(1)}, u32[]{:S(2)}, u32[]{:S(2)}) collective-permute-start(f32[8,768]{1,0:T(8,128)S(1)} %slice_bitcast_fusion), channel_id=1, source_target_pairs={{0,1},{1,0},{2,3},{3,2},{4,5},{5,4},{6,7},{7,6},{8,9},{9,8},{10,11... | collective-permute-start | bytes 73736 | tf_op jit(solution)/shard_map/ppermute | solution.py:298
  67.8 0.8 %collective-permute-done.17.other_ref = f32[8,768]{1,0:T(8,128)S(1)} collective-permute-done((f32[8,768]{1,0:T(8,128)S(1)}, f32[8,768]{1,0:T(8,128)S(1)}, u32[]{:S(2)}, u32[]{:S(2)}) %collective-permute-start.17) | collective-permute-done | bytes 24608 | tf_op jit(solution)/shard_map/ppermute | solution.py:298
  68.7 3.3 %all-to-all-done.1.parts_ref = f32[16,8,1792]{2,1,0:T(8,128)S(1)} async-done(((f32[16,8,1792]{2,1,0:T(8,128)}), f32[16,8,1792]{2,1,0:T(8,128)S(1)}, u32[]{:S(2)}, u32[]{:S(2)}) %all-to-all-start.1) | async-done | bytes 917536 | tf_op jit(solution)/shard_map/all_to_all | solution.py:293
  71.9 0.7 finish.1
  (7 shorter events, 0.1 us)
Async XLA Ops:
  0.6 4.4 %collective-permute-start = (bf16[2,4,768]{2,1,0:T(4,128)(2,1)}, bf16[2,4,768]{2,1,0:T(4,128)(2,1)S(1)}, u32[]{:S(2)}, u32[]{:S(2)}) collective-permute-start(bf16[2,4,768]{2,1,0:T(4,128)(2,1)} %bitcast.16), channel_id=1, source_target_pairs={{0,1},{1,0},{2,3},{3,2},{4,5},{5,4},{6,7},{7,6},{8,9},{9,8},{10,11... | collective-permute-start | bytes 36872 | tf_op jit(solution)/shard_map/ppermute | solution.py:209
  5.0 9.3 %collective-permute-start.2 = (bf16[2,2,4,768]{3,2,1,0:T(4,128)(2,1)S(1)}, bf16[2,2,4,768]{3,2,1,0:T(4,128)(2,1)S(1)}, u32[]{:S(2)}, u32[]{:S(2)}) collective-permute-start(bf16[2,2,4,768]{3,2,1,0:T(4,128)(2,1)S(1)} %pad_maximum_fusion.1.pair), channel_id=1, source_target_pairs={{0,4},{2,6},{4,8},{6,10},{8,12},{10,14},{12,0},{14,2},{1,13},{3,15... | collective-permute-start | bytes 73736 | tf_op jit(solution)/shard_map/ppermute | solution.py:223
  9.4 5.5 %collective-permute-start.6 = (bf16[2,4,1792]{2,1,0:T(4,128)(2,1)}, bf16[2,4,1792]{2,1,0:T(4,128)(2,1)S(1)}, u32[]{:S(2)}, u32[]{:S(2)}) collective-permute-start(bf16[2,4,1792]{2,1,0:T(4,128)(2,1)} %down_hbm.1), channel_id=1, source_target_pairs={{0,64},{1,17},{2,66},{3,19},{4,68},{5,21},{6,70},{7,23},{8,72},{9,... | collective-permute-start | bytes 86024 | tf_op jit(solution)/shard_map/ppermute | solution.py:229
  10.6 4.4 %collective-permute-start.8 = (bf16[2,4,1792]{2,1,0:T(4,128)(2,1)}, bf16[2,4,1792]{2,1,0:T(4,128)(2,1)S(1)}, u32[]{:S(2)}, u32[]{:S(2)}) collective-permute-start(bf16[2,4,1792]{2,1,0:T(4,128)(2,1)} %down_hbm.1), channel_id=1, source_target_pairs={{0,192},{1,49},{2,194},{3,51},{4,196},{5,53},{6,198},{7,55},{8,200... | collective-permute-start | bytes 86024 | tf_op jit(solution)/shard_map/ppermute | solution.py:229
  12.1 4.4 %collective-permute-start.7 = (bf16[2,4,1792]{2,1,0:T(4,128)(2,1)}, bf16[2,4,1792]{2,1,0:T(4,128)(2,1)S(1)}, u32[]{:S(2)}, u32[]{:S(2)}) collective-permute-start(bf16[2,4,1792]{2,1,0:T(4,128)(2,1)} %down_hbm.1), channel_id=1, source_target_pairs={{0,128},{1,33},{2,130},{3,35},{4,132},{5,37},{6,134},{7,39},{8,136... | collective-permute-start | bytes 86024 | tf_op jit(solution)/shard_map/ppermute | solution.py:229
  13.6 6.3 %collective-permute-start.3 = (bf16[2,2,4,768]{3,2,1,0:T(4,128)(2,1)S(1)}, bf16[2,2,4,768]{3,2,1,0:T(4,128)(2,1)S(1)}, u32[]{:S(2)}, u32[]{:S(2)}) collective-permute-start(bf16[2,2,4,768]{3,2,1,0:T(4,128)(2,1)S(1)} %pad_maximum_fusion.1.pair), channel_id=1, source_target_pairs={{0,6},{2,8},{4,10},{6,12},{8,14},{10,0},{12,2},{14,4},{1,11},{3,13... | collective-permute-start | bytes 73736 | tf_op jit(solution)/shard_map/ppermute | solution.py:224
  14.3 6.4 %collective-permute-start.1 = (bf16[2,2,4,768]{3,2,1,0:T(4,128)(2,1)S(1)}, bf16[2,2,4,768]{3,2,1,0:T(4,128)(2,1)S(1)}, u32[]{:S(2)}, u32[]{:S(2)}) collective-permute-start(bf16[2,2,4,768]{3,2,1,0:T(4,128)(2,1)S(1)} %pad_maximum_fusion.1.pair), channel_id=1, source_target_pairs={{0,2},{2,4},{4,6},{6,8},{8,10},{10,12},{12,14},{14,0},{1,15},{3,1}... | collective-permute-start | bytes 73736 | tf_op jit(solution)/shard_map/ppermute | solution.py:224
  14.9 5.8 %collective-permute-start.4 = (bf16[2,4,768]{2,1,0:T(4,128)(2,1)S(1)}, bf16[2,4,768]{2,1,0:T(4,128)(2,1)S(1)}, u32[]{:S(2)}, u32[]{:S(2)}) collective-permute-start(bf16[2,4,768]{2,1,0:T(4,128)(2,1)S(1)} %slice_bitcast_fusion.1), channel_id=1, source_target_pairs={{0,4},{2,6},{4,8},{6,10},{8,12},{10,14},{12,0},{14,2},{1,13},{3,15... | collective-permute-start | bytes 36872 | tf_op jit(solution)/shard_map/ppermute | solution.py:225
  16.5 9.5 %copy-start = (bf16[2,768,1792]{2,1,0:T(8,128)(2,1)S(1)}, bf16[2,768,1792]{2,1,0:T(8,128)(2,1)}, u32[]{:S(2)}) copy-start(bf16[2,768,1792]{2,1,0:T(8,128)(2,1)} %g_ref.3) | copy-start | bytes 16515076
  16.5 9.6 %copy-start.1 = (bf16[2,768,1792]{2,1,0:T(8,128)(2,1)S(1)}, bf16[2,768,1792]{2,1,0:T(8,128)(2,1)}, u32[]{:S(2)}) copy-start(bf16[2,768,1792]{2,1,0:T(8,128)(2,1)} %w_ref.1) | copy-start | bytes 16515076
  16.5 9.5 %collective-permute-start.11 = (bf16[32,1792]{1,0:T(8,128)(2,1)S(1)}, bf16[32,1792]{1,0:T(8,128)(2,1)S(1)}, u32[]{:S(2)}, u32[]{:S(2)}) collective-permute-start(bf16[32,1792]{1,0:T(8,128)(2,1)S(1)} %stack.25.a0), channel_id=1, source_target_pairs={{0,48},{1,193},{2,50},{3,195},{4,52},{5,197},{6,54},{7,199},{8,56}... | collective-permute-start | bytes 344072 | tf_op jit(solution)/shard_map/ppermute | solution.py:239
  19.5 6.5 %collective-permute-start.10 = (bf16[32,1792]{1,0:T(8,128)(2,1)S(1)}, bf16[32,1792]{1,0:T(8,128)(2,1)S(1)}, u32[]{:S(2)}, u32[]{:S(2)}) collective-permute-start(bf16[32,1792]{1,0:T(8,128)(2,1)S(1)} %stack.25.a0), channel_id=1, source_target_pairs={{0,32},{1,129},{2,34},{3,131},{4,36},{5,133},{6,38},{7,135},{8,40}... | collective-permute-start | bytes 344072 | tf_op jit(solution)/shard_map/ppermute | solution.py:239
  19.9 6.1 %collective-permute-start.9 = (bf16[32,1792]{1,0:T(8,128)(2,1)S(1)}, bf16[32,1792]{1,0:T(8,128)(2,1)S(1)}, u32[]{:S(2)}, u32[]{:S(2)}) collective-permute-start(bf16[32,1792]{1,0:T(8,128)(2,1)S(1)} %stack.25.a0), channel_id=1, source_target_pairs={{0,16},{1,65},{2,18},{3,67},{4,20},{5,69},{6,22},{7,71},{8,24},{9,... | collective-permute-start | bytes 344072 | tf_op jit(solution)/shard_map/ppermute | solution.py:239
  20.8 4.4 %collective-permute-start.5 = (bf16[7,2,4,768]{3,2,1,0:T(4,128)(2,1)S(1)}, bf16[7,2,4,768]{3,2,1,0:T(4,128)(2,1)S(1)}, u32[]{:S(2)}, u32[]{:S(2)}) collective-permute-start(bf16[7,2,4,768]{3,2,1,0:T(4,128)(2,1)S(1)} %pad_maximum_fusion.mine), channel_id=1, source_target_pairs={{0,1},{1,0},{2,3},{3,2},{4,5},{5,4},{6,7},{7,6},{8,9},{9,8},{10,11... | collective-permute-start | bytes 258056 | tf_op jit(solution)/shard_map/ppermute | solution.py:227
  26.1 17.4 %copy-start.2 = (f32[2,1792]{1,0:T(2,128)S(1)}, f32[2,1792]{1,0:T(2,128)}, u32[]{:S(2)}) copy-start(f32[2,1792]{1,0:T(2,128)} %mag_ref.1) | copy-start | bytes 43012
  49.2 5.7 %collective-permute-start.12 = (f32[8,8,768]{2,1,0:T(8,128)S(1)}, f32[8,8,768]{2,1,0:T(8,128)S(1)}, u32[]{:S(2)}, u32[]{:S(2)}) collective-permute-start(f32[8,8,768]{2,1,0:T(8,128)S(1)} %get-tuple-element.42), channel_id=1, source_target_pairs={{0,1},{1,0},{2,3},{3,2},{4,5},{5,4},{6,7},{7,6},{8,9},{9,8},{10,11... | collective-permute-start | bytes 589832 | tf_op jit(solution)/shard_map/ppermute | solution.py:292
  51.3 20.7 %all-to-all-start.1 = ((f32[16,8,1792]{2,1,0:T(8,128)}), f32[16,8,1792]{2,1,0:T(8,128)S(1)}, u32[]{:S(2)}, u32[]{:S(2)}) async-start(f32[16,8,1792]{2,1,0:T(8,128)} %get-tuple-element.40), calls=%async_computation.1 | async-start | bytes 1835008 | tf_op jit(solution)/shard_map/all_to_all | solution.py:293
  55.0 4.5 %collective-permute-start.14 = (f32[8,768]{1,0:T(8,128)S(1)}, f32[8,768]{1,0:T(8,128)S(1)}, u32[]{:S(2)}, u32[]{:S(2)}) collective-permute-start(f32[8,768]{1,0:T(8,128)S(1)} %get-tuple-element.46), channel_id=1, source_target_pairs={{0,4},{2,6},{4,8},{6,10},{8,12},{10,14},{12,0},{14,2},{1,13},{3,15... | collective-permute-start | bytes 73736 | tf_op jit(solution)/shard_map/ppermute | solution.py:294
  57.6 4.8 %collective-permute-start.13 = (f32[2,8,768]{2,1,0:T(8,128)S(1)}, f32[2,8,768]{2,1,0:T(8,128)S(1)}, u32[]{:S(2)}, u32[]{:S(2)}) collective-permute-start(f32[2,8,768]{2,1,0:T(8,128)S(1)} %get-tuple-element.44), channel_id=1, source_target_pairs={{0,2},{2,4},{4,6},{6,8},{8,10},{10,12},{12,14},{14,0},{1,15},{3,1}... | collective-permute-start | bytes 147464 | tf_op jit(solution)/shard_map/ppermute | solution.py:295
  58.3 5.0 %collective-permute-start.16 = (f32[2,8,768]{2,1,0:T(8,128)S(1)}, f32[2,8,768]{2,1,0:T(8,128)S(1)}, u32[]{:S(2)}, u32[]{:S(2)}) collective-permute-start(f32[2,8,768]{2,1,0:T(8,128)S(1)} %get-tuple-element.47), channel_id=1, source_target_pairs={{0,6},{2,8},{4,10},{6,12},{8,14},{10,0},{12,2},{14,4},{1,11},{3,13... | collective-permute-start | bytes 147464 | tf_op jit(solution)/shard_map/ppermute | solution.py:295
  59.5 5.0 %collective-permute-start.15 = (f32[2,8,768]{2,1,0:T(8,128)S(1)}, f32[2,8,768]{2,1,0:T(8,128)S(1)}, u32[]{:S(2)}, u32[]{:S(2)}) collective-permute-start(f32[2,8,768]{2,1,0:T(8,128)S(1)} %fusion), channel_id=1, source_target_pairs={{0,4},{2,6},{4,8},{6,10},{8,12},{10,14},{12,0},{14,2},{1,13},{3,15... | collective-permute-start | bytes 147464 | tf_op jit(solution)/shard_map/ppermute | solution.py:296
  64.5 4.2 %collective-permute-start.17 = (f32[8,768]{1,0:T(8,128)S(1)}, f32[8,768]{1,0:T(8,128)S(1)}, u32[]{:S(2)}, u32[]{:S(2)}) collective-permute-start(f32[8,768]{1,0:T(8,128)S(1)} %slice_bitcast_fusion), channel_id=1, source_target_pairs={{0,1},{1,0},{2,3},{3,2},{4,5},{5,4},{6,7},{7,6},{8,9},{9,8},{10,11... | collective-permute-start | bytes 73736 | tf_op jit(solution)/shard_map/ppermute | solution.py:298
